TPU v7x, 256 devices: a whole 4x4x8 slice. The times are simulated.
256 devices in a mesh: trk: 64 (over x, z, core), frm: 4 (over y).
Axes of the slice: x: 4, y: 4, z: 8, core: 2. Of those that a mesh axis runs over, the one named last changes fastest.
Arguments:
- tokens: bfloat16 [2048, 32, 384], P('trk', 'frm'), may hold values from -10 to 10
- visible: int32 [2048, 32], P('trk', 'frm'), may hold values from 0 to 1, as said below
- virtual: bfloat16 [64, 32, 384], P(None, 'frm'), may hold values from -10 to 10
- time_qkv: bfloat16 [384, 1152], replicated, may hold values from -2 to 2
- time_out: bfloat16 [384, 384], replicated, may hold values from -0.3125 to 0.3125
- virt_q: bfloat16 [384, 384], replicated, may hold values from -2 to 2
- virt_kv: bfloat16 [384, 768], replicated, may hold values from -2 to 2
- virt_out: bfloat16 [384, 384], replicated, may hold values from -0.3125 to 0.3125
- self_qkv: bfloat16 [384, 1152], replicated, may hold values from -2 to 2
- self_out: bfloat16 [384, 384], replicated, may hold values from -0.3125 to 0.3125
- back_q: bfloat16 [384, 384], replicated, may hold values from -2 to 2
- back_kv: bfloat16 [384, 768], replicated, may hold values from -2 to 2
- back_out: bfloat16 [384, 384], replicated, may hold values from -0.3125 to 0.3125
Outputs:
- tracks_out: bfloat16 [2048, 32, 384], P('trk', 'frm')
- virtual_out: bfloat16 [64, 32, 384], P(None, 'frm')
Inputs may be any that keep to these rules, and one draw needn't show every extreme that they name: 1 where the track is visible in the frame, else 0; in every frame at least one track is visible.
All inputs are finite; a program needn't handle non-finite values.
Results may differ from a plain program's by a relative error of at most 0.015.
Values may be sent and summed in bfloat16 or wider, within the bound.
No kernel may reach another device: no remote copies, remote signals or barrier semaphores. Data moves between devices by JAX's collectives and lax.ppermute only.
A program may use at most 384 MiB of HBM per device.

v0:
```python
import jax
import jax.numpy as jnp
from jax import lax
from jax.sharding import PartitionSpec as P

HEADS = 8


EPS = 1e-05
NEG = -1e30


def normalize(values):
    widened = values.astype(jnp.float32)
    center = jnp.mean(widened, -1, keepdims=True)
    shifted = widened - center
    return (shifted * lax.rsqrt(jnp.mean(shifted * shifted, -1, keepdims=True) + EPS)).astype(
        jnp.bfloat16
    )


def project(values, weight):
    leading = values.shape[:-1]
    flat = values.reshape(-1, values.shape[-1])
    return jnp.dot(flat, weight, preferred_element_type=jnp.float32).reshape(
        leading + (weight.shape[1],)
    )


def split_heads(values):
    return values.reshape(values.shape[:-1] + (HEADS, values.shape[-1] // HEADS))


def attend_frames(queries, keys_all, values_all, scaling):
    scores = (
        jnp.einsum("bthe,bshe->bhts", queries, keys_all, preferred_element_type=jnp.float32)
        * scaling
    )
    weights = jax.nn.softmax(scores, -1).astype(jnp.bfloat16)
    mixed = jnp.einsum("bhts,bshe->bthe", weights, values_all, preferred_element_type=jnp.float32)
    return mixed.astype(jnp.bfloat16)


def on_device(
    tokens,
    visible,
    virtual,
    time_qkv,
    time_out,
    virt_q,
    virt_kv,
    virt_out,
    self_qkv,
    self_out,
    back_q,
    back_kv,
    back_out,
):
    width = tokens.shape[2]
    scaling = (width // HEADS) ** (-0.5)
    normed = normalize(tokens)
    projected = project(normed, time_qkv).astype(jnp.bfloat16)
    queries = split_heads(projected[..., :width])
    keys_all, values_all = (
        lax.all_gather(split_heads(projected[..., width : 2 * width]), "frm", axis=1, tiled=True),
        lax.all_gather(split_heads(projected[..., 2 * width :]), "frm", axis=1, tiled=True),
    )
    mixed = attend_frames(queries, keys_all, values_all, scaling).reshape(tokens.shape)
    updated = (tokens.astype(jnp.float32) + project(mixed, time_out)).astype(jnp.bfloat16)
    updated_norm = normalize(updated)
    key_value = project(updated_norm, virt_kv).astype(jnp.bfloat16)
    real_keys = split_heads(key_value[..., :width])
    real_values = split_heads(key_value[..., width:]).astype(jnp.float32)
    virt_norm = normalize(virtual)
    virt_query = split_heads(project(virt_norm, virt_q).astype(jnp.bfloat16))
    scores = (
        jnp.einsum("ifhe,bfhe->fihb", virt_query, real_keys, preferred_element_type=jnp.float32)
        * scaling
    )
    is_visible = (jnp.transpose(visible) > 0)[:, None, None, :]
    scores = jnp.where(is_visible, scores, NEG)
    local_peak = jnp.max(scores, -1)
    exp_terms = jnp.exp(scores - local_peak[..., None]) * is_visible.astype(jnp.float32)
    local_denom = jnp.sum(exp_terms, -1)
    local_weighted = jnp.einsum("fihb,bfhe->fihe", exp_terms, real_values)
    global_peak = lax.pmax(local_peak, "trk")
    factor = jnp.exp(local_peak - global_peak)
    denominator, weighted = lax.psum(
        (local_denom * factor, local_weighted * factor[..., None]), "trk"
    )
    frames_here = virtual.shape[1]
    attended = (
        (weighted / denominator[..., None])
        .astype(jnp.bfloat16)
        .reshape(frames_here, virtual.shape[0], width)
    )
    attended = jnp.transpose(attended, (1, 0, 2))
    virt_cross = (virtual.astype(jnp.float32) + project(attended, virt_out)).astype(jnp.bfloat16)
    self_proj = project(normalize(virt_cross), self_qkv).astype(jnp.bfloat16)
    self_query = split_heads(self_proj[..., :width])
    self_keys = split_heads(self_proj[..., width : 2 * width])
    self_values = split_heads(self_proj[..., 2 * width :])
    self_scores = (
        jnp.einsum("ifhe,jfhe->fhij", self_query, self_keys, preferred_element_type=jnp.float32)
        * scaling
    )
    self_weights = jax.nn.softmax(self_scores, -1).astype(jnp.bfloat16)
    self_mixed = jnp.einsum(
        "fhij,jfhe->ifhe", self_weights, self_values, preferred_element_type=jnp.float32
    )
    self_mixed = self_mixed.astype(jnp.bfloat16).reshape(virt_cross.shape)
    virtual_out = (virt_cross.astype(jnp.float32) + project(self_mixed, self_out)).astype(
        jnp.bfloat16
    )
    back_pair = project(normalize(virtual_out), back_kv).astype(jnp.bfloat16)
    back_keys = split_heads(back_pair[..., :width])
    back_values = split_heads(back_pair[..., width:])
    back_query = split_heads(project(updated_norm, back_q).astype(jnp.bfloat16))
    back_scores = (
        jnp.einsum("bfhe,ifhe->bfhi", back_query, back_keys, preferred_element_type=jnp.float32)
        * scaling
    )
    back_weights = jax.nn.softmax(back_scores, -1).astype(jnp.bfloat16)
    back_mixed = jnp.einsum(
        "bfhi,ifhe->bfhe", back_weights, back_values, preferred_element_type=jnp.float32
    )
    back_mixed = back_mixed.astype(jnp.bfloat16).reshape(tokens.shape)
    tracks_out = (updated.astype(jnp.float32) + project(back_mixed, back_out)).astype(jnp.bfloat16)
    return (tracks_out, virtual_out)


def solution(mesh):
    placed = (
        P("trk", "frm", None),
        P("trk", "frm"),
        P(None, "frm", None),
        P(),
        P(),
        P(),
        P(),
        P(),
        P(),
        P(),
        P(),
        P(),
        P(),
    )
    return jax.shard_map(
        on_device,
        mesh=mesh,
        in_specs=placed,
        out_specs=(P("trk", "frm", None), P(None, "frm", None)),
        check_vma=False,
    )
```

profile of v0, /device:TPU:1, one launch (start us, length us, event | category | flops | bytes accessed | tf_op | source)
XLA Modules:
  0.0 639.7 jit_solution(10036532223762797823)
XLA Ops:
  7.2 0.0 copy-start
  7.2 0.0 all-reduce.2.cloned.1.call-start
  7.2 1.1 convert_reduce_fusion.2
  8.4 1.1 fusion.43
  9.5 1.8 convolution_convert_fusion.1
  11.3 0.1 fusion.71
  11.4 0.4 reshape.154
  11.8 0.1 copy.31
  11.9 37.3 %all_gather.7 = bf16[32,32,8,48]{3,1,2,0:T(8,128)(2,1)S(1)} all-gather(bf16[32,8,8,48]{3,1,2,0:T(8,128)(2,1)S(1)} %copy.31), channel_id=1, replica_groups=mesh['trk'=64,'frm'=4] {'frm'}, dimensions={1}, use_global_device_ids=true | all-gather | bytes 983040 | tf_op jit(solution)/shard_map/all_gather | solution.py:65
  49.2 1.2 reshape.153
  50.4 1.2 reshape.152
  51.6 1.1 copy.30
  52.8 35.1 %all_gather.6 = bf16[32,32,8,48]{3,1,2,0:T(8,128)(2,1)} all-gather(bf16[32,8,8,48]{3,1,2,0:T(8,128)(2,1)S(1)} %copy.30), channel_id=1, replica_groups=mesh['trk'=64,'frm'=4] {'frm'}, dimensions={1}, use_global_device_ids=true | all-gather | bytes 983040 | tf_op jit(solution)/shard_map/all_gather | solution.py:66
  87.9 3.3 fusion.73
  91.2 2.6 fusion.14
  93.8 0.0 copy-start.4
  93.9 0.1 copy.33
  94.0 0.4 dot_general.63
  94.4 0.4 fusion.74
  94.8 0.0 copy-start.13
  94.8 0.2 multiply_reduce_fusion.2
  95.0 0.4 convolution_convert_fusion.7
  95.4 0.7 fusion.72
  96.2 1.2 reshape.156
  97.4 0.1 convert_reduce_fusion
  97.5 0.2 fusion.27
  97.8 0.5 convolution_convert_fusion.6
  98.3 0.5 copy.48
  98.8 0.6 fusion.68
  99.4 1.6 fusion.75
  101.0 251.0 %pmax.7 = f32[8,64,8]{1,2,0:T(8,128)S(1)} all-reduce(f32[8,64,8]{1,2,0:T(8,128)S(1)} %get-tuple-element.20), channel_id=1, replica_groups=mesh['trk'=64,'frm'=4] {'trk'}, use_global_device_ids=true, to_apply=%region_9.10 | all-reduce | flops 4096 | bytes 32768 | tf_op jit(solution)/shard_map/pmax | solution.py:86
  352.0 1.4 reshape.155
  353.4 1.0 fusion.26
  354.4 0.0 copy-start.10
  354.4 2.5 bitcast_multiply_fusion
  356.9 0.0 all-reduce.2.cloned.1.call-update
  357.0 1.3 convolution_convert_fusion.8
  358.3 1.3 reshape.164
  359.5 246.5 %psum.15 = f32[8,64,8]{1,2,0:T(8,128)S(1)} all-reduce(f32[8,64,8]{1,2,0:T(8,128)S(1)} %get-tuple-element.2), channel_id=1, replica_groups=mesh['trk'=64,'frm'=4] {'trk'}, use_global_device_ids=true, to_apply=%region_12.13 | all-reduce | flops 4096 | bytes 32768 | tf_op jit(solution)/shard_map/psum | solution.py:88
  606.1 1.6 divide_convert_fusion.1
  607.6 0.4 copy.37
  608.0 0.5 fusion.76
  608.5 0.2 multiply_reduce_fusion.1
  608.8 0.9 convolution_convert_fusion
  609.7 0.1 fusion.69
  609.8 1.3 copy.50
  611.1 1.2 copy.51
  612.3 0.5 copy.49
  612.8 3.7 fusion.77
  616.4 3.1 convolution_convert_fusion.2
  619.5 1.6 copy.42
  621.1 0.5 convert_reduce_fusion.1
  621.6 0.0 copy-start.3
  621.6 0.2 fusion.29
  621.9 0.6 convolution_convert_fusion.3
  622.5 0.1 fusion.70
  622.6 0.5 copy.53
  623.1 1.6 fusion.8
  624.6 0.7 fusion.78
  625.3 0.5 copy.52
  625.8 4.4 fusion.15
  630.2 1.2 copy.46
  631.5 0.4 dot_general.79
  631.8 1.0 fusion.18
  (35 shorter events, 0.2 us)
Async XLA Ops:
  7.2 601.6 %copy-start = (bf16[384,1152]{1,0:T(8,128)(2,1)S(1)}, bf16[384,1152]{1,0:T(8,128)(2,1)}, u32[]{:S(2)}) copy-start(bf16[384,1152]{1,0:T(8,128)(2,1)} %param.21) | copy-start | bytes 2654212
  7.2 598.9 %all-reduce.2.cloned.1.call-start = ((), (), s32[]{:S(2)}) async-start(), calls=%async_computation | async-start | bytes 3145728 | tf_op jit(solution)/shard_map/psum | solution.py:88
  91.2 3.1 copy-start.2
  91.2 3.2 copy-start.5
  93.8 1.1 copy-start.4
  94.4 3.0 copy-start.1
  94.8 3.0 copy-start.13
  95.0 2.8 copy-start.9
  96.2 2.6 copy-start.11
  354.4 2.5 copy-start.10
  358.3 249.7 %copy-start.7 = (bf16[384,384]{1,0:T(8,128)(2,1)S(1)}, bf16[384,384]{1,0:T(8,128)(2,1)}, u32[]{:S(2)}) copy-start(bf16[384,384]{1,0:T(8,128)(2,1)} %param.20) | copy-start | bytes 884740
  616.4 4.7 copy-start.8
  619.5 2.3 copy-start.12
  621.6 1.0 copy-start.3
  625.8 6.1 copy-start.6
Sparse Core Ops, SparseCore 0:
  357.1 182.6 all-reduce.1
where the time goes:
time: 643 us; the launch traced here: 640 us
  blocking collectives  570 us (89%)
  matrix products  30.6 us (5%)
  local copies, waits for them, and re-layouts  17.4 us (3%)
  between operations  14.6 us (2%)
  other arithmetic  7.17 us (1%)
    pmax x1, blocking collectives, on_device(): global_peak = lax.pmax(local_peak, 'trk')  251 us
    psum x1, blocking collectives, on_device(): lax.psum((local_denom * factor, local_weighted * factor[..., None]), 'trk')  247 us
    all_gather x1, blocking collectives, on_device(): lax.all_gather(split_heads(projected[..., width:2 * width]), 'frm', axis=...  37.3 us
    all_gather x1, blocking collectives, on_device(): lax.all_gather(split_heads(projected[..., 2 * width:]), 'frm', axis=1, ti...  35.1 us
  transfers between devices with their start and end apart: 1, of which 0 were waited for; matrix products, arithmetic and copies ran while one was open for 0% of the time, Pallas kernels for 0%

commit v1 on v0

v1 whole, which is shorter than its diff:
```python
import jax
import jax.numpy as jnp
from jax import lax
from jax.experimental import pallas as pl
from jax.experimental.pallas import tpu as pltpu
from jax.sharding import Mesh
from jax.sharding import PartitionSpec as P

HEADS = 8
EPS = 1e-05
NEG = -1e30
MARK = 64.0
BF = jnp.bfloat16
F32 = jnp.float32
TRACK_AXES = ("x", "zh", "zl", "c")


def normalize(values):
    widened = values.astype(F32)
    center = jnp.mean(widened, -1, keepdims=True)
    shifted = widened - center
    return (shifted * lax.rsqrt(jnp.mean(shifted * shifted, -1, keepdims=True) + EPS)).astype(BF)


def matmul(a, b):
    return lax.dot_general(a, b, (((1,), (0,)), ((), ())), preferred_element_type=F32)


def matmul_t(a, b):
    return lax.dot_general(a, b, (((1,), (1,)), ((), ())), preferred_element_type=F32)


def iota(shape, dim):
    return lax.broadcasted_iota(jnp.int32, shape, dim)


def head_masks(width):
    lane = iota((1, width), 1)
    each = width // HEADS
    return [(lane >= h * each) & (lane < (h + 1) * each) for h in range(HEADS)]


def stack_heads(rows):
    width = rows.shape[1]
    return jnp.concatenate(
        [rows * mask.astype(F32).astype(rows.dtype) for mask in head_masks(width)], axis=0
    )


def pick_heads(stacked, count):
    masks = head_masks(stacked.shape[1])
    total = jnp.where(masks[0], stacked[:count], 0.0)
    for h in range(1, HEADS):
        total = jnp.where(masks[h], stacked[h * count : (h + 1) * count], total)
    return total


def softmax_mix(scores, values, factor, count):
    peak = jnp.max(scores, -1, keepdims=True)
    terms = jnp.exp((scores - peak) * factor)
    denominator = jnp.sum(terms, -1, keepdims=True)
    mixed = matmul(terms.astype(BF), values)
    return pick_heads(mixed * (1.0 / denominator), count)


def swap_matrix(outer, inner):
    n = outer * inner
    row, col = iota((n, n), 0), iota((n, n), 1)
    source = (row % inner) * outer + row // inner
    return jnp.where(col == source, 1.0, 0.0).astype(BF)


def own_kernel(tokens_ref, virtual_ref, time_qkv_ref, virt_q_ref, qkv_ref, query_ref):
    qkv_ref[...] = matmul(normalize(tokens_ref[...]), time_qkv_ref[...]).astype(BF)
    query_ref[...] = matmul(normalize(virtual_ref[...]), virt_q_ref[...]).astype(BF)


def time_kernel(
    frames, group, tokens_ref, qkv_ref, p1_ref, p2_ref, p3_ref, visible_ref, time_qkv_ref, time_out_ref, back_q_ref,
    updated_ref, send_ref, query_ref,
):
    width = tokens_ref.shape[1]
    factor = float((width // HEADS) ** (-0.5))
    rows = tokens_ref.shape[0]
    tracks = rows // frames
    size = group * frames
    time_kv = time_qkv_ref[:, width:]
    pairs = [qkv_ref[:, width:]] + [
        matmul(normalize(ref[...]), time_kv).astype(BF) for ref in (p1_ref, p2_ref, p3_ref)
    ]
    row, col = iota((size, 4 * size), 0), iota((size, 4 * size), 1)
    bias = jnp.where(row // frames == (col % size) // frames, 0.0, NEG)[None]
    mixed = []
    for g in range(rows // size):
        span = slice(g * size, (g + 1) * size)
        keys = jnp.concatenate([pair[span, :width] for pair in pairs], axis=0)
        values = jnp.concatenate([pair[span, width:] for pair in pairs], axis=0)
        scores = matmul_t(stack_heads(qkv_ref[span, :width]), keys)
        scores = (scores.reshape(HEADS, size, 4 * size) + bias).reshape(HEADS * size, 4 * size)
        mixed.append(softmax_mix(scores, values, factor, size).astype(BF))
    mixed = jnp.concatenate(mixed, axis=0)
    updated = (tokens_ref[...].astype(F32) + matmul(mixed, time_out_ref[...])).astype(BF)
    updated_ref[...] = updated
    by_frame = swap_matrix(frames, tracks)
    normed = matmul(by_frame, normalize(updated))
    pick = jnp.where(iota((rows, tracks), 0) % tracks == iota((rows, tracks), 1), 1.0, 0.0).astype(BF)
    spread = matmul(pick, visible_ref[...].astype(F32).astype(BF))
    here = iota((rows, frames), 0) // tracks == iota((rows, frames), 1)
    seen = jnp.sum(jnp.where(here, spread, 0.0), -1, keepdims=True) > 0.5
    send_ref[...] = jnp.where(seen, normed, MARK).astype(BF)
    query_ref[...] = matmul(normed.astype(BF), back_q_ref[...]).astype(BF)


def partial_kernel(here_ref, there_ref, query_ref, virt_kv_ref, out_ref):
    width = here_ref.shape[1]
    factor = float((width // HEADS) ** (-0.5))
    count = query_ref.shape[0]
    rows = jnp.concatenate([here_ref[...], there_ref[...]], axis=0)
    pair = matmul(rows, virt_kv_ref[...]).astype(BF)
    first = jnp.where(iota((8, width), 1) == 0, 1.0, 0.0).astype(BF)
    seen = matmul_t(first, rows)[:1] < MARK / 2
    scores = matmul_t(stack_heads(query_ref[...]), pair[:, :width])
    scores = jnp.where(seen, scores * factor, NEG)
    peak = jnp.max(scores, -1, keepdims=True)
    terms = jnp.where(seen, jnp.exp(scores - peak), 0.0)
    denominator = jnp.sum(terms, -1, keepdims=True)
    out_ref[:, :width] = pick_heads(matmul(terms.astype(BF), pair[:, width:]), count)
    lane = iota((count, 128), 1)
    stats = jnp.zeros((count, 128), F32)
    for h in range(HEADS):
        span = slice(h * count, (h + 1) * count)
        stats = jnp.where(lane == h, peak[span], stats)
        stats = jnp.where(lane == HEADS + h, denominator[span], stats)
    out_ref[:, width:] = stats


def virtual_kernel(
    a_ref, b_ref, c_ref, d_ref, virtual_ref, virt_out_ref, self_qkv_ref, self_out_ref, out_ref
):
    count, width = virtual_ref.shape
    factor = float((width // HEADS) ** (-0.5))
    parts = [ref[...] for ref in (a_ref, b_ref, c_ref, d_ref)]
    peaks = [part[:, width : width + HEADS] for part in parts]
    sums = [part[:, width + HEADS : width + 2 * HEADS] for part in parts]
    top = jnp.maximum(jnp.maximum(peaks[0], peaks[1]), jnp.maximum(peaks[2], peaks[3]))
    scales = [jnp.exp(peak - top) for peak in peaks]
    denominator = sum(scale * total for scale, total in zip(scales, sums))
    inverse = 1.0 / denominator
    lane = iota((HEADS, width), 1)
    head = iota((HEADS, width), 0)
    each = width // HEADS
    expand = jnp.where((lane >= head * each) & (lane < (head + 1) * each), 1.0, 0.0)
    attended = jnp.zeros((count, width), F32)
    for scale, part in zip(scales, parts):
        weight = lax.dot_general(
            scale * inverse, expand, (((1,), (0,)), ((), ())),
            precision=lax.Precision.HIGHEST, preferred_element_type=F32,
        )
        attended = attended + weight * part[:, :width]
    cross = (virtual_ref[...].astype(F32) + matmul(attended.astype(BF), virt_out_ref[...])).astype(BF)
    proj = matmul(normalize(cross), self_qkv_ref[...]).astype(BF)
    scores = matmul_t(stack_heads(proj[:, :width]), proj[:, width : 2 * width])
    mixed = softmax_mix(scores, proj[:, 2 * width :], factor, count).astype(BF)
    out_ref[...] = (cross.astype(F32) + matmul(mixed, self_out_ref[...])).astype(BF)


def back_kernel(updated_ref, query_ref, virtual_ref, back_kv_ref, back_out_ref, out_ref, virtual_out_ref):
    frames, count, width = virtual_ref.shape
    rows = updated_ref.shape[0]
    tracks = rows // frames
    factor = float((width // HEADS) ** (-0.5))
    flat = virtual_ref[...].reshape(frames * count, width)
    pair = matmul(normalize(flat), back_kv_ref[...]).astype(BF)
    mixed = []
    for f in range(frames):
        span = slice(f * count, (f + 1) * count)
        scores = matmul_t(stack_heads(query_ref[f * tracks : (f + 1) * tracks]), pair[span, :width])
        mixed.append(softmax_mix(scores, pair[span, width:], factor, tracks).astype(BF))
    by_track = matmul(swap_matrix(tracks, frames), jnp.concatenate(mixed, axis=0)).astype(BF)
    out_ref[...] = (updated_ref[...].astype(F32) + matmul(by_track, back_out_ref[...])).astype(BF)
    virtual_out_ref[...] = matmul(swap_matrix(count, frames), flat).astype(BF)


def call(kernel, outs, *args, megabytes=32):
    return pl.pallas_call(
        kernel,
        out_shape=[jax.ShapeDtypeStruct(shape, dtype) for shape, dtype in outs],
        compiler_params=pltpu.CompilerParams(vmem_limit_bytes=megabytes * 1024 * 1024),
    )(*args)


def shift(value, axis, count, step):
    return lax.ppermute(value, axis, [(i, (i + step) % count) for i in range(count)])


def on_device(
    tokens, visible, virtual, time_qkv, time_out, virt_q, virt_kv, virt_out, self_qkv, self_out, back_q, back_kv,
    back_out,
):
    tracks, frames, width = tokens.shape
    count = virtual.shape[0]
    rows = tracks * frames
    flat = tokens.reshape(rows, width)
    others = [shift(flat, "y", 4, step) for step in (1, 3, 2)]
    frame = lax.axis_index("x") * 2 + lax.axis_index("zl")
    mine = lax.dynamic_slice_in_dim(virtual, frame, 1, axis=1).reshape(count, width)
    qkv, virt_query = call(
        own_kernel, [((rows, 3 * width), BF), ((count, width), BF)], flat, mine, time_qkv, virt_q
    )
    updated, send, back_query = call(
        lambda *refs: time_kernel(frames, 8, *refs),
        [((rows, width), BF)] * 3,
        flat, qkv, *others, visible, time_qkv, time_out, back_q,
    )
    got = lax.all_to_all(send.reshape(frames, tracks, width), ("x", "zl"), 0, 0).reshape(rows, width)
    got_there = shift(got, "c", 2, 1)
    (partial,) = call(partial_kernel, [((count, width + 128), F32)], got, got_there, virt_query, virt_kv)
    partials = [partial] + [shift(partial, "zh", 4, step) for step in (1, 3, 2)]
    (frame_out,) = call(
        virtual_kernel, [((count, width), BF)], *partials, mine, virt_out, self_qkv, self_out
    )
    gathered = lax.all_to_all(
        jnp.broadcast_to(frame_out[None], (frames, count, width)), ("x", "zl"), 0, 0
    )
    tracks_out, virtual_out = call(
        back_kernel,
        [((rows, width), BF), ((count * frames, width), BF)],
        updated, back_query, gathered, back_kv, back_out,
    )
    return tracks_out.reshape(tokens.shape), virtual_out.reshape(virtual.shape)


def solution(mesh):
    fine = Mesh(mesh.devices.reshape(4, 4, 2, 2, 4), ("x", "zh", "zl", "c", "y"))
    tokens = P(TRACK_AXES, "y", None)
    virtual = P(None, "y", None)
    return jax.shard_map(
        on_device,
        mesh=fine,
        in_specs=(tokens, P(TRACK_AXES, "y"), virtual) + (P(),) * 10,
        out_specs=(tokens, virtual),
        check_vma=False,
    )
```

time: 643 us -> 70.2 us (0.11)
  blocking collectives: 570 us -> 20.6 us
  matrix products: 30.6 us -> 0 us
  starting transfers between devices: 0.04 us -> 16.6 us
  waiting for transfers between devices: 0.02 us -> 16.3 us
  between operations: 14.6 us -> 0.76 us
  local copies, waits for them, and re-layouts: 17.4 us -> 4.05 us
  Pallas kernels: 0 us -> 11.3 us
  other arithmetic: 7.17 us -> 0 us
    pmax x1 -> x0, blocking collectives: 251 us -> none  [on_device(): global_peak = lax.pmax(local_peak, 'trk')]
    psum x1 -> x0, blocking collectives: 247 us -> none  [on_device(): lax.psum((local_denom * factor, local_weighted * factor[..., None]), 'trk')]
    all_gather x2 -> x0, blocking collectives: 72.4 us -> none  [the longest x1 37.3 us: on_device(): lax.all_gather(split_heads(projected[..., width:2 * width]), 'frm', axis=...]
    dot_general x16 -> x0, matrix products: 23.6 us -> none  [the longest x10 7.78 us: project(): jnp.dot(flat, weight, preferred_element_type=jnp.float32)]
    all_to_all x0 -> x2, blocking collectives: none -> 20.6 us  [the longest x1 10.4 us: on_device(): lax.all_to_all(send.reshape(frames, tracks, width), ('x', 'zl'), 0, 0)]
    ppermute x0 -> x7, starting transfers between devices: none -> 16.6 us  [shift(): lax.ppermute(value, axis, [(i, (i + step) % count) for i in range(count)])]
    ppermute x0 -> x7, waiting for transfers between devices: none -> 16.3 us  [shift(): lax.ppermute(value, axis, [(i, (i + step) % count) for i in range(count)])]
    reshape x15 -> x0, local copies, waits for them, and re-layouts: 12.7 us -> none  [the longest x14 12.3 us: split_heads(): values.reshape(values.shape[:-1] + (HEADS, values.shape[-1] // HEADS))]
  transfers between devices with their start and end apart: 1 -> 7, of which waited for: 0 -> 5; matrix products, arithmetic and copies ran while one was open for 0% -> 1% of each run, Pallas kernels for 0% -> 1%
where the time goes in v1:
time: 70.2 us; the launch traced here: 69.6 us
  blocking collectives  20.6 us (29%)
  starting transfers between devices  16.6 us (24%)
  waiting for transfers between devices  16.3 us (23%)
  Pallas kernels  11.3 us (16%)
  local copies, waits for them, and re-layouts  4.05 us (6%)
  between operations  0.76 us (1%)
    ppermute x7, starting transfers between devices, shift(): lax.ppermute(value, axis, [(i, (i + step) % count) for i in range(count)])  16.6 us
    ppermute x7, waiting for transfers between devices, shift(): lax.ppermute(value, axis, [(i, (i + step) % count) for i in range(count)])  16.3 us
    pallas_call x5, Pallas kernels, call(): pl.pallas_call(kernel, out_shape=[jax.ShapeDtypeStruct(shape, dtype) for...  11.3 us
    all_to_all x1, blocking collectives, on_device(): lax.all_to_all(send.reshape(frames, tracks, width), ('x', 'zl'), 0, 0)  10.4 us
    all_to_all x1, blocking collectives, on_device(): lax.all_to_all(jnp.broadcast_to(frame_out[None], (frames, count, width)),...  10.2 us
    unnamed x28, local copies, waits for them, and re-layouts  3.91 us
  transfers between devices with their start and end apart: 7, of which 5 were waited for; matrix products, arithmetic and copies ran while one was open for 1% of the time, Pallas kernels for 1%

profile of v1, /device:TPU:1, one launch (start us, length us, event | category | flops | bytes accessed | tf_op | source)
XLA Modules:
  0.0 69.6 jit_solution(13386043015693075832)
XLA Ops:
  0.6 0.0 copy-start
  0.6 0.0 copy-start.4
  0.7 3.8 %collective-permute-start.2 = (bf16[256,384]{1,0:T(8,128)(2,1)}, bf16[256,384]{1,0:T(8,128)(2,1)S(1)}, u32[]{:S(2)}, u32[]{:S(2)}) collective-permute-start(bf16[256,384]{1,0:T(8,128)(2,1)} %bitcast.10), channel_id=1, source_target_pairs={{0,2},{1,3},{2,0},{3,1},{4,6},{5,7},{6,4},{7,5},{8,10},{9,11},{10,... | collective-permute-start | bytes 589832 | tf_op jit(solution)/shard_map/ppermute | solution.py:193
  4.5 0.8 %collective-permute-start.1 = (bf16[256,384]{1,0:T(8,128)(2,1)}, bf16[256,384]{1,0:T(8,128)(2,1)S(1)}, u32[]{:S(2)}, u32[]{:S(2)}) collective-permute-start(bf16[256,384]{1,0:T(8,128)(2,1)} %bitcast.11), channel_id=1, source_target_pairs={{0,3},{1,0},{2,1},{3,2},{4,7},{5,4},{6,5},{7,6},{8,11},{9,8},{10,9... | collective-permute-start | bytes 589832 | tf_op jit(solution)/shard_map/ppermute | solution.py:193
  5.3 0.7 collective-permute-start
  6.0 0.8 %copy.17.refs_5_ = s32[32,8]{1,0:T(8,128)S(1)} copy(s32[32,8]{0,1:T(8,128)} %param.14) | data formatting | bytes 2048 | tf_op args[1]
  6.7 0.0 copy-done
  6.7 0.1 constant_dynamic-slice_fusion
  6.8 0.0 copy-done.4
  6.9 0.0 copy-start.1
  6.9 1.2 %copy-done.1 = bf16[384,1152]{1,0:T(8,128)(2,1)S(1)} copy-done((bf16[384,1152]{1,0:T(8,128)(2,1)S(1)}, bf16[384,1152]{1,0:T(8,128)(2,1)}, u32[]{:S(2)}) %copy-start.1) | copy-done | bytes 884760
  8.0 0.0 copy-start.8
  8.0 1.0 %copy-done.8 = bf16[384,384]{1,0:T(8,128)(2,1)S(1)} copy-done((bf16[384,384]{1,0:T(8,128)(2,1)S(1)}, bf16[384,384]{1,0:T(8,128)(2,1)}, u32[]{:S(2)}) %copy-start.8) | copy-done | bytes 294936
  9.0 0.0 copy-start.2
  9.0 0.0 copy-start.9
  9.0 0.7 %shard_map.140 = (bf16[256,1152]{1,0:T(8,128)(2,1)S(1)}, bf16[64,384]{1,0:T(8,128)(2,1)S(1)}) custom-call(bf16[256,384]{1,0:T(8,128)(2,1)S(1)} %bitcast.13, bf16[64,384]{1,0:T(8,128)(2,1)S(1)} %bitcast.15, bf16[384,1152]{1,0:T(8,128)(2,1)S(1)} %copy-done.1, bf16[384,384]{1,0:T(8,128)(2,1)S(1)} %copy-done.8), custom_call_target="tpu_custom_call" | custom-call | tf_op jit(solution)/shard_map/pallas_call | solution.py:185
  9.7 0.0 collective-permute-done.2.refs_4_
  9.7 4.0 %collective-permute-done.1.refs_3_ = bf16[256,384]{1,0:T(8,128)(2,1)S(1)} collective-permute-done((bf16[256,384]{1,0:T(8,128)(2,1)}, bf16[256,384]{1,0:T(8,128)(2,1)S(1)}, u32[]{:S(2)}, u32[]{:S(2)}) %collective-permute-start.1) | collective-permute-done | bytes 196640 | tf_op jit(solution)/shard_map/ppermute | solution.py:193
  13.8 0.8 %collective-permute-done.refs_2_ = bf16[256,384]{1,0:T(8,128)(2,1)S(1)} collective-permute-done((bf16[256,384]{1,0:T(8,128)(2,1)}, bf16[256,384]{1,0:T(8,128)(2,1)S(1)}, u32[]{:S(2)}, u32[]{:S(2)}) %collective-permute-start) | collective-permute-done | bytes 196640 | tf_op jit(solution)/shard_map/ppermute | solution.py:193
  14.5 0.0 copy-done.2
  14.5 0.0 copy-done.9
  14.5 0.0 copy-start.10
  14.5 1.0 %copy-done.10 = bf16[384,384]{1,0:T(8,128)(2,1)S(1)} copy-done((bf16[384,384]{1,0:T(8,128)(2,1)S(1)}, bf16[384,384]{1,0:T(8,128)(2,1)}, u32[]{:S(2)}) %copy-start.10) | copy-done | bytes 294936
  15.5 0.0 copy-start.6
  15.5 3.1 %shard_map.141 = (bf16[256,384]{1,0:T(8,128)(2,1)S(1)}, bf16[256,384]{1,0:T(8,128)(2,1)S(1)}, bf16[256,384]{1,0:T(8,128)(2,1)S(1)}) custom-call(bf16[256,384]{1,0:T(8,128)(2,1)S(1)} %bitcast.14, bf16[256,1152]{1,0:T(8,128)(2,1)S(1)} %get-tuple-element.9.refs_1_, bf16[256,384]{1,0:T(8,128)(2,1)S(1)} %collective-permute-done.refs_2_, ...), custom_call_target="tpu_custom_call" | custom-call | tf_op jit(solution)/shard_map/pallas_call | solution.py:185
  18.6 0.0 copy-start.3
  18.6 10.4 %all_to_all.10 = bf16[8,32,384]{2,1,0:T(8,128)(2,1)S(1)} all-to-all(bf16[8,32,384]{2,1,0:T(8,128)(2,1)S(1)} %bitcast.17), channel_id=1, replica_groups=mesh['x'=4,'zh'=4,'zl'=2,'c'=2,'y'=4] {'x','zl'}, dimensions={0} | all-to-all | bytes 393216 | tf_op jit(solution)/shard_map/all_to_all | solution.py:215
  29.0 2.9 %collective-permute-start.3 = (bf16[256,384]{1,0:T(8,128)(2,1)S(1)}, bf16[256,384]{1,0:T(8,128)(2,1)S(1)}, u32[]{:S(2)}, u32[]{:S(2)}) collective-permute-start(bf16[256,384]{1,0:T(8,128)(2,1)S(1)} %bitcast.8), channel_id=1, source_target_pairs={{0,4},{4,0},{1,5},{5,1},{2,6},{6,2},{3,7},{7,3},{8,12},{12,8},{9,1... | collective-permute-start | bytes 589832 | tf_op jit(solution)/shard_map/ppermute | solution.py:193
  31.8 1.1 %collective-permute-done.3.there_ref = bf16[256,384]{1,0:T(8,128)(2,1)S(1)} collective-permute-done((bf16[256,384]{1,0:T(8,128)(2,1)S(1)}, bf16[256,384]{1,0:T(8,128)(2,1)S(1)}, u32[]{:S(2)}, u32[]{:S(2)}) %collective-permute-start.3) | collective-permute-done | bytes 196640 | tf_op jit(solution)/shard_map/ppermute | solution.py:193
  32.9 0.0 copy-done.6
  32.9 0.0 copy-start.11
  32.9 0.0 copy-start.12
  32.9 1.4 %shard_map.142.a_ref = f32[64,512]{1,0:T(8,128)S(1)} custom-call(bf16[256,384]{1,0:T(8,128)(2,1)S(1)} %bitcast.9, bf16[256,384]{1,0:T(8,128)(2,1)S(1)} %collective-permute-done.3.there_ref, bf16[64,384]{1,0:T(8,128)(2,1)S(1)} %get-tuple-element.13.query_ref, bf16[384,768]{1,0:T(8,128)(2,1)S(1)} %copy-done.6), custom_call_target="tpu_custom_call" | custom-call | tf_op jit(solution)/shard_map/pallas_call | solution.py:185
  34.3 6.1 %collective-permute-start.6 = (f32[64,512]{1,0:T(8,128)S(1)}, f32[64,512]{1,0:T(8,128)S(1)}, u32[]{:S(2)}, u32[]{:S(2)}) collective-permute-start(f32[64,512]{1,0:T(8,128)S(1)} %shard_map.142.a_ref), channel_id=1, source_target_pairs={{0,32},{16,48},{32,0},{48,16},{1,33},{17,49},{33,1},{49,17},{2,34}... | collective-permute-start | bytes 393224 | tf_op jit(solution)/shard_map/ppermute | solution.py:193
  40.4 0.3 collective-permute-start.5
  40.7 2.1 %collective-permute-start.4 = (f32[64,512]{1,0:T(8,128)S(1)}, f32[64,512]{1,0:T(8,128)S(1)}, u32[]{:S(2)}, u32[]{:S(2)}) collective-permute-start(f32[64,512]{1,0:T(8,128)S(1)} %shard_map.142.a_ref), channel_id=1, source_target_pairs={{0,16},{16,32},{32,48},{48,0},{1,17},{17,33},{33,49},{49,1},{2,18}... | collective-permute-start | bytes 393224 | tf_op jit(solution)/shard_map/ppermute | solution.py:193
  42.8 1.2 %collective-permute-done.6.d_ref = f32[64,512]{1,0:T(8,128)S(1)} collective-permute-done((f32[64,512]{1,0:T(8,128)S(1)}, f32[64,512]{1,0:T(8,128)S(1)}, u32[]{:S(2)}, u32[]{:S(2)}) %collective-permute-start.6) | collective-permute-done | bytes 131104 | tf_op jit(solution)/shard_map/ppermute | solution.py:193
  44.0 9.2 %collective-permute-done.5.c_ref = f32[64,512]{1,0:T(8,128)S(1)} collective-permute-done((f32[64,512]{1,0:T(8,128)S(1)}, f32[64,512]{1,0:T(8,128)S(1)}, u32[]{:S(2)}, u32[]{:S(2)}) %collective-permute-start.5) | collective-permute-done | bytes 131104 | tf_op jit(solution)/shard_map/ppermute | solution.py:193
  53.1 0.0 collective-permute-done.4.b_ref
  53.1 0.0 copy-done.3
  53.1 0.0 copy-done.11
  53.2 0.0 copy-done.12
  53.2 1.7 %shard_map.143 = bf16[64,384]{1,0:T(8,128)(2,1)S(1)} custom-call(f32[64,512]{1,0:T(8,128)S(1)} %shard_map.142.a_ref, f32[64,512]{1,0:T(8,128)S(1)} %collective-permute-done.4.b_ref, f32[64,512]{1,0:T(8,128)S(1)} %collective-permute-done.5.c_ref, f32[64,512]{1,0:T(8,128)S(1)} %collective-permute-done.6.d_ref, bf16[64,384]{1,0:T(8,128)(2,1)S(1)} %bitcast.16, ...), custom_call_target="tpu_custom_call" | custom-call | tf_op jit(solution)/shard_map/pallas_call | solution.py:185
  54.9 0.0 copy-start.5
  54.9 0.0 copy-start.7
  54.9 10.2 %all_to_all.11.virtual_ref = bf16[8,64,384]{2,1,0:T(8,128)(2,1)S(1)} all-to-all(bf16[8,64,384]{2,1,0:T(8,128)(2,1)S(1)} %broadcast_in_dim.2), channel_id=1, replica_groups=mesh['x'=4,'zh'=4,'zl'=2,'c'=2,'y'=4] {'x','zl'}, dimensions={0} | all-to-all | bytes 786432 | tf_op jit(solution)/shard_map/all_to_all | solution.py:222
  65.1 0.0 copy-done.5
  65.1 0.0 copy-done.7
  65.2 4.4 %shard_map.144 = (bf16[256,384]{1,0:T(8,128)(2,1)}, bf16[512,384]{1,0:T(8,128)(2,1)}) custom-call(bf16[256,384]{1,0:T(8,128)(2,1)S(1)} %get-tuple-element.10.updated_ref, bf16[256,384]{1,0:T(8,128)(2,1)S(1)} %get-tuple-element.11.query_ref, bf16[8,64,384]{2,1,0:T(8,128)(2,1)S(1)} %all_to_all.11.virtual_ref, bf16[384,768]{1,0:T(8,128)(2,1)S(1)} %copy-done.5, ...), custom_call_target="tpu_custom_call" | custom-call | tf_op jit(solution)/shard_map/pallas_call | solution.py:185
  (2 shorter events, 0.0 us)
Async XLA Ops:
  0.6 6.1 %copy-start = (bf16[64,8,384]{2,1,0:T(8,128)(2,1)S(1)}, bf16[64,8,384]{2,1,0:T(8,128)(2,1)}, u32[]{:S(2)}) copy-start(bf16[64,8,384]{2,1,0:T(8,128)(2,1)} %param.15) | copy-start | bytes 1179652
  0.6 6.2 %copy-start.4 = (bf16[32,8,384]{2,1,0:T(8,128)(2,1)S(1)}, bf16[32,8,384]{2,1,0:T(8,128)(2,1)}, u32[]{:S(2)}) copy-start(bf16[32,8,384]{2,1,0:T(8,128)(2,1)} %param.13) | copy-start | bytes 589828
  0.7 9.1 %collective-permute-start.2 = (bf16[256,384]{1,0:T(8,128)(2,1)}, bf16[256,384]{1,0:T(8,128)(2,1)S(1)}, u32[]{:S(2)}, u32[]{:S(2)}) collective-permute-start(bf16[256,384]{1,0:T(8,128)(2,1)} %bitcast.10), channel_id=1, source_target_pairs={{0,2},{1,3},{2,0},{3,1},{4,6},{5,7},{6,4},{7,5},{8,10},{9,11},{10,... | collective-permute-start | bytes 589832 | tf_op jit(solution)/shard_map/ppermute | solution.py:193
  4.5 9.3 %collective-permute-start.1 = (bf16[256,384]{1,0:T(8,128)(2,1)}, bf16[256,384]{1,0:T(8,128)(2,1)S(1)}, u32[]{:S(2)}, u32[]{:S(2)}) collective-permute-start(bf16[256,384]{1,0:T(8,128)(2,1)} %bitcast.11), channel_id=1, source_target_pairs={{0,3},{1,0},{2,1},{3,2},{4,7},{5,4},{6,5},{7,6},{8,11},{9,8},{10,9... | collective-permute-start | bytes 589832 | tf_op jit(solution)/shard_map/ppermute | solution.py:193
  5.3 9.2 %collective-permute-start = (bf16[256,384]{1,0:T(8,128)(2,1)}, bf16[256,384]{1,0:T(8,128)(2,1)S(1)}, u32[]{:S(2)}, u32[]{:S(2)}) collective-permute-start(bf16[256,384]{1,0:T(8,128)(2,1)} %bitcast.12), channel_id=1, source_target_pairs={{0,1},{1,2},{2,3},{3,0},{4,5},{5,6},{6,7},{7,4},{8,9},{9,10},{10,1... | collective-permute-start | bytes 589832 | tf_op jit(solution)/shard_map/ppermute | solution.py:193
  6.9 1.2 %copy-start.1 = (bf16[384,1152]{1,0:T(8,128)(2,1)S(1)}, bf16[384,1152]{1,0:T(8,128)(2,1)}, u32[]{:S(2)}) copy-start(bf16[384,1152]{1,0:T(8,128)(2,1)} %refs_6_.1) | copy-start | bytes 2654212
  8.0 1.0 %copy-start.8 = (bf16[384,384]{1,0:T(8,128)(2,1)S(1)}, bf16[384,384]{1,0:T(8,128)(2,1)}, u32[]{:S(2)}) copy-start(bf16[384,384]{1,0:T(8,128)(2,1)} %virt_q_ref.1) | copy-start | bytes 884740
  9.0 5.5 %copy-start.2 = (bf16[384,1152]{1,0:T(8,128)(2,1)S(1)}, bf16[384,1152]{1,0:T(8,128)(2,1)}, u32[]{:S(2)}) copy-start(bf16[384,1152]{1,0:T(8,128)(2,1)} %refs_6_.1) | copy-start | bytes 2654212
  9.0 5.5 %copy-start.9 = (bf16[384,384]{1,0:T(8,128)(2,1)S(1)}, bf16[384,384]{1,0:T(8,128)(2,1)}, u32[]{:S(2)}) copy-start(bf16[384,384]{1,0:T(8,128)(2,1)} %refs_7_.1) | copy-start | bytes 884740
  14.5 1.0 %copy-start.10 = (bf16[384,384]{1,0:T(8,128)(2,1)S(1)}, bf16[384,384]{1,0:T(8,128)(2,1)}, u32[]{:S(2)}) copy-start(bf16[384,384]{1,0:T(8,128)(2,1)} %refs_8_.1) | copy-start | bytes 884740
  15.5 17.4 %copy-start.6 = (bf16[384,768]{1,0:T(8,128)(2,1)S(1)}, bf16[384,768]{1,0:T(8,128)(2,1)}, u32[]{:S(2)}) copy-start(bf16[384,768]{1,0:T(8,128)(2,1)} %virt_kv_ref.1) | copy-start | bytes 1769476
  18.6 34.6 %copy-start.3 = (bf16[384,1152]{1,0:T(8,128)(2,1)S(1)}, bf16[384,1152]{1,0:T(8,128)(2,1)}, u32[]{:S(2)}) copy-start(bf16[384,1152]{1,0:T(8,128)(2,1)} %self_qkv_ref.1) | copy-start | bytes 2654212
  29.0 4.0 %collective-permute-start.3 = (bf16[256,384]{1,0:T(8,128)(2,1)S(1)}, bf16[256,384]{1,0:T(8,128)(2,1)S(1)}, u32[]{:S(2)}, u32[]{:S(2)}) collective-permute-start(bf16[256,384]{1,0:T(8,128)(2,1)S(1)} %bitcast.8), channel_id=1, source_target_pairs={{0,4},{4,0},{1,5},{5,1},{2,6},{6,2},{3,7},{7,3},{8,12},{12,8},{9,1... | collective-permute-start | bytes 589832 | tf_op jit(solution)/shard_map/ppermute | solution.py:193
  32.9 20.2 %copy-start.11 = (bf16[384,384]{1,0:T(8,128)(2,1)S(1)}, bf16[384,384]{1,0:T(8,128)(2,1)}, u32[]{:S(2)}) copy-start(bf16[384,384]{1,0:T(8,128)(2,1)} %virt_out_ref.1) | copy-start | bytes 884740
  32.9 20.2 %copy-start.12 = (bf16[384,384]{1,0:T(8,128)(2,1)S(1)}, bf16[384,384]{1,0:T(8,128)(2,1)}, u32[]{:S(2)}) copy-start(bf16[384,384]{1,0:T(8,128)(2,1)} %self_out_ref.1) | copy-start | bytes 884740
  34.3 9.7 %collective-permute-start.6 = (f32[64,512]{1,0:T(8,128)S(1)}, f32[64,512]{1,0:T(8,128)S(1)}, u32[]{:S(2)}, u32[]{:S(2)}) collective-permute-start(f32[64,512]{1,0:T(8,128)S(1)} %shard_map.142.a_ref), channel_id=1, source_target_pairs={{0,32},{16,48},{32,0},{48,16},{1,33},{17,49},{33,1},{49,17},{2,34}... | collective-permute-start | bytes 393224 | tf_op jit(solution)/shard_map/ppermute | solution.py:193
  40.4 12.8 %collective-permute-start.5 = (f32[64,512]{1,0:T(8,128)S(1)}, f32[64,512]{1,0:T(8,128)S(1)}, u32[]{:S(2)}, u32[]{:S(2)}) collective-permute-start(f32[64,512]{1,0:T(8,128)S(1)} %shard_map.142.a_ref), channel_id=1, source_target_pairs={{0,48},{16,0},{32,16},{48,32},{1,49},{17,1},{33,17},{49,33},{2,50}... | collective-permute-start | bytes 393224 | tf_op jit(solution)/shard_map/ppermute | solution.py:193
  40.7 12.5 %collective-permute-start.4 = (f32[64,512]{1,0:T(8,128)S(1)}, f32[64,512]{1,0:T(8,128)S(1)}, u32[]{:S(2)}, u32[]{:S(2)}) collective-permute-start(f32[64,512]{1,0:T(8,128)S(1)} %shard_map.142.a_ref), channel_id=1, source_target_pairs={{0,16},{16,32},{32,48},{48,0},{1,17},{17,33},{33,49},{49,1},{2,18}... | collective-permute-start | bytes 393224 | tf_op jit(solution)/shard_map/ppermute | solution.py:193
  54.9 10.3 %copy-start.5 = (bf16[384,768]{1,0:T(8,128)(2,1)S(1)}, bf16[384,768]{1,0:T(8,128)(2,1)}, u32[]{:S(2)}) copy-start(bf16[384,768]{1,0:T(8,128)(2,1)} %back_kv_ref.1) | copy-start | bytes 1769476
  54.9 10.2 %copy-start.7 = (bf16[384,384]{1,0:T(8,128)(2,1)S(1)}, bf16[384,384]{1,0:T(8,128)(2,1)}, u32[]{:S(2)}) copy-start(bf16[384,384]{1,0:T(8,128)(2,1)} %back_out_ref.1) | copy-start | bytes 884740

commit v2 on v1

v2 whole, which is shorter than its diff:
```python
import jax
import jax.numpy as jnp
from jax import lax
from jax.experimental import pallas as pl
from jax.experimental.pallas import tpu as pltpu
from jax.sharding import Mesh
from jax.sharding import PartitionSpec as P

HEADS = 8
TILE = 256
EPS = 1e-05
NEG = -1e30
LOG2E = 1.4426950408889634
GROUP = 4
STEPS = (2, 1, 3)
EARLY = 1
ZSTEPS = (1, 3, 2)
MARK = 64.0
BF = jnp.bfloat16
F32 = jnp.float32
TRACK_AXES = ("x", "zh", "zl", "c")


def normalize(values):
    widened = values.astype(F32)
    center = jnp.mean(widened, -1, keepdims=True)
    shifted = widened - center
    return (shifted * lax.rsqrt(jnp.mean(shifted * shifted, -1, keepdims=True) + EPS)).astype(BF)


def matmul(a, b):
    return lax.dot_general(a, b, (((1,), (0,)), ((), ())), preferred_element_type=F32)


def matmul_t(a, b):
    return lax.dot_general(a, b, (((1,), (1,)), ((), ())), preferred_element_type=F32)


def iota(shape, dim):
    return lax.broadcasted_iota(jnp.int32, shape, dim)


def scale_of(width):
    return float((width // HEADS) ** (-0.5)) * LOG2E


def tile(rows, j):
    return rows[:, :TILE] if j == 0 else rows[:, rows.shape[1] - TILE :]


def tile_masks(width, j):
    each = width // HEADS
    lane = iota((1, TILE), 1) + j * (width - TILE)
    return [(lane >= h * each) & (lane < (h + 1) * each) for h in range(4 * j, 4 * j + 4)]


def stack_heads(rows, j):
    part = tile(rows, j)
    return jnp.concatenate(
        [part * mask.astype(F32).astype(rows.dtype) for mask in tile_masks(rows.shape[1], j)], axis=0
    )


def pick_heads(stacked, j, width):
    masks = tile_masks(width, j)
    count = stacked.shape[0] // 4
    total = stacked[:count]
    for k in range(1, 4):
        total = jnp.where(masks[k], stacked[k * count : (k + 1) * count], total)
    return total


def join_tiles(a, b, width):
    middle = jnp.where(iota((1, 128), 1) < width // 2 - 128, a[:, 128:], b[:, :128])
    return jnp.concatenate([a[:, :128], middle, b[:, 128:]], axis=1)


def attend(items, width):
    scale = scale_of(width)
    tiles = [(j, *item) for item in items for j in (0, 1)]
    scores = []
    for j, queries, keys, _, bias in tiles:
        raw = matmul_t(stack_heads(queries, j), tile(keys, j))
        if bias is not None:
            raw = (raw.reshape(4, queries.shape[0], -1) + bias).reshape(raw.shape)
        scores.append(raw)
    terms = [jnp.exp2((raw - jnp.max(raw, -1, keepdims=True)) * scale) for raw in scores]
    mixed = []
    for (j, _, _, values, _), term in zip(tiles, terms):
        share = 1.0 / jnp.sum(term, -1, keepdims=True)
        mixed.append(pick_heads(matmul(term.astype(BF), tile(values, j)) * share, j, width))
    return [join_tiles(a, b, width).astype(BF) for a, b in zip(mixed[::2], mixed[1::2])]


def swap_matrix(outer, inner):
    n = outer * inner
    row, col = iota((n, n), 0), iota((n, n), 1)
    source = (row & (inner - 1)) * outer + (row >> (inner.bit_length() - 1))
    return jnp.where(col == source, 1.0, 0.0).astype(BF)


def own_kernel(tokens_ref, virtual_ref, time_qkv_ref, virt_q_ref, qkv_ref, query_ref):
    qkv_ref[...] = matmul(normalize(tokens_ref[...]), time_qkv_ref[...]).astype(BF)
    query_ref[...] = matmul(normalize(virtual_ref[...]), virt_q_ref[...]).astype(BF)


def pair_kernel(tokens_ref, time_qkv_ref, out_ref):
    width = tokens_ref.shape[1]
    out_ref[...] = matmul(normalize(tokens_ref[...]), time_qkv_ref[:, width:]).astype(BF)


def time_kernel(
    frames, group, early, tokens_ref, qkv_ref, *refs
):
    piece_refs = refs[:3]
    visible_ref, time_qkv_ref, time_out_ref, updated_ref, send_ref, normed_ref = refs[3:]
    rows, width = tokens_ref.shape
    tracks = rows // frames
    size = group * frames
    pairs = [qkv_ref[:, width:]] + [ref[...] for ref in piece_refs[:early]]
    pairs += [matmul(normalize(ref[...]), time_qkv_ref[:, width:]).astype(BF) for ref in piece_refs[early:]]
    row, col = iota((size, 4 * size), 0), iota((size, 4 * size), 1)
    bias = jnp.where(row // frames == (col & (size - 1)) // frames, 0.0, NEG)[None]
    items = []
    for start in range(0, rows, size):
        span = slice(start, start + size)
        keys = jnp.concatenate([pair[span, :width] for pair in pairs], axis=0)
        values = jnp.concatenate([pair[span, width:] for pair in pairs], axis=0)
        items.append((qkv_ref[span, :width], keys, values, bias))
    mixed = jnp.concatenate(attend(items, width), axis=0)
    updated = (tokens_ref[...].astype(F32) + matmul(mixed, time_out_ref[...])).astype(BF)
    updated_ref[...] = updated
    normed = matmul(swap_matrix(frames, tracks), normalize(updated))
    pick = jnp.where((iota((rows, tracks), 0) & (tracks - 1)) == iota((rows, tracks), 1), 1.0, 0.0).astype(BF)
    spread = matmul(pick, visible_ref[...].astype(F32).astype(BF))
    here = iota((rows, frames), 0) // tracks == iota((rows, frames), 1)
    seen = jnp.sum(jnp.where(here, spread, 0.0), -1, keepdims=True) > 0.5
    send_ref[...] = jnp.where(seen, normed, MARK).astype(BF)
    normed_ref[...] = normed.astype(BF)


def split(value):
    high = value.astype(BF)
    rest = value - high.astype(F32)
    middle = rest.astype(BF)
    return [high, middle, (rest - middle.astype(F32)).astype(BF)]


def partial_kernel(here_ref, there_ref, query_ref, virt_kv_ref, out_ref):
    width = here_ref.shape[1]
    count = query_ref.shape[0]
    scale = scale_of(width)
    rows = jnp.concatenate([here_ref[...], there_ref[...]], axis=0)
    pair = matmul(rows, virt_kv_ref[...]).astype(BF)
    first = jnp.where(iota((8, width), 1) == 0, 1.0, 0.0).astype(BF)
    bias = jnp.where(matmul_t(first, rows)[:1] < MARK / 2, 0.0, NEG)
    scores = [matmul_t(stack_heads(query_ref[...], j), tile(pair[:, :width], j)) + bias for j in (0, 1)]
    peaks = [jnp.max(raw, -1, keepdims=True) for raw in scores]
    terms = [jnp.exp2((raw - peak) * scale) for raw, peak in zip(scores, peaks)]
    sums = [jnp.sum(term, -1, keepdims=True) for term in terms]
    mixed = [
        pick_heads(matmul(term.astype(BF), tile(pair[:, width:], j)), j, width) for j, term in enumerate(terms)
    ]
    out_ref[:, :width] = join_tiles(*mixed, width).astype(BF)
    lane = iota((count, 128), 1)
    peak, total = jnp.zeros((count, 128), F32), jnp.zeros((count, 128), F32)
    for h in range(HEADS):
        span = slice(h % 4 * count, (h % 4 + 1) * count)
        peak = jnp.where((lane & 7) == h, peaks[h // 4][span], peak)
        total = jnp.where((lane & 7) == h, sums[h // 4][span], total)
    stats = jnp.zeros((count, 128), F32)
    for k, piece in enumerate(split(peak) + split(total)):
        stats = jnp.where(lane >> 3 == k, piece.astype(F32), stats)
    out_ref[:, width:] = stats.astype(BF)


def merge(parts, width):
    scale = scale_of(width)
    each = width // HEADS
    lane, column = iota((128, width), 0), iota((128, width), 1)
    mine = (column >= (lane & 7) * each) & (column < ((lane & 7) + 1) * each)
    spread_peak = jnp.where(mine & (lane < 24), 1.0, 0.0).astype(BF)
    spread_sum = jnp.where(mine & (lane >= 24) & (lane < 48), 1.0, 0.0).astype(BF)
    peaks = [matmul(part[:, width:], spread_peak) for part in parts]
    sums = [matmul(part[:, width:], spread_sum) for part in parts]
    top = peaks[0]
    for peak in peaks[1:]:
        top = jnp.maximum(top, peak)
    weighted, denominator = 0.0, 0.0
    for part, peak, total in zip(parts, peaks, sums):
        weight = jnp.exp2((peak - top) * scale)
        weighted = weighted + weight * part[:, :width].astype(F32)
        denominator = denominator + weight * total
    return (weighted / denominator).astype(BF)


def virtual_kernel(*refs):
    *part_refs, virtual_ref, virt_out_ref, self_qkv_ref, self_out_ref, out_ref = refs
    width = virtual_ref.shape[1]
    attended = merge([ref[...] for ref in part_refs], width)
    cross = (virtual_ref[...].astype(F32) + matmul(attended, virt_out_ref[...])).astype(BF)
    proj = matmul(normalize(cross), self_qkv_ref[...]).astype(BF)
    (mixed,) = attend([(proj[:, :width], proj[:, width : 2 * width], proj[:, 2 * width :], None)], width)
    out_ref[...] = (cross.astype(F32) + matmul(mixed, self_out_ref[...])).astype(BF)


def back_kernel(
    updated_ref, normed_ref, virtual_ref, back_q_ref, back_kv_ref, back_out_ref, out_ref, virtual_out_ref
):
    frames, count, width = virtual_ref.shape
    rows = updated_ref.shape[0]
    tracks = rows // frames
    query = matmul(normed_ref[...], back_q_ref[...]).astype(BF)
    flat = virtual_ref[...].reshape(frames * count, width)
    pair = matmul(normalize(flat), back_kv_ref[...]).astype(BF)
    items = []
    for f in range(frames):
        span = slice(f * count, (f + 1) * count)
        items.append((query[f * tracks : (f + 1) * tracks], pair[span, :width], pair[span, width:], None))
    mixed = jnp.concatenate(attend(items, width), axis=0)
    by_track = matmul(swap_matrix(tracks, frames), mixed).astype(BF)
    out_ref[...] = (updated_ref[...].astype(F32) + matmul(by_track, back_out_ref[...])).astype(BF)
    step = count // 4
    for start in range(0, count, step):
        block = jnp.concatenate([virtual_ref[f, start : start + step] for f in range(frames)], axis=0)
        virtual_out_ref[start * frames : (start + step) * frames] = matmul(
            swap_matrix(step, frames), block
        ).astype(BF)


def call(kernel, outs, *args, megabytes=32):
    return pl.pallas_call(
        kernel,
        out_shape=[jax.ShapeDtypeStruct(shape, dtype) for shape, dtype in outs],
        compiler_params=pltpu.CompilerParams(vmem_limit_bytes=megabytes * 1024 * 1024),
    )(*args)


def shift(value, axis, count, step):
    return lax.ppermute(value, axis, [(i, (i + step) % count) for i in range(count)])


def on_device(
    tokens, visible, virtual, time_qkv, time_out, virt_q, virt_kv, virt_out, self_qkv, self_out, back_q, back_kv,
    back_out,
):
    tracks, frames, width = tokens.shape
    count = virtual.shape[0]
    rows = tracks * frames
    flat = tokens.reshape(rows, width)
    others = [shift(flat, "y", 4, step) for step in STEPS]
    frame = lax.axis_index("x") * 2 + lax.axis_index("zl")
    mine = lax.dynamic_slice_in_dim(virtual, frame, 1, axis=1).reshape(count, width)
    qkv, virt_query = call(
        own_kernel, [((rows, 3 * width), BF), ((count, width), BF)], flat, mine, time_qkv, virt_q
    )
    for k in range(EARLY):
        (others[k],) = call(pair_kernel, [((rows, 2 * width), BF)], others[k], time_qkv)
    updated, send, normed = call(
        lambda *refs: time_kernel(frames, GROUP, EARLY, *refs),
        [((rows, width), BF)] * 3,
        flat, qkv, *others, visible, time_qkv, time_out,
    )
    got = lax.all_to_all(send.reshape(frames, tracks, width), ("x", "zl"), 0, 0).reshape(rows, width)
    got_there = shift(got, "c", 2, 1)
    (partial,) = call(partial_kernel, [((count, width + 128), BF)], got, got_there, virt_query, virt_kv)
    partials = [partial] + [shift(partial, "zh", 4, step) for step in ZSTEPS]
    (frame_out,) = call(
        virtual_kernel, [((count, width), BF)], *partials, mine, virt_out, self_qkv, self_out
    )
    gathered = lax.all_to_all(
        jnp.broadcast_to(frame_out[None], (frames, count, width)), ("x", "zl"), 0, 0
    )
    tracks_out, virtual_out = call(
        back_kernel,
        [((rows, width), BF), ((count * frames, width), BF)],
        updated, normed, gathered, back_q, back_kv, back_out,
    )
    return tracks_out.reshape(tokens.shape), virtual_out.reshape(virtual.shape)


def solution(mesh):
    fine = Mesh(mesh.devices.reshape(4, 4, 2, 2, 4), ("x", "zh", "zl", "c", "y"))
    tokens = P(TRACK_AXES, "y", None)
    virtual = P(None, "y", None)
    return jax.shard_map(
        on_device,
        mesh=fine,
        in_specs=(tokens, P(TRACK_AXES, "y"), virtual) + (P(),) * 10,
        out_specs=(tokens, virtual),
        check_vma=False,
    )
```

time: 70.2 us -> 60.3 us (0.86)
  waiting for transfers between devices: 16.3 us -> 9.63 us
  Pallas kernels: 11.3 us -> 8.54 us
    ppermute x7, waiting for transfers between devices: 16.3 us -> 9.63 us  [shift(): lax.ppermute(value, axis, [(i, (i + step) % count) for i in range(count)])]
    pallas_call x5 -> x6, Pallas kernels: 11.3 us -> 8.54 us  [call(): pl.pallas_call(kernel, out_shape=[jax.ShapeDtypeStruct(shape, dtype) for...]
  transfers between devices with their start and end apart: 7 -> 7, of which waited for: 5 -> 4; matrix products, arithmetic and copies ran while one was open for 1% -> 1% of each run, Pallas kernels for 1% -> 2%
where the time goes in v2:
time: 60.3 us; the launch traced here: 59.3 us
  blocking collectives  20.2 us (33%)
  starting transfers between devices  16.6 us (28%)
  waiting for transfers between devices  9.63 us (16%)
  Pallas kernels  8.54 us (14%)
  local copies, waits for them, and re-layouts  3.53 us (6%)
  between operations  0.79 us (1%)
    ppermute x7, starting transfers between devices, shift(): lax.ppermute(value, axis, [(i, (i + step) % count) for i in range(count)])  16.6 us
    all_to_all x1, blocking collectives, on_device(): lax.all_to_all(send.reshape(frames, tracks, width), ('x', 'zl'), 0, 0)  10.4 us
    all_to_all x1, blocking collectives, on_device(): lax.all_to_all(jnp.broadcast_to(frame_out[None], (frames, count, width)),...  9.85 us
    ppermute x7, waiting for transfers between devices, shift(): lax.ppermute(value, axis, [(i, (i + step) % count) for i in range(count)])  9.63 us
    pallas_call x6, Pallas kernels, call(): pl.pallas_call(kernel, out_shape=[jax.ShapeDtypeStruct(shape, dtype) for...  8.54 us
    unnamed x28, local copies, waits for them, and re-layouts  3.38 us
  transfers between devices with their start and end apart: 7, of which 4 were waited for; matrix products, arithmetic and copies ran while one was open for 1% of the time, Pallas kernels for 2%

profile of v2, /device:TPU:1, one launch (start us, length us, event | category | flops | bytes accessed | tf_op | source)
XLA Modules:
  0.0 59.3 jit_solution(14584409988536545812)
XLA Ops:
  0.6 0.0 copy-start
  0.6 0.0 copy-start.4
  0.7 3.8 %collective-permute-start = (bf16[256,384]{1,0:T(8,128)(2,1)}, bf16[256,384]{1,0:T(8,128)(2,1)S(1)}, u32[]{:S(2)}, u32[]{:S(2)}) collective-permute-start(bf16[256,384]{1,0:T(8,128)(2,1)} %bitcast.10), channel_id=1, source_target_pairs={{0,2},{1,3},{2,0},{3,1},{4,6},{5,7},{6,4},{7,5},{8,10},{9,11},{10,... | collective-permute-start | bytes 589832 | tf_op jit(solution)/shard_map/ppermute | solution.py:240
  4.5 0.8 %collective-permute-start.2 = (bf16[256,384]{1,0:T(8,128)(2,1)}, bf16[256,384]{1,0:T(8,128)(2,1)S(1)}, u32[]{:S(2)}, u32[]{:S(2)}) collective-permute-start(bf16[256,384]{1,0:T(8,128)(2,1)} %bitcast.11), channel_id=1, source_target_pairs={{0,3},{1,0},{2,1},{3,2},{4,7},{5,4},{6,5},{7,6},{8,11},{9,8},{10,9... | collective-permute-start | bytes 589832 | tf_op jit(solution)/shard_map/ppermute | solution.py:240
  5.3 0.7 %collective-permute-start.1 = (bf16[256,384]{1,0:T(8,128)(2,1)}, bf16[256,384]{1,0:T(8,128)(2,1)S(1)}, u32[]{:S(2)}, u32[]{:S(2)}) collective-permute-start(bf16[256,384]{1,0:T(8,128)(2,1)} %bitcast.12), channel_id=1, source_target_pairs={{0,1},{1,2},{2,3},{3,0},{4,5},{5,6},{6,7},{7,4},{8,9},{9,10},{10,1... | collective-permute-start | bytes 589832 | tf_op jit(solution)/shard_map/ppermute | solution.py:240
  6.0 0.8 %copy.17.refs_5_ = s32[32,8]{1,0:T(8,128)S(1)} copy(s32[32,8]{0,1:T(8,128)} %param.14) | data formatting | bytes 2048 | tf_op args[1]
  6.7 0.0 copy-done
  6.7 0.1 constant_dynamic-slice_fusion
  6.8 0.0 copy-done.4
  6.9 0.0 copy-start.1
  6.9 1.2 %copy-done.1 = bf16[384,1152]{1,0:T(8,128)(2,1)S(1)} copy-done((bf16[384,1152]{1,0:T(8,128)(2,1)S(1)}, bf16[384,1152]{1,0:T(8,128)(2,1)}, u32[]{:S(2)}) %copy-start.1) | copy-done | bytes 884760
  8.0 0.0 copy-start.9
  8.0 1.0 %copy-done.9 = bf16[384,384]{1,0:T(8,128)(2,1)S(1)} copy-done((bf16[384,384]{1,0:T(8,128)(2,1)S(1)}, bf16[384,384]{1,0:T(8,128)(2,1)}, u32[]{:S(2)}) %copy-start.9) | copy-done | bytes 294936
  9.0 0.0 copy-start.2
  9.0 0.7 %shard_map.140 = (bf16[256,1152]{1,0:T(8,128)(2,1)S(1)}, bf16[64,384]{1,0:T(8,128)(2,1)S(1)}) custom-call(bf16[256,384]{1,0:T(8,128)(2,1)S(1)} %bitcast.13, bf16[64,384]{1,0:T(8,128)(2,1)S(1)} %bitcast.15, bf16[384,1152]{1,0:T(8,128)(2,1)S(1)} %copy-done.1, bf16[384,384]{1,0:T(8,128)(2,1)S(1)} %copy-done.9), custom_call_target="tpu_custom_call" | custom-call | tf_op jit(solution)/shard_map/pallas_call | solution.py:232
  9.7 0.0 copy-start.10
  9.7 0.0 collective-permute-done.tokens_ref
  9.7 0.4 copy-done.2
  10.2 0.5 shard_map.141.refs_2_
  10.7 3.0 %collective-permute-done.2.refs_4_ = bf16[256,384]{1,0:T(8,128)(2,1)S(1)} collective-permute-done((bf16[256,384]{1,0:T(8,128)(2,1)}, bf16[256,384]{1,0:T(8,128)(2,1)S(1)}, u32[]{:S(2)}, u32[]{:S(2)}) %collective-permute-start.2) | collective-permute-done | bytes 196640 | tf_op jit(solution)/shard_map/ppermute | solution.py:240
  13.8 0.8 %collective-permute-done.1.refs_3_ = bf16[256,384]{1,0:T(8,128)(2,1)S(1)} collective-permute-done((bf16[256,384]{1,0:T(8,128)(2,1)}, bf16[256,384]{1,0:T(8,128)(2,1)S(1)}, u32[]{:S(2)}, u32[]{:S(2)}) %collective-permute-start.1) | collective-permute-done | bytes 196640 | tf_op jit(solution)/shard_map/ppermute | solution.py:240
  14.5 0.0 copy-done.10
  14.5 0.0 copy-start.5
  14.5 2.1 %shard_map.142 = (bf16[256,384]{1,0:T(8,128)(2,1)S(1)}, bf16[256,384]{1,0:T(8,128)(2,1)S(1)}, bf16[256,384]{1,0:T(8,128)(2,1)S(1)}) custom-call(bf16[256,384]{1,0:T(8,128)(2,1)S(1)} %bitcast.14, bf16[256,1152]{1,0:T(8,128)(2,1)S(1)} %get-tuple-element.9.refs_1_, bf16[256,768]{1,0:T(8,128)(2,1)S(1)} %shard_map.141.refs_2_, ...), custom_call_target="tpu_custom_call" | custom-call | tf_op jit(solution)/shard_map/pallas_call | solution.py:232
  16.6 0.0 copy-start.3
  16.6 10.4 %all_to_all.10 = bf16[8,32,384]{2,1,0:T(8,128)(2,1)S(1)} all-to-all(bf16[8,32,384]{2,1,0:T(8,128)(2,1)S(1)} %bitcast.17), channel_id=1, replica_groups=mesh['x'=4,'zh'=4,'zl'=2,'c'=2,'y'=4] {'x','zl'}, dimensions={0} | all-to-all | bytes 393216 | tf_op jit(solution)/shard_map/all_to_all | solution.py:264
  27.0 2.9 %collective-permute-start.3 = (bf16[256,384]{1,0:T(8,128)(2,1)S(1)}, bf16[256,384]{1,0:T(8,128)(2,1)S(1)}, u32[]{:S(2)}, u32[]{:S(2)}) collective-permute-start(bf16[256,384]{1,0:T(8,128)(2,1)S(1)} %bitcast.8), channel_id=1, source_target_pairs={{0,4},{4,0},{1,5},{5,1},{2,6},{6,2},{3,7},{7,3},{8,12},{12,8},{9,1... | collective-permute-start | bytes 589832 | tf_op jit(solution)/shard_map/ppermute | solution.py:240
  29.8 1.1 %collective-permute-done.3.there_ref = bf16[256,384]{1,0:T(8,128)(2,1)S(1)} collective-permute-done((bf16[256,384]{1,0:T(8,128)(2,1)S(1)}, bf16[256,384]{1,0:T(8,128)(2,1)S(1)}, u32[]{:S(2)}, u32[]{:S(2)}) %collective-permute-start.3) | collective-permute-done | bytes 196640 | tf_op jit(solution)/shard_map/ppermute | solution.py:240
  30.9 0.0 copy-done.5
  30.9 0.0 copy-start.7
  30.9 0.0 copy-start.8
  30.9 1.1 %shard_map.143.refs_0_ = bf16[64,512]{1,0:T(8,128)(2,1)S(1)} custom-call(bf16[256,384]{1,0:T(8,128)(2,1)S(1)} %bitcast.9, bf16[256,384]{1,0:T(8,128)(2,1)S(1)} %collective-permute-done.3.there_ref, bf16[64,384]{1,0:T(8,128)(2,1)S(1)} %get-tuple-element.13.query_ref, bf16[384,768]{1,0:T(8,128)(2,1)S(1)} %copy-done.5), custom_call_target="tpu_custom_call" | custom-call | tf_op jit(solution)/shard_map/pallas_call | solution.py:232
  32.1 6.1 %collective-permute-start.6 = (bf16[64,512]{1,0:T(8,128)(2,1)S(1)}, bf16[64,512]{1,0:T(8,128)(2,1)S(1)}, u32[]{:S(2)}, u32[]{:S(2)}) collective-permute-start(bf16[64,512]{1,0:T(8,128)(2,1)S(1)} %shard_map.143.refs_0_), channel_id=1, source_target_pairs={{0,32},{16,48},{32,0},{48,16},{1,33},{17,49},{33,1},{49,17},{2,34}... | collective-permute-start | bytes 196616 | tf_op jit(solution)/shard_map/ppermute | solution.py:240
  38.2 0.3 collective-permute-start.5
  38.5 2.1 %collective-permute-start.4 = (bf16[64,512]{1,0:T(8,128)(2,1)S(1)}, bf16[64,512]{1,0:T(8,128)(2,1)S(1)}, u32[]{:S(2)}, u32[]{:S(2)}) collective-permute-start(bf16[64,512]{1,0:T(8,128)(2,1)S(1)} %shard_map.143.refs_0_), channel_id=1, source_target_pairs={{0,16},{16,32},{32,48},{48,0},{1,17},{17,33},{33,49},{49,1},{2,18}... | collective-permute-start | bytes 196616 | tf_op jit(solution)/shard_map/ppermute | solution.py:240
  40.5 0.0 collective-permute-done.6.refs_3_
  40.5 4.8 %collective-permute-done.5.refs_2_ = bf16[64,512]{1,0:T(8,128)(2,1)S(1)} collective-permute-done((bf16[64,512]{1,0:T(8,128)(2,1)S(1)}, bf16[64,512]{1,0:T(8,128)(2,1)S(1)}, u32[]{:S(2)}, u32[]{:S(2)}) %collective-permute-start.5) | collective-permute-done | bytes 65568 | tf_op jit(solution)/shard_map/ppermute | solution.py:240
  45.3 0.0 collective-permute-done.4.refs_1_
  45.3 0.0 copy-done.3
  45.3 0.0 copy-done.7
  45.3 0.0 copy-done.8
  45.3 1.4 %shard_map.144 = bf16[64,384]{1,0:T(8,128)(2,1)S(1)} custom-call(bf16[64,512]{1,0:T(8,128)(2,1)S(1)} %shard_map.143.refs_0_, bf16[64,512]{1,0:T(8,128)(2,1)S(1)} %collective-permute-done.4.refs_1_, bf16[64,512]{1,0:T(8,128)(2,1)S(1)} %collective-permute-done.5.refs_2_, bf16[64,512]{1,0:T(8,128)(2,1)S(1)} %collective-permute-done.6.refs_3_, ...), custom_call_target="tpu_custom_call" | custom-call | tf_op jit(solution)/shard_map/pallas_call | solution.py:232
  46.7 0.0 copy-start.6
  46.8 0.0 copy-start.11
  46.8 0.0 copy-start.12
  46.8 9.8 %all_to_all.11.virtual_ref = bf16[8,64,384]{2,1,0:T(8,128)(2,1)S(1)} all-to-all(bf16[8,64,384]{2,1,0:T(8,128)(2,1)S(1)} %broadcast_in_dim.2), channel_id=1, replica_groups=mesh['x'=4,'zh'=4,'zl'=2,'c'=2,'y'=4] {'x','zl'}, dimensions={0} | all-to-all | bytes 786432 | tf_op jit(solution)/shard_map/all_to_all | solution.py:271
  56.6 0.0 copy-done.6
  56.6 0.0 copy-done.11
  56.6 0.0 copy-done.12
  56.6 2.7 %shard_map.145 = (bf16[256,384]{1,0:T(8,128)(2,1)}, bf16[512,384]{1,0:T(8,128)(2,1)}) custom-call(bf16[256,384]{1,0:T(8,128)(2,1)S(1)} %get-tuple-element.10.updated_ref, bf16[256,384]{1,0:T(8,128)(2,1)S(1)} %get-tuple-element.11.normed_ref, bf16[8,64,384]{2,1,0:T(8,128)(2,1)S(1)} %all_to_all.11.virtual_ref, bf16[384,384]{1,0:T(8,128)(2,1)S(1)} %copy-done.11, ...), custom_call_target="tpu_custom_call" | custom-call | tf_op jit(solution)/shard_map/pallas_call | solution.py:232
  (2 shorter events, 0.0 us)
Async XLA Ops:
  0.6 6.1 %copy-start = (bf16[64,8,384]{2,1,0:T(8,128)(2,1)S(1)}, bf16[64,8,384]{2,1,0:T(8,128)(2,1)}, u32[]{:S(2)}) copy-start(bf16[64,8,384]{2,1,0:T(8,128)(2,1)} %param.15) | copy-start | bytes 1179652
  0.6 6.2 %copy-start.4 = (bf16[32,8,384]{2,1,0:T(8,128)(2,1)S(1)}, bf16[32,8,384]{2,1,0:T(8,128)(2,1)}, u32[]{:S(2)}) copy-start(bf16[32,8,384]{2,1,0:T(8,128)(2,1)} %param.13) | copy-start | bytes 589828
  0.7 9.1 %collective-permute-start = (bf16[256,384]{1,0:T(8,128)(2,1)}, bf16[256,384]{1,0:T(8,128)(2,1)S(1)}, u32[]{:S(2)}, u32[]{:S(2)}) collective-permute-start(bf16[256,384]{1,0:T(8,128)(2,1)} %bitcast.10), channel_id=1, source_target_pairs={{0,2},{1,3},{2,0},{3,1},{4,6},{5,7},{6,4},{7,5},{8,10},{9,11},{10,... | collective-permute-start | bytes 589832 | tf_op jit(solution)/shard_map/ppermute | solution.py:240
  4.5 9.3 %collective-permute-start.2 = (bf16[256,384]{1,0:T(8,128)(2,1)}, bf16[256,384]{1,0:T(8,128)(2,1)S(1)}, u32[]{:S(2)}, u32[]{:S(2)}) collective-permute-start(bf16[256,384]{1,0:T(8,128)(2,1)} %bitcast.11), channel_id=1, source_target_pairs={{0,3},{1,0},{2,1},{3,2},{4,7},{5,4},{6,5},{7,6},{8,11},{9,8},{10,9... | collective-permute-start | bytes 589832 | tf_op jit(solution)/shard_map/ppermute | solution.py:240
  5.3 9.2 %collective-permute-start.1 = (bf16[256,384]{1,0:T(8,128)(2,1)}, bf16[256,384]{1,0:T(8,128)(2,1)S(1)}, u32[]{:S(2)}, u32[]{:S(2)}) collective-permute-start(bf16[256,384]{1,0:T(8,128)(2,1)} %bitcast.12), channel_id=1, source_target_pairs={{0,1},{1,2},{2,3},{3,0},{4,5},{5,6},{6,7},{7,4},{8,9},{9,10},{10,1... | collective-permute-start | bytes 589832 | tf_op jit(solution)/shard_map/ppermute | solution.py:240
  6.9 1.2 %copy-start.1 = (bf16[384,1152]{1,0:T(8,128)(2,1)S(1)}, bf16[384,1152]{1,0:T(8,128)(2,1)}, u32[]{:S(2)}) copy-start(bf16[384,1152]{1,0:T(8,128)(2,1)} %refs_6_.2) | copy-start | bytes 2654212
  8.0 1.0 %copy-start.9 = (bf16[384,384]{1,0:T(8,128)(2,1)S(1)}, bf16[384,384]{1,0:T(8,128)(2,1)}, u32[]{:S(2)}) copy-start(bf16[384,384]{1,0:T(8,128)(2,1)} %virt_q_ref.1) | copy-start | bytes 884740
  9.0 1.2 %copy-start.2 = (bf16[384,1152]{1,0:T(8,128)(2,1)S(1)}, bf16[384,1152]{1,0:T(8,128)(2,1)}, u32[]{:S(2)}) copy-start(bf16[384,1152]{1,0:T(8,128)(2,1)} %refs_6_.2) | copy-start | bytes 2654212
  9.7 4.8 %copy-start.10 = (bf16[384,384]{1,0:T(8,128)(2,1)S(1)}, bf16[384,384]{1,0:T(8,128)(2,1)}, u32[]{:S(2)}) copy-start(bf16[384,384]{1,0:T(8,128)(2,1)} %refs_7_.2) | copy-start | bytes 884740
  14.5 16.4 %copy-start.5 = (bf16[384,768]{1,0:T(8,128)(2,1)S(1)}, bf16[384,768]{1,0:T(8,128)(2,1)}, u32[]{:S(2)}) copy-start(bf16[384,768]{1,0:T(8,128)(2,1)} %virt_kv_ref.1) | copy-start | bytes 1769476
  16.6 28.7 %copy-start.3 = (bf16[384,1152]{1,0:T(8,128)(2,1)S(1)}, bf16[384,1152]{1,0:T(8,128)(2,1)}, u32[]{:S(2)}) copy-start(bf16[384,1152]{1,0:T(8,128)(2,1)} %refs_6_.3) | copy-start | bytes 2654212
  27.0 4.0 %collective-permute-start.3 = (bf16[256,384]{1,0:T(8,128)(2,1)S(1)}, bf16[256,384]{1,0:T(8,128)(2,1)S(1)}, u32[]{:S(2)}, u32[]{:S(2)}) collective-permute-start(bf16[256,384]{1,0:T(8,128)(2,1)S(1)} %bitcast.8), channel_id=1, source_target_pairs={{0,4},{4,0},{1,5},{5,1},{2,6},{6,2},{3,7},{7,3},{8,12},{12,8},{9,1... | collective-permute-start | bytes 589832 | tf_op jit(solution)/shard_map/ppermute | solution.py:240
  30.9 14.4 %copy-start.7 = (bf16[384,384]{1,0:T(8,128)(2,1)S(1)}, bf16[384,384]{1,0:T(8,128)(2,1)}, u32[]{:S(2)}) copy-start(bf16[384,384]{1,0:T(8,128)(2,1)} %refs_5_.2) | copy-start | bytes 884740
  30.9 14.4 %copy-start.8 = (bf16[384,384]{1,0:T(8,128)(2,1)S(1)}, bf16[384,384]{1,0:T(8,128)(2,1)}, u32[]{:S(2)}) copy-start(bf16[384,384]{1,0:T(8,128)(2,1)} %refs_7_.3) | copy-start | bytes 884740
  32.1 8.5 %collective-permute-start.6 = (bf16[64,512]{1,0:T(8,128)(2,1)S(1)}, bf16[64,512]{1,0:T(8,128)(2,1)S(1)}, u32[]{:S(2)}, u32[]{:S(2)}) collective-permute-start(bf16[64,512]{1,0:T(8,128)(2,1)S(1)} %shard_map.143.refs_0_), channel_id=1, source_target_pairs={{0,32},{16,48},{32,0},{48,16},{1,33},{17,49},{33,1},{49,17},{2,34}... | collective-permute-start | bytes 196616 | tf_op jit(solution)/shard_map/ppermute | solution.py:240
  38.2 7.1 %collective-permute-start.5 = (bf16[64,512]{1,0:T(8,128)(2,1)S(1)}, bf16[64,512]{1,0:T(8,128)(2,1)S(1)}, u32[]{:S(2)}, u32[]{:S(2)}) collective-permute-start(bf16[64,512]{1,0:T(8,128)(2,1)S(1)} %shard_map.143.refs_0_), channel_id=1, source_target_pairs={{0,48},{16,0},{32,16},{48,32},{1,49},{17,1},{33,17},{49,33},{2,50}... | collective-permute-start | bytes 196616 | tf_op jit(solution)/shard_map/ppermute | solution.py:240
  38.5 6.9 %collective-permute-start.4 = (bf16[64,512]{1,0:T(8,128)(2,1)S(1)}, bf16[64,512]{1,0:T(8,128)(2,1)S(1)}, u32[]{:S(2)}, u32[]{:S(2)}) collective-permute-start(bf16[64,512]{1,0:T(8,128)(2,1)S(1)} %shard_map.143.refs_0_), channel_id=1, source_target_pairs={{0,16},{16,32},{32,48},{48,0},{1,17},{17,33},{33,49},{49,1},{2,18}... | collective-permute-start | bytes 196616 | tf_op jit(solution)/shard_map/ppermute | solution.py:240
  46.7 9.9 %copy-start.6 = (bf16[384,768]{1,0:T(8,128)(2,1)S(1)}, bf16[384,768]{1,0:T(8,128)(2,1)}, u32[]{:S(2)}) copy-start(bf16[384,768]{1,0:T(8,128)(2,1)} %back_kv_ref.1) | copy-start | bytes 1769476
  46.8 9.9 %copy-start.11 = (bf16[384,384]{1,0:T(8,128)(2,1)S(1)}, bf16[384,384]{1,0:T(8,128)(2,1)}, u32[]{:S(2)}) copy-start(bf16[384,384]{1,0:T(8,128)(2,1)} %back_q_ref.1) | copy-start | bytes 884740
  46.8 9.9 %copy-start.12 = (bf16[384,384]{1,0:T(8,128)(2,1)S(1)}, bf16[384,384]{1,0:T(8,128)(2,1)}, u32[]{:S(2)}) copy-start(bf16[384,384]{1,0:T(8,128)(2,1)} %back_out_ref.1) | copy-start | bytes 884740

commit v3 on v2

--- a/solution.py
+++ b/solution.py
@@ -146,11 +146,19 @@
     return [high, middle, (rest - middle.astype(F32)).astype(BF)]
 
 
-def partial_kernel(here_ref, there_ref, query_ref, virt_kv_ref, out_ref):
-    width = here_ref.shape[1]
+def pack_stats(peak, total):
+    lane = iota(peak.shape, 1)
+    stats = jnp.zeros(peak.shape, F32)
+    for k, piece in enumerate(split(peak) + split(total)):
+        stats = jnp.where(lane >> 3 == k, piece.astype(F32), stats)
+    return stats.astype(BF)
+
+
+def partial_kernel(rows_ref, query_ref, virt_kv_ref, out_ref):
+    rows = rows_ref[...]
+    width = rows.shape[1]
     count = query_ref.shape[0]
     scale = scale_of(width)
-    rows = jnp.concatenate([here_ref[...], there_ref[...]], axis=0)
     pair = matmul(rows, virt_kv_ref[...]).astype(BF)
     first = jnp.where(iota((8, width), 1) == 0, 1.0, 0.0).astype(BF)
     bias = jnp.where(matmul_t(first, rows)[:1] < MARK / 2, 0.0, NEG)
@@ -168,10 +176,7 @@
         span = slice(h % 4 * count, (h % 4 + 1) * count)
         peak = jnp.where((lane & 7) == h, peaks[h // 4][span], peak)
         total = jnp.where((lane & 7) == h, sums[h // 4][span], total)
-    stats = jnp.zeros((count, 128), F32)
-    for k, piece in enumerate(split(peak) + split(total)):
-        stats = jnp.where(lane >> 3 == k, piece.astype(F32), stats)
-    out_ref[:, width:] = stats.astype(BF)
+    out_ref[:, width:] = pack_stats(peak, total)
 
 
 def merge(parts, width):
@@ -194,8 +199,36 @@
     return (weighted / denominator).astype(BF)
 
 
+def both_kernel(a_ref, b_ref, out_ref):
+    width = a_ref.shape[1] - 128
+    scale = scale_of(width)
+    each = width // HEADS
+    source, lane = iota((128, 256), 0), iota((128, 256), 1)
+    same = (source & 7) == (lane & 7)
+    here = ((lane < 128) & (source < 24)) | ((lane >= 128) & (source >= 24) & (source < 48))
+    gather = jnp.where(same & here, 1.0, 0.0).astype(BF)
+    parts = [a_ref[...], b_ref[...]]
+    stats = [matmul(part[:, width:], gather) for part in parts]
+    peaks, sums = [s[:, :128] for s in stats], [s[:, 128:] for s in stats]
+    top = jnp.maximum(*peaks)
+    weights = [jnp.exp2((peak - top) * scale) for peak in peaks]
+    lane, column = iota((128, width), 0), iota((128, width), 1)
+    spread = jnp.where(
+        (column >= (lane & 7) * each) & (column < ((lane & 7) + 1) * each) & (lane < 16), 1.0, 0.0
+    ).astype(BF)
+    total, mixed = 0.0, 0.0
+    for part, weight, count in zip(parts, weights, sums):
+        high = weight.astype(BF)
+        low = weight - high.astype(F32)
+        pieces = jnp.where(iota(weight.shape, 1) < 8, high.astype(F32), low).astype(BF)
+        mixed = mixed + matmul(pieces, spread) * part[:, :width].astype(F32)
+        total = total + weight * count
+    out_ref[:, :width] = mixed.astype(BF)
+    out_ref[:, width:] = pack_stats(top, total)
+
+
 def virtual_kernel(*refs):
-    *part_refs, virtual_ref, virt_out_ref, self_qkv_ref, self_out_ref, out_ref = refs
+    _, *part_refs, virtual_ref, virt_out_ref, self_qkv_ref, self_out_ref, out_ref = refs
     width = virtual_ref.shape[1]
     attended = merge([ref[...] for ref in part_refs], width)
     cross = (virtual_ref[...].astype(F32) + matmul(attended, virt_out_ref[...])).astype(BF)
@@ -204,13 +237,23 @@
     out_ref[...] = (cross.astype(F32) + matmul(mixed, self_out_ref[...])).astype(BF)
 
 
+def query_kernel(normed_ref, back_q_ref, out_ref):
+    out_ref[...] = matmul(normed_ref[...], back_q_ref[...]).astype(BF)
+
+
 def back_kernel(
-    updated_ref, normed_ref, virtual_ref, back_q_ref, back_kv_ref, back_out_ref, out_ref, virtual_out_ref
+    updated_ref, query_ref, virtual_ref, back_kv_ref, back_out_ref, out_ref, virtual_out_ref
 ):
     frames, count, width = virtual_ref.shape
     rows = updated_ref.shape[0]
     tracks = rows // frames
-    query = matmul(normed_ref[...], back_q_ref[...]).astype(BF)
+    step = count // 4
+    for start in range(0, count, step):
+        block = jnp.concatenate([virtual_ref[f, start : start + step] for f in range(frames)], axis=0)
+        virtual_out_ref[start * frames : (start + step) * frames] = matmul(
+            swap_matrix(step, frames), block
+        ).astype(BF)
+    query = query_ref[...]
     flat = virtual_ref[...].reshape(frames * count, width)
     pair = matmul(normalize(flat), back_kv_ref[...]).astype(BF)
     items = []
@@ -220,12 +263,6 @@
     mixed = jnp.concatenate(attend(items, width), axis=0)
     by_track = matmul(swap_matrix(tracks, frames), mixed).astype(BF)
     out_ref[...] = (updated_ref[...].astype(F32) + matmul(by_track, back_out_ref[...])).astype(BF)
-    step = count // 4
-    for start in range(0, count, step):
-        block = jnp.concatenate([virtual_ref[f, start : start + step] for f in range(frames)], axis=0)
-        virtual_out_ref[start * frames : (start + step) * frames] = matmul(
-            swap_matrix(step, frames), block
-        ).astype(BF)
 
 
 def call(kernel, outs, *args, megabytes=32):
@@ -262,11 +299,12 @@
         flat, qkv, *others, visible, time_qkv, time_out,
     )
     got = lax.all_to_all(send.reshape(frames, tracks, width), ("x", "zl"), 0, 0).reshape(rows, width)
-    got_there = shift(got, "c", 2, 1)
-    (partial,) = call(partial_kernel, [((count, width + 128), BF)], got, got_there, virt_query, virt_kv)
-    partials = [partial] + [shift(partial, "zh", 4, step) for step in ZSTEPS]
+    (partial,) = call(partial_kernel, [((count, width + 128), BF)], got, virt_query, virt_kv)
+    (partial,) = call(both_kernel, [((count, width + 128), BF)], partial, shift(partial, "c", 2, 1))
+    (query,) = call(query_kernel, [((rows, width), BF)], normed, back_q)
+    partials = [partial] + [lax.ppermute(partial, "zh", [(i, i ^ k) for i in range(4)]) for k in ZSTEPS]
     (frame_out,) = call(
-        virtual_kernel, [((count, width), BF)], *partials, mine, virt_out, self_qkv, self_out
+        virtual_kernel, [((count, width), BF)], query, *partials, mine, virt_out, self_qkv, self_out
     )
     gathered = lax.all_to_all(
         jnp.broadcast_to(frame_out[None], (frames, count, width)), ("x", "zl"), 0, 0
@@ -274,7 +312,7 @@
     tracks_out, virtual_out = call(
         back_kernel,
         [((rows, width), BF), ((count * frames, width), BF)],
-        updated, normed, gathered, back_q, back_kv, back_out,
+        updated, query, gathered, back_kv, back_out,
     )
     return tracks_out.reshape(tokens.shape), virtual_out.reshape(virtual.shape)
 

time: 60.3 us -> 59.7 us (0.990)
  starting transfers between devices: 16.6 us -> 15.6 us
    ppermute x7 -> x4, starting transfers between devices: 16.6 us -> 8.27 us  [shift(): lax.ppermute(value, axis, [(i, (i + step) % count) for i in range(count)])]
    ppermute x0 -> x3, starting transfers between devices: none -> 7.29 us  [on_device(): lax.ppermute(partial, 'zh', [(i, i ^ k) for i in range(4)])]
    ppermute x0 -> x3, waiting for transfers between devices: none -> 5.53 us  [on_device(): lax.ppermute(partial, 'zh', [(i, i ^ k) for i in range(4)])]
    ppermute x7 -> x4, waiting for transfers between devices: 9.63 us -> 4.71 us  [shift(): lax.ppermute(value, axis, [(i, (i + step) % count) for i in range(count)])]
    pallas_call x6 -> x8, Pallas kernels: 8.54 us -> 8.54 us  [call(): pl.pallas_call(kernel, out_shape=[jax.ShapeDtypeStruct(shape, dtype) for...]
  transfers between devices with their start and end apart: 7 -> 7, of which waited for: 4 -> 6; matrix products, arithmetic and copies ran while one was open for 1% -> 1% of each run, Pallas kernels for 2% -> 3%
where the time goes in v3:
time: 59.7 us; the launch traced here: 59 us
  blocking collectives  20.3 us (34%)
  starting transfers between devices  15.6 us (26%)
  waiting for transfers between devices  10.2 us (17%)
  Pallas kernels  8.54 us (14%)
  local copies, waits for them, and re-layouts  3.52 us (6%)
  between operations  0.78 us (1%)
    all_to_all x1, blocking collectives, on_device(): lax.all_to_all(send.reshape(frames, tracks, width), ('x', 'zl'), 0, 0)  10.2 us
    all_to_all x1, blocking collectives, on_device(): lax.all_to_all(jnp.broadcast_to(frame_out[None], (frames, count, width)),...  10.1 us
    pallas_call x8, Pallas kernels, call(): pl.pallas_call(kernel, out_shape=[jax.ShapeDtypeStruct(shape, dtype) for...  8.54 us
    ppermute x4, starting transfers between devices, shift(): lax.ppermute(value, axis, [(i, (i + step) % count) for i in range(count)])  8.27 us
    ppermute x3, starting transfers between devices, on_device(): lax.ppermute(partial, 'zh', [(i, i ^ k) for i in range(4)])  7.29 us
    ppermute x3, waiting for transfers between devices, on_device(): lax.ppermute(partial, 'zh', [(i, i ^ k) for i in range(4)])  5.53 us
    ppermute x4, waiting for transfers between devices, shift(): lax.ppermute(value, axis, [(i, (i + step) % count) for i in range(count)])  4.71 us
    unnamed x28, local copies, waits for them, and re-layouts  3.38 us
  transfers between devices with their start and end apart: 7, of which 6 were waited for; matrix products, arithmetic and copies ran while one was open for 1% of the time, Pallas kernels for 3%

profile of v3, /device:TPU:1, one launch (start us, length us, event | category | flops | bytes accessed | tf_op | source)
XLA Modules:
  0.0 59.0 jit_solution(17060023300700043246)
XLA Ops:
  0.6 0.0 copy-start
  0.6 0.0 copy-start.4
  0.7 3.8 %collective-permute-start = (bf16[256,384]{1,0:T(8,128)(2,1)}, bf16[256,384]{1,0:T(8,128)(2,1)S(1)}, u32[]{:S(2)}, u32[]{:S(2)}) collective-permute-start(bf16[256,384]{1,0:T(8,128)(2,1)} %bitcast.9), channel_id=1, source_target_pairs={{0,2},{1,3},{2,0},{3,1},{4,6},{5,7},{6,4},{7,5},{8,10},{9,11},{10,... | collective-permute-start | bytes 589832 | tf_op jit(solution)/shard_map/ppermute | solution.py:277
  4.5 0.8 %collective-permute-start.2 = (bf16[256,384]{1,0:T(8,128)(2,1)}, bf16[256,384]{1,0:T(8,128)(2,1)S(1)}, u32[]{:S(2)}, u32[]{:S(2)}) collective-permute-start(bf16[256,384]{1,0:T(8,128)(2,1)} %bitcast.10), channel_id=1, source_target_pairs={{0,3},{1,0},{2,1},{3,2},{4,7},{5,4},{6,5},{7,6},{8,11},{9,8},{10,9... | collective-permute-start | bytes 589832 | tf_op jit(solution)/shard_map/ppermute | solution.py:277
  5.3 0.7 %collective-permute-start.1 = (bf16[256,384]{1,0:T(8,128)(2,1)}, bf16[256,384]{1,0:T(8,128)(2,1)S(1)}, u32[]{:S(2)}, u32[]{:S(2)}) collective-permute-start(bf16[256,384]{1,0:T(8,128)(2,1)} %bitcast.11), channel_id=1, source_target_pairs={{0,1},{1,2},{2,3},{3,0},{4,5},{5,6},{6,7},{7,4},{8,9},{9,10},{10,1... | collective-permute-start | bytes 589832 | tf_op jit(solution)/shard_map/ppermute | solution.py:277
  6.0 0.8 %copy.17.refs_5_ = s32[32,8]{1,0:T(8,128)S(1)} copy(s32[32,8]{0,1:T(8,128)} %param.14) | data formatting | bytes 2048 | tf_op args[1]
  6.7 0.0 copy-done
  6.7 0.1 constant_dynamic-slice_fusion
  6.8 0.0 copy-done.4
  6.9 0.0 copy-start.1
  6.9 1.2 %copy-done.1 = bf16[384,1152]{1,0:T(8,128)(2,1)S(1)} copy-done((bf16[384,1152]{1,0:T(8,128)(2,1)S(1)}, bf16[384,1152]{1,0:T(8,128)(2,1)}, u32[]{:S(2)}) %copy-start.1) | copy-done | bytes 884760
  8.0 0.0 copy-start.8
  8.0 1.0 %copy-done.8 = bf16[384,384]{1,0:T(8,128)(2,1)S(1)} copy-done((bf16[384,384]{1,0:T(8,128)(2,1)S(1)}, bf16[384,384]{1,0:T(8,128)(2,1)}, u32[]{:S(2)}) %copy-start.8) | copy-done | bytes 294936
  9.0 0.0 copy-start.2
  9.0 0.7 %shard_map.140 = (bf16[256,1152]{1,0:T(8,128)(2,1)S(1)}, bf16[64,384]{1,0:T(8,128)(2,1)S(1)}) custom-call(bf16[256,384]{1,0:T(8,128)(2,1)S(1)} %bitcast.12, bf16[64,384]{1,0:T(8,128)(2,1)S(1)} %bitcast.14, bf16[384,1152]{1,0:T(8,128)(2,1)S(1)} %copy-done.1, bf16[384,384]{1,0:T(8,128)(2,1)S(1)} %copy-done.8), custom_call_target="tpu_custom_call" | custom-call | tf_op jit(solution)/shard_map/pallas_call | solution.py:269
  9.7 0.0 copy-start.9
  9.7 0.0 collective-permute-done.tokens_ref
  9.7 0.4 copy-done.2
  10.2 0.5 shard_map.141.refs_2_
  10.7 3.0 %collective-permute-done.2.refs_4_ = bf16[256,384]{1,0:T(8,128)(2,1)S(1)} collective-permute-done((bf16[256,384]{1,0:T(8,128)(2,1)}, bf16[256,384]{1,0:T(8,128)(2,1)S(1)}, u32[]{:S(2)}, u32[]{:S(2)}) %collective-permute-start.2) | collective-permute-done | bytes 196640 | tf_op jit(solution)/shard_map/ppermute | solution.py:277
  13.8 0.8 %collective-permute-done.1.refs_3_ = bf16[256,384]{1,0:T(8,128)(2,1)S(1)} collective-permute-done((bf16[256,384]{1,0:T(8,128)(2,1)}, bf16[256,384]{1,0:T(8,128)(2,1)S(1)}, u32[]{:S(2)}, u32[]{:S(2)}) %collective-permute-start.1) | collective-permute-done | bytes 196640 | tf_op jit(solution)/shard_map/ppermute | solution.py:277
  14.5 0.0 copy-done.9
  14.5 0.0 copy-start.6
  14.5 2.1 %shard_map.142 = (bf16[256,384]{1,0:T(8,128)(2,1)S(1)}, bf16[256,384]{1,0:T(8,128)(2,1)S(1)}, bf16[256,384]{1,0:T(8,128)(2,1)S(1)}) custom-call(bf16[256,384]{1,0:T(8,128)(2,1)S(1)} %bitcast.13, bf16[256,1152]{1,0:T(8,128)(2,1)S(1)} %get-tuple-element.9.refs_1_, bf16[256,768]{1,0:T(8,128)(2,1)S(1)} %shard_map.141.refs_2_, ...), custom_call_target="tpu_custom_call" | custom-call | tf_op jit(solution)/shard_map/pallas_call | solution.py:269
  16.6 10.2 %all_to_all.10 = bf16[8,32,384]{2,1,0:T(8,128)(2,1)S(1)} all-to-all(bf16[8,32,384]{2,1,0:T(8,128)(2,1)S(1)} %bitcast.16), channel_id=1, replica_groups=mesh['x'=4,'zh'=4,'zl'=2,'c'=2,'y'=4] {'x','zl'}, dimensions={0} | all-to-all | bytes 393216 | tf_op jit(solution)/shard_map/all_to_all | solution.py:301
  26.8 0.0 copy-start.10
  26.8 0.0 copy-done.6
  26.8 0.0 copy-start.3
  26.8 0.8 %shard_map.144.a_ref = bf16[64,512]{1,0:T(8,128)(2,1)S(1)} custom-call(bf16[256,384]{1,0:T(8,128)(2,1)S(1)} %bitcast.8, bf16[64,384]{1,0:T(8,128)(2,1)S(1)} %get-tuple-element.13.query_ref, bf16[384,768]{1,0:T(8,128)(2,1)S(1)} %copy-done.6), custom_call_target="tpu_custom_call" | custom-call | tf_op jit(solution)/shard_map/pallas_call | solution.py:269
  27.6 3.0 %collective-permute-start.3 = (bf16[64,512]{1,0:T(8,128)(2,1)S(1)}, bf16[64,512]{1,0:T(8,128)(2,1)S(1)}, u32[]{:S(2)}, u32[]{:S(2)}) collective-permute-start(bf16[64,512]{1,0:T(8,128)(2,1)S(1)} %shard_map.144.a_ref), channel_id=1, source_target_pairs={{0,4},{4,0},{1,5},{5,1},{2,6},{6,2},{3,7},{7,3},{8,12},{12,8},{9,1... | collective-permute-start | bytes 196616 | tf_op jit(solution)/shard_map/ppermute | solution.py:277
  30.6 0.9 %collective-permute-done.3.b_ref = bf16[64,512]{1,0:T(8,128)(2,1)S(1)} collective-permute-done((bf16[64,512]{1,0:T(8,128)(2,1)S(1)}, bf16[64,512]{1,0:T(8,128)(2,1)S(1)}, u32[]{:S(2)}, u32[]{:S(2)}) %collective-permute-start.3) | collective-permute-done | bytes 65568 | tf_op jit(solution)/shard_map/ppermute | solution.py:277
  31.5 0.3 shard_map.145.refs_1_
  31.8 6.1 %collective-permute-start.6 = (bf16[64,512]{1,0:T(8,128)(2,1)S(1)}, bf16[64,512]{1,0:T(8,128)(2,1)S(1)}, u32[]{:S(2)}, u32[]{:S(2)}) collective-permute-start(bf16[64,512]{1,0:T(8,128)(2,1)S(1)} %shard_map.145.refs_1_), channel_id=1, source_target_pairs={{0,32},{16,48},{32,0},{48,16},{1,33},{17,49},{33,1},{49,17},{2,34}... | collective-permute-start | bytes 196616 | tf_op jit(solution)/shard_map/ppermute | solution.py:305
  37.9 0.3 collective-permute-start.5
  38.1 0.9 %collective-permute-start.4 = (bf16[64,512]{1,0:T(8,128)(2,1)S(1)}, bf16[64,512]{1,0:T(8,128)(2,1)S(1)}, u32[]{:S(2)}, u32[]{:S(2)}) collective-permute-start(bf16[64,512]{1,0:T(8,128)(2,1)S(1)} %shard_map.145.refs_1_), channel_id=1, source_target_pairs={{0,16},{16,0},{32,48},{48,32},{1,17},{17,1},{33,49},{49,33},{2,18}... | collective-permute-start | bytes 196616 | tf_op jit(solution)/shard_map/ppermute | solution.py:305
  39.1 0.0 copy-done.10
  39.1 0.0 copy-start.11
  39.1 0.0 copy-start.12
  39.1 0.3 shard_map.143.refs_0_.query_ref
  39.3 0.7 %collective-permute-done.6.refs_4_ = bf16[64,512]{1,0:T(8,128)(2,1)S(1)} collective-permute-done((bf16[64,512]{1,0:T(8,128)(2,1)S(1)}, bf16[64,512]{1,0:T(8,128)(2,1)S(1)}, u32[]{:S(2)}, u32[]{:S(2)}) %collective-permute-start.6) | collective-permute-done | bytes 65568 | tf_op jit(solution)/shard_map/ppermute | solution.py:305
  40.1 3.7 %collective-permute-done.5.refs_3_ = bf16[64,512]{1,0:T(8,128)(2,1)S(1)} collective-permute-done((bf16[64,512]{1,0:T(8,128)(2,1)S(1)}, bf16[64,512]{1,0:T(8,128)(2,1)S(1)}, u32[]{:S(2)}, u32[]{:S(2)}) %collective-permute-start.5) | collective-permute-done | bytes 65568 | tf_op jit(solution)/shard_map/ppermute | solution.py:305
  43.8 1.1 %collective-permute-done.4.refs_2_ = bf16[64,512]{1,0:T(8,128)(2,1)S(1)} collective-permute-done((bf16[64,512]{1,0:T(8,128)(2,1)S(1)}, bf16[64,512]{1,0:T(8,128)(2,1)S(1)}, u32[]{:S(2)}, u32[]{:S(2)}) %collective-permute-start.4) | collective-permute-done | bytes 65568 | tf_op jit(solution)/shard_map/ppermute | solution.py:305
  44.9 0.0 copy-done.3
  44.9 0.0 copy-done.11
  44.9 0.0 copy-done.12
  44.9 1.4 %shard_map.146 = bf16[64,384]{1,0:T(8,128)(2,1)S(1)} custom-call(bf16[256,384]{1,0:T(8,128)(2,1)S(1)} %shard_map.143.refs_0_.query_ref, bf16[64,512]{1,0:T(8,128)(2,1)S(1)} %shard_map.145.refs_1_, bf16[64,512]{1,0:T(8,128)(2,1)S(1)} %collective-permute-done.4.refs_2_, bf16[64,512]{1,0:T(8,128)(2,1)S(1)} %collective-permute-done.5.refs_3_, ...), custom_call_target="tpu_custom_call" | custom-call | tf_op jit(solution)/shard_map/pallas_call | solution.py:269
  46.3 0.0 copy-start.5
  46.3 0.0 copy-start.7
  46.3 10.1 %all_to_all.11.virtual_ref = bf16[8,64,384]{2,1,0:T(8,128)(2,1)S(1)} all-to-all(bf16[8,64,384]{2,1,0:T(8,128)(2,1)S(1)} %broadcast_in_dim.2), channel_id=1, replica_groups=mesh['x'=4,'zh'=4,'zl'=2,'c'=2,'y'=4] {'x','zl'}, dimensions={0} | all-to-all | bytes 786432 | tf_op jit(solution)/shard_map/all_to_all | solution.py:309
  56.5 0.0 copy-done.5
  56.5 0.0 copy-done.7
  56.5 2.5 %shard_map.147 = (bf16[256,384]{1,0:T(8,128)(2,1)}, bf16[512,384]{1,0:T(8,128)(2,1)}) custom-call(bf16[256,384]{1,0:T(8,128)(2,1)S(1)} %get-tuple-element.10.updated_ref, bf16[256,384]{1,0:T(8,128)(2,1)S(1)} %shard_map.143.refs_0_.query_ref, bf16[8,64,384]{2,1,0:T(8,128)(2,1)S(1)} %all_to_all.11.virtual_ref, bf16[384,768]{1,0:T(8,128)(2,1)S(1)} %copy-done.5, ...), custom_call_target="tpu_custom_call" | custom-call | tf_op jit(solution)/shard_map/pallas_call | solution.py:269
  (2 shorter events, 0.0 us)
Async XLA Ops:
  0.6 6.1 %copy-start = (bf16[64,8,384]{2,1,0:T(8,128)(2,1)S(1)}, bf16[64,8,384]{2,1,0:T(8,128)(2,1)}, u32[]{:S(2)}) copy-start(bf16[64,8,384]{2,1,0:T(8,128)(2,1)} %param.15) | copy-start | bytes 1179652
  0.6 6.2 %copy-start.4 = (bf16[32,8,384]{2,1,0:T(8,128)(2,1)S(1)}, bf16[32,8,384]{2,1,0:T(8,128)(2,1)}, u32[]{:S(2)}) copy-start(bf16[32,8,384]{2,1,0:T(8,128)(2,1)} %param.13) | copy-start | bytes 589828
  0.7 9.1 %collective-permute-start = (bf16[256,384]{1,0:T(8,128)(2,1)}, bf16[256,384]{1,0:T(8,128)(2,1)S(1)}, u32[]{:S(2)}, u32[]{:S(2)}) collective-permute-start(bf16[256,384]{1,0:T(8,128)(2,1)} %bitcast.9), channel_id=1, source_target_pairs={{0,2},{1,3},{2,0},{3,1},{4,6},{5,7},{6,4},{7,5},{8,10},{9,11},{10,... | collective-permute-start | bytes 589832 | tf_op jit(solution)/shard_map/ppermute | solution.py:277
  4.5 9.3 %collective-permute-start.2 = (bf16[256,384]{1,0:T(8,128)(2,1)}, bf16[256,384]{1,0:T(8,128)(2,1)S(1)}, u32[]{:S(2)}, u32[]{:S(2)}) collective-permute-start(bf16[256,384]{1,0:T(8,128)(2,1)} %bitcast.10), channel_id=1, source_target_pairs={{0,3},{1,0},{2,1},{3,2},{4,7},{5,4},{6,5},{7,6},{8,11},{9,8},{10,9... | collective-permute-start | bytes 589832 | tf_op jit(solution)/shard_map/ppermute | solution.py:277
  5.3 9.2 %collective-permute-start.1 = (bf16[256,384]{1,0:T(8,128)(2,1)}, bf16[256,384]{1,0:T(8,128)(2,1)S(1)}, u32[]{:S(2)}, u32[]{:S(2)}) collective-permute-start(bf16[256,384]{1,0:T(8,128)(2,1)} %bitcast.11), channel_id=1, source_target_pairs={{0,1},{1,2},{2,3},{3,0},{4,5},{5,6},{6,7},{7,4},{8,9},{9,10},{10,1... | collective-permute-start | bytes 589832 | tf_op jit(solution)/shard_map/ppermute | solution.py:277
  6.9 1.2 %copy-start.1 = (bf16[384,1152]{1,0:T(8,128)(2,1)S(1)}, bf16[384,1152]{1,0:T(8,128)(2,1)}, u32[]{:S(2)}) copy-start(bf16[384,1152]{1,0:T(8,128)(2,1)} %refs_6_.2) | copy-start | bytes 2654212
  8.0 1.0 %copy-start.8 = (bf16[384,384]{1,0:T(8,128)(2,1)S(1)}, bf16[384,384]{1,0:T(8,128)(2,1)}, u32[]{:S(2)}) copy-start(bf16[384,384]{1,0:T(8,128)(2,1)} %virt_q_ref.1) | copy-start | bytes 884740
  9.0 1.2 %copy-start.2 = (bf16[384,1152]{1,0:T(8,128)(2,1)S(1)}, bf16[384,1152]{1,0:T(8,128)(2,1)}, u32[]{:S(2)}) copy-start(bf16[384,1152]{1,0:T(8,128)(2,1)} %refs_6_.2) | copy-start | bytes 2654212
  9.7 4.8 %copy-start.9 = (bf16[384,384]{1,0:T(8,128)(2,1)S(1)}, bf16[384,384]{1,0:T(8,128)(2,1)}, u32[]{:S(2)}) copy-start(bf16[384,384]{1,0:T(8,128)(2,1)} %refs_7_.2) | copy-start | bytes 884740
  14.5 12.3 %copy-start.6 = (bf16[384,768]{1,0:T(8,128)(2,1)S(1)}, bf16[384,768]{1,0:T(8,128)(2,1)}, u32[]{:S(2)}) copy-start(bf16[384,768]{1,0:T(8,128)(2,1)} %virt_kv_ref.1) | copy-start | bytes 1769476
  26.8 12.3 %copy-start.10 = (bf16[384,384]{1,0:T(8,128)(2,1)S(1)}, bf16[384,384]{1,0:T(8,128)(2,1)}, u32[]{:S(2)}) copy-start(bf16[384,384]{1,0:T(8,128)(2,1)} %back_q_ref.1) | copy-start | bytes 884740
  26.8 18.1 %copy-start.3 = (bf16[384,1152]{1,0:T(8,128)(2,1)S(1)}, bf16[384,1152]{1,0:T(8,128)(2,1)}, u32[]{:S(2)}) copy-start(bf16[384,1152]{1,0:T(8,128)(2,1)} %refs_7_.3) | copy-start | bytes 2654212
  27.6 3.9 %collective-permute-start.3 = (bf16[64,512]{1,0:T(8,128)(2,1)S(1)}, bf16[64,512]{1,0:T(8,128)(2,1)S(1)}, u32[]{:S(2)}, u32[]{:S(2)}) collective-permute-start(bf16[64,512]{1,0:T(8,128)(2,1)S(1)} %shard_map.144.a_ref), channel_id=1, source_target_pairs={{0,4},{4,0},{1,5},{5,1},{2,6},{6,2},{3,7},{7,3},{8,12},{12,8},{9,1... | collective-permute-start | bytes 196616 | tf_op jit(solution)/shard_map/ppermute | solution.py:277
  31.8 8.3 %collective-permute-start.6 = (bf16[64,512]{1,0:T(8,128)(2,1)S(1)}, bf16[64,512]{1,0:T(8,128)(2,1)S(1)}, u32[]{:S(2)}, u32[]{:S(2)}) collective-permute-start(bf16[64,512]{1,0:T(8,128)(2,1)S(1)} %shard_map.145.refs_1_), channel_id=1, source_target_pairs={{0,32},{16,48},{32,0},{48,16},{1,33},{17,49},{33,1},{49,17},{2,34}... | collective-permute-start | bytes 196616 | tf_op jit(solution)/shard_map/ppermute | solution.py:305
  37.9 5.9 %collective-permute-start.5 = (bf16[64,512]{1,0:T(8,128)(2,1)S(1)}, bf16[64,512]{1,0:T(8,128)(2,1)S(1)}, u32[]{:S(2)}, u32[]{:S(2)}) collective-permute-start(bf16[64,512]{1,0:T(8,128)(2,1)S(1)} %shard_map.145.refs_1_), channel_id=1, source_target_pairs={{0,48},{16,32},{32,16},{48,0},{1,49},{17,33},{33,17},{49,1},{2,50}... | collective-permute-start | bytes 196616 | tf_op jit(solution)/shard_map/ppermute | solution.py:305
  38.1 6.7 %collective-permute-start.4 = (bf16[64,512]{1,0:T(8,128)(2,1)S(1)}, bf16[64,512]{1,0:T(8,128)(2,1)S(1)}, u32[]{:S(2)}, u32[]{:S(2)}) collective-permute-start(bf16[64,512]{1,0:T(8,128)(2,1)S(1)} %shard_map.145.refs_1_), channel_id=1, source_target_pairs={{0,16},{16,0},{32,48},{48,32},{1,17},{17,1},{33,49},{49,33},{2,18}... | collective-permute-start | bytes 196616 | tf_op jit(solution)/shard_map/ppermute | solution.py:305
  39.1 5.8 %copy-start.11 = (bf16[384,384]{1,0:T(8,128)(2,1)S(1)}, bf16[384,384]{1,0:T(8,128)(2,1)}, u32[]{:S(2)}) copy-start(bf16[384,384]{1,0:T(8,128)(2,1)} %refs_6_.3) | copy-start | bytes 884740
  39.1 5.8 %copy-start.12 = (bf16[384,384]{1,0:T(8,128)(2,1)S(1)}, bf16[384,384]{1,0:T(8,128)(2,1)}, u32[]{:S(2)}) copy-start(bf16[384,384]{1,0:T(8,128)(2,1)} %refs_8_.1) | copy-start | bytes 884740
  46.3 10.2 %copy-start.5 = (bf16[384,768]{1,0:T(8,128)(2,1)S(1)}, bf16[384,768]{1,0:T(8,128)(2,1)}, u32[]{:S(2)}) copy-start(bf16[384,768]{1,0:T(8,128)(2,1)} %back_kv_ref.1) | copy-start | bytes 1769476
  46.3 10.1 %copy-start.7 = (bf16[384,384]{1,0:T(8,128)(2,1)S(1)}, bf16[384,384]{1,0:T(8,128)(2,1)}, u32[]{:S(2)}) copy-start(bf16[384,384]{1,0:T(8,128)(2,1)} %back_out_ref.1) | copy-start | bytes 884740

commit v4 on v3

--- a/solution.py
+++ b/solution.py
@@ -14,7 +14,6 @@
 GROUP = 4
 STEPS = (2, 1, 3)
 EARLY = 1
-ZSTEPS = (1, 3, 2)
 MARK = 64.0
 BF = jnp.bfloat16
 F32 = jnp.float32
@@ -302,7 +301,10 @@
     (partial,) = call(partial_kernel, [((count, width + 128), BF)], got, virt_query, virt_kv)
     (partial,) = call(both_kernel, [((count, width + 128), BF)], partial, shift(partial, "c", 2, 1))
     (query,) = call(query_kernel, [((rows, width), BF)], normed, back_q)
-    partials = [partial] + [lax.ppermute(partial, "zh", [(i, i ^ k) for i in range(4)]) for k in ZSTEPS]
+    split_pairs = [(z * 2 + c, (z ^ (2, 3)[c]) * 2 + c) for z in range(4) for c in range(2)]
+    fetched = lax.ppermute(partial, ("zh", "c"), split_pairs)
+    near = lax.ppermute(partial, "zh", [(z, z ^ 1) for z in range(4)])
+    partials = [partial, fetched, shift(fetched, "c", 2, 1), near]
     (frame_out,) = call(
         virtual_kernel, [((count, width), BF)], query, *partials, mine, virt_out, self_qkv, self_out
     )

time: 59.7 us -> 58.8 us (0.985)
  waiting for transfers between devices: 10.2 us -> 7.94 us
  starting transfers between devices: 15.6 us -> 17 us
    ppermute x4 -> x5, starting transfers between devices: 8.27 us -> 10.6 us  [shift(): lax.ppermute(value, axis, [(i, (i + step) % count) for i in range(count)])]
    ppermute x3 -> x2, waiting for transfers between devices: 5.53 us -> 3.22 us  [the longest x1 2.49 us: on_device(): near = lax.ppermute(partial, 'zh', [(z, z ^ 1) for z in range(4)])]
    ppermute x3 -> x2, starting transfers between devices: 7.29 us -> 6.38 us  [the longest x1 5.21 us: on_device(): fetched = lax.ppermute(partial, ('zh', 'c'), split_pairs)]
    ppermute x4 -> x5, waiting for transfers between devices: 4.71 us -> 4.71 us  [shift(): lax.ppermute(value, axis, [(i, (i + step) % count) for i in range(count)])]
  transfers between devices with their start and end apart: 7 -> 7, of which waited for: 6 -> 5; matrix products, arithmetic and copies ran while one was open for 1% -> 2% of each run, Pallas kernels for 3% -> 3%
where the time goes in v4:
time: 58.8 us; the launch traced here: 58.3 us
  blocking collectives  20.5 us (35%)
  starting transfers between devices  17 us (29%)
  Pallas kernels  8.55 us (15%)
  waiting for transfers between devices  7.94 us (14%)
  local copies, waits for them, and re-layouts  3.52 us (6%)
  between operations  0.79 us (1%)
    ppermute x5, starting transfers between devices, shift(): lax.ppermute(value, axis, [(i, (i + step) % count) for i in range(count)])  10.6 us
    all_to_all x1, blocking collectives, on_device(): lax.all_to_all(jnp.broadcast_to(frame_out[None], (frames, count, width)),...  10.3 us
    all_to_all x1, blocking collectives, on_device(): lax.all_to_all(send.reshape(frames, tracks, width), ('x', 'zl'), 0, 0)  10.2 us
    pallas_call x8, Pallas kernels, call(): pl.pallas_call(kernel, out_shape=[jax.ShapeDtypeStruct(shape, dtype) for...  8.55 us
    ppermute x1, starting transfers between devices, on_device(): fetched = lax.ppermute(partial, ('zh', 'c'), split_pairs)  5.21 us
    ppermute x5, waiting for transfers between devices, shift(): lax.ppermute(value, axis, [(i, (i + step) % count) for i in range(count)])  4.71 us
    unnamed x28, local copies, waits for them, and re-layouts  3.38 us
    ppermute x1, waiting for transfers between devices, on_device(): near = lax.ppermute(partial, 'zh', [(z, z ^ 1) for z in range(4)])  2.49 us
  transfers between devices with their start and end apart: 7, of which 5 were waited for; matrix products, arithmetic and copies ran while one was open for 2% of the time, Pallas kernels for 3%

profile of v4, /device:TPU:1, one launch (start us, length us, event | category | flops | bytes accessed | tf_op | source)
XLA Modules:
  0.0 58.3 jit_solution(3254904332394753299)
XLA Ops:
  0.6 0.0 copy-start
  0.6 0.0 copy-start.4
  0.7 3.8 %collective-permute-start = (bf16[256,384]{1,0:T(8,128)(2,1)}, bf16[256,384]{1,0:T(8,128)(2,1)S(1)}, u32[]{:S(2)}, u32[]{:S(2)}) collective-permute-start(bf16[256,384]{1,0:T(8,128)(2,1)} %bitcast.9), channel_id=1, source_target_pairs={{0,2},{1,3},{2,0},{3,1},{4,6},{5,7},{6,4},{7,5},{8,10},{9,11},{10,... | collective-permute-start | bytes 589832 | tf_op jit(solution)/shard_map/ppermute | solution.py:276
  4.5 0.8 %collective-permute-start.2 = (bf16[256,384]{1,0:T(8,128)(2,1)}, bf16[256,384]{1,0:T(8,128)(2,1)S(1)}, u32[]{:S(2)}, u32[]{:S(2)}) collective-permute-start(bf16[256,384]{1,0:T(8,128)(2,1)} %bitcast.10), channel_id=1, source_target_pairs={{0,3},{1,0},{2,1},{3,2},{4,7},{5,4},{6,5},{7,6},{8,11},{9,8},{10,9... | collective-permute-start | bytes 589832 | tf_op jit(solution)/shard_map/ppermute | solution.py:276
  5.3 0.7 %collective-permute-start.1 = (bf16[256,384]{1,0:T(8,128)(2,1)}, bf16[256,384]{1,0:T(8,128)(2,1)S(1)}, u32[]{:S(2)}, u32[]{:S(2)}) collective-permute-start(bf16[256,384]{1,0:T(8,128)(2,1)} %bitcast.11), channel_id=1, source_target_pairs={{0,1},{1,2},{2,3},{3,0},{4,5},{5,6},{6,7},{7,4},{8,9},{9,10},{10,1... | collective-permute-start | bytes 589832 | tf_op jit(solution)/shard_map/ppermute | solution.py:276
  6.0 0.8 %copy.17.refs_5_ = s32[32,8]{1,0:T(8,128)S(1)} copy(s32[32,8]{0,1:T(8,128)} %param.14) | data formatting | bytes 2048 | tf_op args[1]
  6.7 0.0 copy-done
  6.7 0.1 constant_dynamic-slice_fusion
  6.8 0.0 copy-done.4
  6.9 0.0 copy-start.1
  6.9 1.2 %copy-done.1 = bf16[384,1152]{1,0:T(8,128)(2,1)S(1)} copy-done((bf16[384,1152]{1,0:T(8,128)(2,1)S(1)}, bf16[384,1152]{1,0:T(8,128)(2,1)}, u32[]{:S(2)}) %copy-start.1) | copy-done | bytes 884760
  8.0 0.0 copy-start.8
  8.0 1.0 %copy-done.8 = bf16[384,384]{1,0:T(8,128)(2,1)S(1)} copy-done((bf16[384,384]{1,0:T(8,128)(2,1)S(1)}, bf16[384,384]{1,0:T(8,128)(2,1)}, u32[]{:S(2)}) %copy-start.8) | copy-done | bytes 294936
  9.0 0.0 copy-start.2
  9.0 0.7 %shard_map.140 = (bf16[256,1152]{1,0:T(8,128)(2,1)S(1)}, bf16[64,384]{1,0:T(8,128)(2,1)S(1)}) custom-call(bf16[256,384]{1,0:T(8,128)(2,1)S(1)} %bitcast.12, bf16[64,384]{1,0:T(8,128)(2,1)S(1)} %bitcast.14, bf16[384,1152]{1,0:T(8,128)(2,1)S(1)} %copy-done.1, bf16[384,384]{1,0:T(8,128)(2,1)S(1)} %copy-done.8), custom_call_target="tpu_custom_call" | custom-call | tf_op jit(solution)/shard_map/pallas_call | solution.py:268
  9.7 0.0 copy-start.9
  9.7 0.0 collective-permute-done.tokens_ref
  9.7 0.4 copy-done.2
  10.2 0.5 shard_map.141.refs_2_
  10.7 3.0 %collective-permute-done.2.refs_4_ = bf16[256,384]{1,0:T(8,128)(2,1)S(1)} collective-permute-done((bf16[256,384]{1,0:T(8,128)(2,1)}, bf16[256,384]{1,0:T(8,128)(2,1)S(1)}, u32[]{:S(2)}, u32[]{:S(2)}) %collective-permute-start.2) | collective-permute-done | bytes 196640 | tf_op jit(solution)/shard_map/ppermute | solution.py:276
  13.8 0.8 %collective-permute-done.1.refs_3_ = bf16[256,384]{1,0:T(8,128)(2,1)S(1)} collective-permute-done((bf16[256,384]{1,0:T(8,128)(2,1)}, bf16[256,384]{1,0:T(8,128)(2,1)S(1)}, u32[]{:S(2)}, u32[]{:S(2)}) %collective-permute-start.1) | collective-permute-done | bytes 196640 | tf_op jit(solution)/shard_map/ppermute | solution.py:276
  14.5 0.0 copy-done.9
  14.5 0.0 copy-start.6
  14.5 2.1 %shard_map.142 = (bf16[256,384]{1,0:T(8,128)(2,1)S(1)}, bf16[256,384]{1,0:T(8,128)(2,1)S(1)}, bf16[256,384]{1,0:T(8,128)(2,1)S(1)}) custom-call(bf16[256,384]{1,0:T(8,128)(2,1)S(1)} %bitcast.13, bf16[256,1152]{1,0:T(8,128)(2,1)S(1)} %get-tuple-element.9.refs_1_, bf16[256,768]{1,0:T(8,128)(2,1)S(1)} %shard_map.141.refs_2_, ...), custom_call_target="tpu_custom_call" | custom-call | tf_op jit(solution)/shard_map/pallas_call | solution.py:268
  16.6 10.2 %all_to_all.10 = bf16[8,32,384]{2,1,0:T(8,128)(2,1)S(1)} all-to-all(bf16[8,32,384]{2,1,0:T(8,128)(2,1)S(1)} %bitcast.16), channel_id=1, replica_groups=mesh['x'=4,'zh'=4,'zl'=2,'c'=2,'y'=4] {'x','zl'}, dimensions={0} | all-to-all | bytes 393216 | tf_op jit(solution)/shard_map/all_to_all | solution.py:300
  26.8 0.0 copy-start.10
  26.8 0.0 copy-done.6
  26.8 0.0 copy-start.3
  26.8 0.8 %shard_map.144.a_ref = bf16[64,512]{1,0:T(8,128)(2,1)S(1)} custom-call(bf16[256,384]{1,0:T(8,128)(2,1)S(1)} %bitcast.8, bf16[64,384]{1,0:T(8,128)(2,1)S(1)} %get-tuple-element.13.query_ref, bf16[384,768]{1,0:T(8,128)(2,1)S(1)} %copy-done.6), custom_call_target="tpu_custom_call" | custom-call | tf_op jit(solution)/shard_map/pallas_call | solution.py:268
  27.6 3.0 %collective-permute-start.3 = (bf16[64,512]{1,0:T(8,128)(2,1)S(1)}, bf16[64,512]{1,0:T(8,128)(2,1)S(1)}, u32[]{:S(2)}, u32[]{:S(2)}) collective-permute-start(bf16[64,512]{1,0:T(8,128)(2,1)S(1)} %shard_map.144.a_ref), channel_id=1, source_target_pairs={{0,4},{4,0},{1,5},{5,1},{2,6},{6,2},{3,7},{7,3},{8,12},{12,8},{9,1... | collective-permute-start | bytes 196616 | tf_op jit(solution)/shard_map/ppermute | solution.py:276
  30.6 0.9 %collective-permute-done.3.b_ref = bf16[64,512]{1,0:T(8,128)(2,1)S(1)} collective-permute-done((bf16[64,512]{1,0:T(8,128)(2,1)S(1)}, bf16[64,512]{1,0:T(8,128)(2,1)S(1)}, u32[]{:S(2)}, u32[]{:S(2)}) %collective-permute-start.3) | collective-permute-done | bytes 65568 | tf_op jit(solution)/shard_map/ppermute | solution.py:276
  31.5 0.3 shard_map.145.refs_1_
  31.8 5.2 %collective-permute-start.4 = (bf16[64,512]{1,0:T(8,128)(2,1)S(1)}, bf16[64,512]{1,0:T(8,128)(2,1)S(1)}, u32[]{:S(2)}, u32[]{:S(2)}) collective-permute-start(bf16[64,512]{1,0:T(8,128)(2,1)S(1)} %shard_map.145.refs_1_), channel_id=1, source_target_pairs={{0,32},{4,52},{16,48},{20,36},{32,0},{36,20},{48,16},{52,4},{1,33}... | collective-permute-start | bytes 196616 | tf_op jit(solution)/shard_map/ppermute | solution.py:305
  37.0 1.2 %collective-permute-start.6 = (bf16[64,512]{1,0:T(8,128)(2,1)S(1)}, bf16[64,512]{1,0:T(8,128)(2,1)S(1)}, u32[]{:S(2)}, u32[]{:S(2)}) collective-permute-start(bf16[64,512]{1,0:T(8,128)(2,1)S(1)} %shard_map.145.refs_1_), channel_id=1, source_target_pairs={{0,16},{16,0},{32,48},{48,32},{1,17},{17,1},{33,49},{49,33},{2,18}... | collective-permute-start | bytes 196616 | tf_op jit(solution)/shard_map/ppermute | solution.py:306
  38.2 0.7 %collective-permute-done.4.refs_2_ = bf16[64,512]{1,0:T(8,128)(2,1)S(1)} collective-permute-done((bf16[64,512]{1,0:T(8,128)(2,1)S(1)}, bf16[64,512]{1,0:T(8,128)(2,1)S(1)}, u32[]{:S(2)}, u32[]{:S(2)}) %collective-permute-start.4) | collective-permute-done | bytes 65568 | tf_op jit(solution)/shard_map/ppermute | solution.py:305
  38.9 2.3 %collective-permute-start.5 = (bf16[64,512]{1,0:T(8,128)(2,1)S(1)}, bf16[64,512]{1,0:T(8,128)(2,1)S(1)}, u32[]{:S(2)}, u32[]{:S(2)}) collective-permute-start(bf16[64,512]{1,0:T(8,128)(2,1)S(1)} %collective-permute-done.4.refs_2_), channel_id=1, source_target_pairs={{0,4},{4,0},{1,5},{5,1},{2,6},{6,2},{3,7},{7,3},{8,12},{12,8},{9,1... | collective-permute-start | bytes 196616 | tf_op jit(solution)/shard_map/ppermute | solution.py:276
  41.2 0.0 copy-done.10
  41.2 0.0 copy-start.11
  41.2 0.0 copy-start.12
  41.2 0.3 shard_map.143.refs_0_.query_ref
  41.5 2.5 %collective-permute-done.6.refs_4_ = bf16[64,512]{1,0:T(8,128)(2,1)S(1)} collective-permute-done((bf16[64,512]{1,0:T(8,128)(2,1)S(1)}, bf16[64,512]{1,0:T(8,128)(2,1)S(1)}, u32[]{:S(2)}, u32[]{:S(2)}) %collective-permute-start.6) | collective-permute-done | bytes 65568 | tf_op jit(solution)/shard_map/ppermute | solution.py:306
  44.0 0.0 collective-permute-done.5.refs_3_
  44.0 0.0 copy-done.3
  44.0 0.0 copy-done.11
  44.0 0.0 copy-done.12
  44.0 1.4 %shard_map.146 = bf16[64,384]{1,0:T(8,128)(2,1)S(1)} custom-call(bf16[256,384]{1,0:T(8,128)(2,1)S(1)} %shard_map.143.refs_0_.query_ref, bf16[64,512]{1,0:T(8,128)(2,1)S(1)} %shard_map.145.refs_1_, bf16[64,512]{1,0:T(8,128)(2,1)S(1)} %collective-permute-done.4.refs_2_, bf16[64,512]{1,0:T(8,128)(2,1)S(1)} %collective-permute-done.5.refs_3_, ...), custom_call_target="tpu_custom_call" | custom-call | tf_op jit(solution)/shard_map/pallas_call | solution.py:268
  45.4 0.0 copy-start.5
  45.4 0.0 copy-start.7
  45.5 10.3 %all_to_all.11.virtual_ref = bf16[8,64,384]{2,1,0:T(8,128)(2,1)S(1)} all-to-all(bf16[8,64,384]{2,1,0:T(8,128)(2,1)S(1)} %broadcast_in_dim.2), channel_id=1, replica_groups=mesh['x'=4,'zh'=4,'zl'=2,'c'=2,'y'=4] {'x','zl'}, dimensions={0} | all-to-all | bytes 786432 | tf_op jit(solution)/shard_map/all_to_all | solution.py:311
  55.8 0.0 copy-done.5
  55.8 0.0 copy-done.7
  55.8 2.5 %shard_map.147 = (bf16[256,384]{1,0:T(8,128)(2,1)}, bf16[512,384]{1,0:T(8,128)(2,1)}) custom-call(bf16[256,384]{1,0:T(8,128)(2,1)S(1)} %get-tuple-element.10.updated_ref, bf16[256,384]{1,0:T(8,128)(2,1)S(1)} %shard_map.143.refs_0_.query_ref, bf16[8,64,384]{2,1,0:T(8,128)(2,1)S(1)} %all_to_all.11.virtual_ref, bf16[384,768]{1,0:T(8,128)(2,1)S(1)} %copy-done.5, ...), custom_call_target="tpu_custom_call" | custom-call | tf_op jit(solution)/shard_map/pallas_call | solution.py:268
  (2 shorter events, 0.0 us)
Async XLA Ops:
  0.6 6.1 %copy-start = (bf16[64,8,384]{2,1,0:T(8,128)(2,1)S(1)}, bf16[64,8,384]{2,1,0:T(8,128)(2,1)}, u32[]{:S(2)}) copy-start(bf16[64,8,384]{2,1,0:T(8,128)(2,1)} %param.15) | copy-start | bytes 1179652
  0.6 6.2 %copy-start.4 = (bf16[32,8,384]{2,1,0:T(8,128)(2,1)S(1)}, bf16[32,8,384]{2,1,0:T(8,128)(2,1)}, u32[]{:S(2)}) copy-start(bf16[32,8,384]{2,1,0:T(8,128)(2,1)} %param.13) | copy-start | bytes 589828
  0.7 9.1 %collective-permute-start = (bf16[256,384]{1,0:T(8,128)(2,1)}, bf16[256,384]{1,0:T(8,128)(2,1)S(1)}, u32[]{:S(2)}, u32[]{:S(2)}) collective-permute-start(bf16[256,384]{1,0:T(8,128)(2,1)} %bitcast.9), channel_id=1, source_target_pairs={{0,2},{1,3},{2,0},{3,1},{4,6},{5,7},{6,4},{7,5},{8,10},{9,11},{10,... | collective-permute-start | bytes 589832 | tf_op jit(solution)/shard_map/ppermute | solution.py:276
  4.5 9.3 %collective-permute-start.2 = (bf16[256,384]{1,0:T(8,128)(2,1)}, bf16[256,384]{1,0:T(8,128)(2,1)S(1)}, u32[]{:S(2)}, u32[]{:S(2)}) collective-permute-start(bf16[256,384]{1,0:T(8,128)(2,1)} %bitcast.10), channel_id=1, source_target_pairs={{0,3},{1,0},{2,1},{3,2},{4,7},{5,4},{6,5},{7,6},{8,11},{9,8},{10,9... | collective-permute-start | bytes 589832 | tf_op jit(solution)/shard_map/ppermute | solution.py:276
  5.3 9.2 %collective-permute-start.1 = (bf16[256,384]{1,0:T(8,128)(2,1)}, bf16[256,384]{1,0:T(8,128)(2,1)S(1)}, u32[]{:S(2)}, u32[]{:S(2)}) collective-permute-start(bf16[256,384]{1,0:T(8,128)(2,1)} %bitcast.11), channel_id=1, source_target_pairs={{0,1},{1,2},{2,3},{3,0},{4,5},{5,6},{6,7},{7,4},{8,9},{9,10},{10,1... | collective-permute-start | bytes 589832 | tf_op jit(solution)/shard_map/ppermute | solution.py:276
  6.9 1.2 %copy-start.1 = (bf16[384,1152]{1,0:T(8,128)(2,1)S(1)}, bf16[384,1152]{1,0:T(8,128)(2,1)}, u32[]{:S(2)}) copy-start(bf16[384,1152]{1,0:T(8,128)(2,1)} %refs_6_.2) | copy-start | bytes 2654212
  8.0 1.0 %copy-start.8 = (bf16[384,384]{1,0:T(8,128)(2,1)S(1)}, bf16[384,384]{1,0:T(8,128)(2,1)}, u32[]{:S(2)}) copy-start(bf16[384,384]{1,0:T(8,128)(2,1)} %virt_q_ref.1) | copy-start | bytes 884740
  9.0 1.2 %copy-start.2 = (bf16[384,1152]{1,0:T(8,128)(2,1)S(1)}, bf16[384,1152]{1,0:T(8,128)(2,1)}, u32[]{:S(2)}) copy-start(bf16[384,1152]{1,0:T(8,128)(2,1)} %refs_6_.2) | copy-start | bytes 2654212
  9.7 4.8 %copy-start.9 = (bf16[384,384]{1,0:T(8,128)(2,1)S(1)}, bf16[384,384]{1,0:T(8,128)(2,1)}, u32[]{:S(2)}) copy-start(bf16[384,384]{1,0:T(8,128)(2,1)} %refs_7_.2) | copy-start | bytes 884740
  14.5 12.3 %copy-start.6 = (bf16[384,768]{1,0:T(8,128)(2,1)S(1)}, bf16[384,768]{1,0:T(8,128)(2,1)}, u32[]{:S(2)}) copy-start(bf16[384,768]{1,0:T(8,128)(2,1)} %virt_kv_ref.1) | copy-start | bytes 1769476
  26.8 14.4 %copy-start.10 = (bf16[384,384]{1,0:T(8,128)(2,1)S(1)}, bf16[384,384]{1,0:T(8,128)(2,1)}, u32[]{:S(2)}) copy-start(bf16[384,384]{1,0:T(8,128)(2,1)} %back_q_ref.1) | copy-start | bytes 884740
  26.8 17.2 %copy-start.3 = (bf16[384,1152]{1,0:T(8,128)(2,1)S(1)}, bf16[384,1152]{1,0:T(8,128)(2,1)}, u32[]{:S(2)}) copy-start(bf16[384,1152]{1,0:T(8,128)(2,1)} %refs_7_.3) | copy-start | bytes 2654212
  27.6 3.9 %collective-permute-start.3 = (bf16[64,512]{1,0:T(8,128)(2,1)S(1)}, bf16[64,512]{1,0:T(8,128)(2,1)S(1)}, u32[]{:S(2)}, u32[]{:S(2)}) collective-permute-start(bf16[64,512]{1,0:T(8,128)(2,1)S(1)} %shard_map.144.a_ref), channel_id=1, source_target_pairs={{0,4},{4,0},{1,5},{5,1},{2,6},{6,2},{3,7},{7,3},{8,12},{12,8},{9,1... | collective-permute-start | bytes 196616 | tf_op jit(solution)/shard_map/ppermute | solution.py:276
  31.8 7.1 %collective-permute-start.4 = (bf16[64,512]{1,0:T(8,128)(2,1)S(1)}, bf16[64,512]{1,0:T(8,128)(2,1)S(1)}, u32[]{:S(2)}, u32[]{:S(2)}) collective-permute-start(bf16[64,512]{1,0:T(8,128)(2,1)S(1)} %shard_map.145.refs_1_), channel_id=1, source_target_pairs={{0,32},{4,52},{16,48},{20,36},{32,0},{36,20},{48,16},{52,4},{1,33}... | collective-permute-start | bytes 196616 | tf_op jit(solution)/shard_map/ppermute | solution.py:305
  37.0 7.0 %collective-permute-start.6 = (bf16[64,512]{1,0:T(8,128)(2,1)S(1)}, bf16[64,512]{1,0:T(8,128)(2,1)S(1)}, u32[]{:S(2)}, u32[]{:S(2)}) collective-permute-start(bf16[64,512]{1,0:T(8,128)(2,1)S(1)} %shard_map.145.refs_1_), channel_id=1, source_target_pairs={{0,16},{16,0},{32,48},{48,32},{1,17},{17,1},{33,49},{49,33},{2,18}... | collective-permute-start | bytes 196616 | tf_op jit(solution)/shard_map/ppermute | solution.py:306
  38.9 5.1 %collective-permute-start.5 = (bf16[64,512]{1,0:T(8,128)(2,1)S(1)}, bf16[64,512]{1,0:T(8,128)(2,1)S(1)}, u32[]{:S(2)}, u32[]{:S(2)}) collective-permute-start(bf16[64,512]{1,0:T(8,128)(2,1)S(1)} %collective-permute-done.4.refs_2_), channel_id=1, source_target_pairs={{0,4},{4,0},{1,5},{5,1},{2,6},{6,2},{3,7},{7,3},{8,12},{12,8},{9,1... | collective-permute-start | bytes 196616 | tf_op jit(solution)/shard_map/ppermute | solution.py:276
  41.2 2.8 %copy-start.11 = (bf16[384,384]{1,0:T(8,128)(2,1)S(1)}, bf16[384,384]{1,0:T(8,128)(2,1)}, u32[]{:S(2)}) copy-start(bf16[384,384]{1,0:T(8,128)(2,1)} %refs_6_.3) | copy-start | bytes 884740
  41.2 2.8 %copy-start.12 = (bf16[384,384]{1,0:T(8,128)(2,1)S(1)}, bf16[384,384]{1,0:T(8,128)(2,1)}, u32[]{:S(2)}) copy-start(bf16[384,384]{1,0:T(8,128)(2,1)} %refs_8_.1) | copy-start | bytes 884740
  45.4 10.4 %copy-start.5 = (bf16[384,768]{1,0:T(8,128)(2,1)S(1)}, bf16[384,768]{1,0:T(8,128)(2,1)}, u32[]{:S(2)}) copy-start(bf16[384,768]{1,0:T(8,128)(2,1)} %back_kv_ref.1) | copy-start | bytes 1769476
  45.4 10.3 %copy-start.7 = (bf16[384,384]{1,0:T(8,128)(2,1)S(1)}, bf16[384,384]{1,0:T(8,128)(2,1)}, u32[]{:S(2)}) copy-start(bf16[384,384]{1,0:T(8,128)(2,1)} %back_out_ref.1) | copy-start | bytes 884740

commit v5 on v4

--- a/solution.py
+++ b/solution.py
@@ -14,6 +14,7 @@
 GROUP = 4
 STEPS = (2, 1, 3)
 EARLY = 1
+GATHER_STEPS = (4, 2, 6)
 MARK = 64.0
 BF = jnp.bfloat16
 F32 = jnp.float32
@@ -236,38 +237,54 @@
     out_ref[...] = (cross.astype(F32) + matmul(mixed, self_out_ref[...])).astype(BF)
 
 
-def query_kernel(normed_ref, back_q_ref, out_ref):
-    out_ref[...] = matmul(normed_ref[...], back_q_ref[...]).astype(BF)
-
-
-def back_kernel(
-    updated_ref, query_ref, virtual_ref, back_kv_ref, back_out_ref, out_ref, virtual_out_ref
-):
-    frames, count, width = virtual_ref.shape
-    rows = updated_ref.shape[0]
+def query_kernel(place_ref, normed_ref, back_q_ref, out_ref, swap_part_ref, swap_ref):
+    frame, core = place_ref[0], place_ref[1]
+    rows = normed_ref.shape[0]
+    frames = 8
     tracks = rows // frames
-    step = count // 4
+
+    def turn(place):
+        return jnp.where(place >= 2, place ^ core, place)
+
+    def swap(n):
+        row, col = iota((n, n), 0), iota((n, n), 1)
+        source = turn((row & (frames - 1)) ^ frame) * (n // frames) + (row >> (frames.bit_length() - 1))
+        return jnp.where(col == source, 1.0, 0.0).astype(BF)
+
+    swap_part_ref[...] = swap(swap_part_ref.shape[0])
+    swap_ref[...] = swap(rows)
+    starts = [pl.multiple_of((turn(jnp.int32(place)) ^ frame) * tracks, tracks) for place in range(frames)]
+    ordered = jnp.concatenate([normed_ref[pl.ds(start, tracks)] for start in starts], axis=0)
+    out_ref[...] = matmul(ordered, back_q_ref[...]).astype(BF)
+
+
+def back_kernel(updated_ref, query_ref, swap_part_ref, swap_ref, *refs):
+    *piece_refs, back_kv_ref, back_out_ref, out_ref, virtual_out_ref = refs
+    frames = len(piece_refs)
+    count, width = piece_refs[0].shape
+    tracks = updated_ref.shape[0] // frames
+    step = swap_part_ref.shape[0] // frames
     for start in range(0, count, step):
-        block = jnp.concatenate([virtual_ref[f, start : start + step] for f in range(frames)], axis=0)
-        virtual_out_ref[start * frames : (start + step) * frames] = matmul(
-            swap_matrix(step, frames), block
-        ).astype(BF)
-    query = query_ref[...]
-    flat = virtual_ref[...].reshape(frames * count, width)
+        block = jnp.concatenate([ref[start : start + step] for ref in piece_refs], axis=0)
+        virtual_out_ref[start * frames : (start + step) * frames] = matmul(swap_part_ref[...], block).astype(BF)
+    flat = jnp.concatenate([ref[...] for ref in piece_refs], axis=0)
     pair = matmul(normalize(flat), back_kv_ref[...]).astype(BF)
     items = []
-    for f in range(frames):
-        span = slice(f * count, (f + 1) * count)
-        items.append((query[f * tracks : (f + 1) * tracks], pair[span, :width], pair[span, width:], None))
+    for place in range(frames):
+        span = slice(place * count, (place + 1) * count)
+        queries = query_ref[place * tracks : (place + 1) * tracks]
+        items.append((queries, pair[span, :width], pair[span, width:], None))
     mixed = jnp.concatenate(attend(items, width), axis=0)
-    by_track = matmul(swap_matrix(tracks, frames), mixed).astype(BF)
+    by_track = matmul(swap_ref[...], mixed).astype(BF)
     out_ref[...] = (updated_ref[...].astype(F32) + matmul(by_track, back_out_ref[...])).astype(BF)
 
 
 def call(kernel, outs, *args, megabytes=32):
+    spaces = [pltpu.SMEM if arg.dtype == jnp.int32 and arg.ndim == 1 else pltpu.VMEM for arg in args]
     return pl.pallas_call(
         kernel,
         out_shape=[jax.ShapeDtypeStruct(shape, dtype) for shape, dtype in outs],
+        in_specs=[pl.BlockSpec(memory_space=space) for space in spaces],
         compiler_params=pltpu.CompilerParams(vmem_limit_bytes=megabytes * 1024 * 1024),
     )(*args)
 
@@ -300,7 +317,10 @@
     got = lax.all_to_all(send.reshape(frames, tracks, width), ("x", "zl"), 0, 0).reshape(rows, width)
     (partial,) = call(partial_kernel, [((count, width + 128), BF)], got, virt_query, virt_kv)
     (partial,) = call(both_kernel, [((count, width + 128), BF)], partial, shift(partial, "c", 2, 1))
-    (query,) = call(query_kernel, [((rows, width), BF)], normed, back_q)
+    place = jnp.stack([frame, lax.axis_index("c")]).astype(jnp.int32)
+    query, swap_part, swap = call(
+        query_kernel, [((rows, width), BF), ((2 * count, 2 * count), BF), ((rows, rows), BF)], place, normed, back_q
+    )
     split_pairs = [(z * 2 + c, (z ^ (2, 3)[c]) * 2 + c) for z in range(4) for c in range(2)]
     fetched = lax.ppermute(partial, ("zh", "c"), split_pairs)
     near = lax.ppermute(partial, "zh", [(z, z ^ 1) for z in range(4)])
@@ -308,13 +328,17 @@
     (frame_out,) = call(
         virtual_kernel, [((count, width), BF)], query, *partials, mine, virt_out, self_qkv, self_out
     )
-    gathered = lax.all_to_all(
-        jnp.broadcast_to(frame_out[None], (frames, count, width)), ("x", "zl"), 0, 0
-    )
+    pieces = [frame_out] + [None] * (frames - 1)
+    for k in GATHER_STEPS:
+        pairs = [(f * 2 + c, (f ^ (k + c)) * 2 + c) for f in range(frames) for c in range(2)]
+        pieces[k] = lax.ppermute(frame_out, ("x", "zl", "c"), pairs)
+    pieces[1] = lax.ppermute(frame_out, "zl", [(0, 1), (1, 0)])
+    for k in GATHER_STEPS:
+        pieces[k + 1] = shift(pieces[k], "c", 2, 1)
     tracks_out, virtual_out = call(
         back_kernel,
         [((rows, width), BF), ((count * frames, width), BF)],
-        updated, query, gathered, back_kv, back_out,
+        updated, query, swap_part, swap, *pieces, back_kv, back_out,
     )
     return tracks_out.reshape(tokens.shape), virtual_out.reshape(virtual.shape)
 

time: 58.8 us -> 57.4 us (0.976)
  blocking collectives: 20.5 us -> 10.4 us
  starting transfers between devices: 17 us -> 25.2 us
    all_to_all x1 -> x0, blocking collectives: 10.3 us -> none  [on_device(): lax.all_to_all(jnp.broadcast_to(frame_out[None], (frames, count, width)),...]
    ppermute x0 -> x4, starting transfers between devices: none -> 5.41 us  [the longest x3 3.03 us: on_device(): pieces[k] = lax.ppermute(frame_out, ('x', 'zl', 'c'), pairs)]
    ppermute x5 -> x8, starting transfers between devices: 10.6 us -> 13.4 us  [shift(): lax.ppermute(value, axis, [(i, (i + step) % count) for i in range(count)])]
    ppermute x5 -> x8, waiting for transfers between devices: 4.71 us -> 5.59 us  [shift(): lax.ppermute(value, axis, [(i, (i + step) % count) for i in range(count)])]
    ppermute x1, waiting for transfers between devices: 2.49 us -> 1.87 us  [on_device(): near = lax.ppermute(partial, 'zh', [(z, z ^ 1) for z in range(4)])]
  transfers between devices with their start and end apart: 7 -> 14, of which waited for: 5 -> 7; matrix products, arithmetic and copies ran while one was open for 2% -> 2% of each run, Pallas kernels for 3% -> 4%
where the time goes in v5:
time: 57.4 us; the launch traced here: 57.2 us
  starting transfers between devices  25.2 us (44%)
  blocking collectives  10.4 us (18%)
  Pallas kernels  9.07 us (16%)
  waiting for transfers between devices  8.2 us (14%)
  local copies, waits for them, and re-layouts  3.49 us (6%)
  between operations  0.81 us (1%)
    ppermute x8, starting transfers between devices, shift(): lax.ppermute(value, axis, [(i, (i + step) % count) for i in range(count)])  13.4 us
    all_to_all x1, blocking collectives, on_device(): lax.all_to_all(send.reshape(frames, tracks, width), ('x', 'zl'), 0, 0)  10.4 us
    pallas_call x8, Pallas kernels, call(): pl.pallas_call(kernel, out_shape=[jax.ShapeDtypeStruct(shape, dtype) for...  9.07 us
    ppermute x8, waiting for transfers between devices, shift(): lax.ppermute(value, axis, [(i, (i + step) % count) for i in range(count)])  5.59 us
    ppermute x1, starting transfers between devices, on_device(): fetched = lax.ppermute(partial, ('zh', 'c'), split_pairs)  5.21 us
    unnamed x28, local copies, waits for them, and re-layouts  3.38 us
    ppermute x3, starting transfers between devices, on_device(): pieces[k] = lax.ppermute(frame_out, ('x', 'zl', 'c'), pairs)  3.03 us
    ppermute x1, starting transfers between devices, on_device(): pieces[1] = lax.ppermute(frame_out, 'zl', [(0, 1), (1, 0)])  2.38 us
  transfers between devices with their start and end apart: 14, of which 7 were waited for; matrix products, arithmetic and copies ran while one was open for 2% of the time, Pallas kernels for 4%

profile of v5, /device:TPU:1, one launch (start us, length us, event | category | flops | bytes accessed | tf_op | source)
XLA Modules:
  0.0 57.2 jit_solution(3053697868751879071)
XLA Ops:
  0.6 0.0 copy-start
  0.6 0.0 copy-start.4
  0.7 3.8 %collective-permute-start = (bf16[256,384]{1,0:T(8,128)(2,1)}, bf16[256,384]{1,0:T(8,128)(2,1)S(1)}, u32[]{:S(2)}, u32[]{:S(2)}) collective-permute-start(bf16[256,384]{1,0:T(8,128)(2,1)} %bitcast.11), channel_id=1, source_target_pairs={{0,2},{1,3},{2,0},{3,1},{4,6},{5,7},{6,4},{7,5},{8,10},{9,11},{10,... | collective-permute-start | bytes 589832 | tf_op jit(solution)/shard_map/ppermute | solution.py:293
  4.5 0.8 %collective-permute-start.2 = (bf16[256,384]{1,0:T(8,128)(2,1)}, bf16[256,384]{1,0:T(8,128)(2,1)S(1)}, u32[]{:S(2)}, u32[]{:S(2)}) collective-permute-start(bf16[256,384]{1,0:T(8,128)(2,1)} %bitcast.12), channel_id=1, source_target_pairs={{0,3},{1,0},{2,1},{3,2},{4,7},{5,4},{6,5},{7,6},{8,11},{9,8},{10,9... | collective-permute-start | bytes 589832 | tf_op jit(solution)/shard_map/ppermute | solution.py:293
  5.3 0.7 %collective-permute-start.1 = (bf16[256,384]{1,0:T(8,128)(2,1)}, bf16[256,384]{1,0:T(8,128)(2,1)S(1)}, u32[]{:S(2)}, u32[]{:S(2)}) collective-permute-start(bf16[256,384]{1,0:T(8,128)(2,1)} %bitcast.13), channel_id=1, source_target_pairs={{0,1},{1,2},{2,3},{3,0},{4,5},{5,6},{6,7},{7,4},{8,9},{9,10},{10,1... | collective-permute-start | bytes 589832 | tf_op jit(solution)/shard_map/ppermute | solution.py:293
  6.0 0.8 %copy.17.refs_5_ = s32[32,8]{1,0:T(8,128)S(1)} copy(s32[32,8]{0,1:T(8,128)} %param.14) | data formatting | bytes 2048 | tf_op args[1]
  6.7 0.0 copy-done
  6.7 0.1 constant_dynamic-slice_fusion
  6.8 0.0 copy-done.4
  6.9 0.0 copy-start.1
  6.9 1.2 %copy-done.1 = bf16[384,1152]{1,0:T(8,128)(2,1)S(1)} copy-done((bf16[384,1152]{1,0:T(8,128)(2,1)S(1)}, bf16[384,1152]{1,0:T(8,128)(2,1)}, u32[]{:S(2)}) %copy-start.1) | copy-done | bytes 884760
  8.0 0.0 copy-start.9
  8.0 1.0 %copy-done.9 = bf16[384,384]{1,0:T(8,128)(2,1)S(1)} copy-done((bf16[384,384]{1,0:T(8,128)(2,1)S(1)}, bf16[384,384]{1,0:T(8,128)(2,1)}, u32[]{:S(2)}) %copy-start.9) | copy-done | bytes 294936
  9.0 0.0 copy-start.2
  9.0 0.7 %shard_map.140 = (bf16[256,1152]{1,0:T(8,128)(2,1)S(1)}, bf16[64,384]{1,0:T(8,128)(2,1)S(1)}) custom-call(bf16[256,384]{1,0:T(8,128)(2,1)S(1)} %bitcast.14, bf16[64,384]{1,0:T(8,128)(2,1)S(1)} %bitcast.16, bf16[384,1152]{1,0:T(8,128)(2,1)S(1)} %copy-done.1, bf16[384,384]{1,0:T(8,128)(2,1)S(1)} %copy-done.9), custom_call_target="tpu_custom_call" | custom-call | tf_op jit(solution)/shard_map/pallas_call | solution.py:284
  9.7 0.0 copy-start.10
  9.7 0.0 collective-permute-done.tokens_ref
  9.7 0.4 copy-done.2
  10.2 0.5 shard_map.141.refs_2_
  10.7 3.0 %collective-permute-done.2.refs_4_ = bf16[256,384]{1,0:T(8,128)(2,1)S(1)} collective-permute-done((bf16[256,384]{1,0:T(8,128)(2,1)}, bf16[256,384]{1,0:T(8,128)(2,1)S(1)}, u32[]{:S(2)}, u32[]{:S(2)}) %collective-permute-start.2) | collective-permute-done | bytes 196640 | tf_op jit(solution)/shard_map/ppermute | solution.py:293
  13.8 0.8 %collective-permute-done.1.refs_3_ = bf16[256,384]{1,0:T(8,128)(2,1)S(1)} collective-permute-done((bf16[256,384]{1,0:T(8,128)(2,1)}, bf16[256,384]{1,0:T(8,128)(2,1)S(1)}, u32[]{:S(2)}, u32[]{:S(2)}) %collective-permute-start.1) | collective-permute-done | bytes 196640 | tf_op jit(solution)/shard_map/ppermute | solution.py:293
  14.5 0.0 copy-done.10
  14.5 0.0 copy-start.6
  14.5 2.1 %shard_map.142 = (bf16[256,384]{1,0:T(8,128)(2,1)S(1)}, bf16[256,384]{1,0:T(8,128)(2,1)S(1)}, bf16[256,384]{1,0:T(8,128)(2,1)S(1)}) custom-call(bf16[256,384]{1,0:T(8,128)(2,1)S(1)} %bitcast.15, bf16[256,1152]{1,0:T(8,128)(2,1)S(1)} %get-tuple-element.12.refs_1_, bf16[256,768]{1,0:T(8,128)(2,1)S(1)} %shard_map.141.refs_2_, ...), custom_call_target="tpu_custom_call" | custom-call | tf_op jit(solution)/shard_map/pallas_call | solution.py:284
  16.6 0.0 copy-start.8
  16.6 10.4 %all_to_all.5 = bf16[8,32,384]{2,1,0:T(8,128)(2,1)S(1)} all-to-all(bf16[8,32,384]{2,1,0:T(8,128)(2,1)S(1)} %bitcast.18), channel_id=1, replica_groups=mesh['x'=4,'zh'=4,'zl'=2,'c'=2,'y'=4] {'x','zl'}, dimensions={0} | all-to-all | bytes 393216 | tf_op jit(solution)/shard_map/all_to_all | solution.py:317
  27.0 0.0 copy-done.6
  27.0 0.7 %shard_map.144.a_ref = bf16[64,512]{1,0:T(8,128)(2,1)S(1)} custom-call(bf16[256,384]{1,0:T(8,128)(2,1)S(1)} %bitcast.10, bf16[64,384]{1,0:T(8,128)(2,1)S(1)} %get-tuple-element.19.query_ref, bf16[384,768]{1,0:T(8,128)(2,1)S(1)} %copy-done.6), custom_call_target="tpu_custom_call" | custom-call | tf_op jit(solution)/shard_map/pallas_call | solution.py:284
  27.7 3.0 %collective-permute-start.3 = (bf16[64,512]{1,0:T(8,128)(2,1)S(1)}, bf16[64,512]{1,0:T(8,128)(2,1)S(1)}, u32[]{:S(2)}, u32[]{:S(2)}) collective-permute-start(bf16[64,512]{1,0:T(8,128)(2,1)S(1)} %shard_map.144.a_ref), channel_id=1, source_target_pairs={{0,4},{4,0},{1,5},{5,1},{2,6},{6,2},{3,7},{7,3},{8,12},{12,8},{9,1... | collective-permute-start | bytes 196616 | tf_op jit(solution)/shard_map/ppermute | solution.py:293
  30.7 0.9 %collective-permute-done.3.b_ref = bf16[64,512]{1,0:T(8,128)(2,1)S(1)} collective-permute-done((bf16[64,512]{1,0:T(8,128)(2,1)S(1)}, bf16[64,512]{1,0:T(8,128)(2,1)S(1)}, u32[]{:S(2)}, u32[]{:S(2)}) %collective-permute-start.3) | collective-permute-done | bytes 65568 | tf_op jit(solution)/shard_map/ppermute | solution.py:293
  31.6 0.3 shard_map.145.refs_1_
  31.9 0.0 copy-start.11
  31.9 5.2 %collective-permute-start.4 = (bf16[64,512]{1,0:T(8,128)(2,1)S(1)}, bf16[64,512]{1,0:T(8,128)(2,1)S(1)}, u32[]{:S(2)}, u32[]{:S(2)}) collective-permute-start(bf16[64,512]{1,0:T(8,128)(2,1)S(1)} %shard_map.145.refs_1_), channel_id=1, source_target_pairs={{0,32},{4,52},{16,48},{20,36},{32,0},{36,20},{48,16},{52,4},{1,33}... | collective-permute-start | bytes 196616 | tf_op jit(solution)/shard_map/ppermute | solution.py:325
  37.1 1.2 %collective-permute-start.6 = (bf16[64,512]{1,0:T(8,128)(2,1)S(1)}, bf16[64,512]{1,0:T(8,128)(2,1)S(1)}, u32[]{:S(2)}, u32[]{:S(2)}) collective-permute-start(bf16[64,512]{1,0:T(8,128)(2,1)S(1)} %shard_map.145.refs_1_), channel_id=1, source_target_pairs={{0,16},{16,0},{32,48},{48,32},{1,17},{17,1},{33,49},{49,33},{2,18}... | collective-permute-start | bytes 196616 | tf_op jit(solution)/shard_map/ppermute | solution.py:326
  38.3 0.7 %collective-permute-done.4.refs_2_ = bf16[64,512]{1,0:T(8,128)(2,1)S(1)} collective-permute-done((bf16[64,512]{1,0:T(8,128)(2,1)S(1)}, bf16[64,512]{1,0:T(8,128)(2,1)S(1)}, u32[]{:S(2)}, u32[]{:S(2)}) %collective-permute-start.4) | collective-permute-done | bytes 65568 | tf_op jit(solution)/shard_map/ppermute | solution.py:325
  39.0 2.3 %collective-permute-start.5 = (bf16[64,512]{1,0:T(8,128)(2,1)S(1)}, bf16[64,512]{1,0:T(8,128)(2,1)S(1)}, u32[]{:S(2)}, u32[]{:S(2)}) collective-permute-start(bf16[64,512]{1,0:T(8,128)(2,1)S(1)} %collective-permute-done.4.refs_2_), channel_id=1, source_target_pairs={{0,4},{4,0},{1,5},{5,1},{2,6},{6,2},{3,7},{7,3},{8,12},{12,8},{9,1... | collective-permute-start | bytes 196616 | tf_op jit(solution)/shard_map/ppermute | solution.py:293
  41.4 0.1 pad_add_fusion.place_ref
  41.4 0.0 copy-done.8
  41.4 0.8 %shard_map.143 = (bf16[256,384]{1,0:T(8,128)(2,1)S(1)}, bf16[128,128]{1,0:T(8,128)(2,1)S(1)}, bf16[256,256]{1,0:T(8,128)(2,1)S(1)}) custom-call(s32[2]{0:T(128)S(1)} %pad_add_fusion.place_ref, bf16[256,384]{1,0:T(8,128)(2,1)S(1)} %get-tuple-element.14.normed_ref, bf16[384,384]{1,0:T(8,128)(2,1)S(1)} %copy-done.8), custom_call_target="tpu_custom_call" | custom-call | tf_op jit(solution)/shard_map/pallas_call | solution.py:284
  42.3 1.9 %collective-permute-done.6.refs_4_ = bf16[64,512]{1,0:T(8,128)(2,1)S(1)} collective-permute-done((bf16[64,512]{1,0:T(8,128)(2,1)S(1)}, bf16[64,512]{1,0:T(8,128)(2,1)S(1)}, u32[]{:S(2)}, u32[]{:S(2)}) %collective-permute-start.6) | collective-permute-done | bytes 65568 | tf_op jit(solution)/shard_map/ppermute | solution.py:326
  44.1 0.0 collective-permute-done.5.refs_3_
  44.1 0.0 copy-done.3
  44.1 0.0 copy-done.12
  44.1 0.0 copy-done.11
  44.2 0.0 copy-start.5
  44.2 0.0 copy-start.7
  44.2 1.4 %shard_map.146.refs_0_ = bf16[64,384]{1,0:T(8,128)(2,1)S(1)} custom-call(bf16[256,384]{1,0:T(8,128)(2,1)S(1)} %get-tuple-element.15.refs_0_.query_ref, bf16[64,512]{1,0:T(8,128)(2,1)S(1)} %shard_map.145.refs_1_, bf16[64,512]{1,0:T(8,128)(2,1)S(1)} %collective-permute-done.4.refs_2_, bf16[64,512]{1,0:T(8,128)(2,1)S(1)} %collective-permute-done.5.refs_3_, ...), custom_call_target="tpu_custom_call" | custom-call | tf_op jit(solution)/shard_map/pallas_call | solution.py:284
  45.6 0.1 collective-permute-start.12
  45.7 2.9 %collective-permute-start.10 = (bf16[64,384]{1,0:T(8,128)(2,1)S(1)}, bf16[64,384]{1,0:T(8,128)(2,1)S(1)}, u32[]{:S(2)}, u32[]{:S(2)}) collective-permute-start(bf16[64,384]{1,0:T(8,128)(2,1)S(1)} %shard_map.146.refs_0_), channel_id=1, source_target_pairs={{0,128},{4,140},{8,136},{12,132},{64,192},{68,204},{72,200},{76,19... | collective-permute-start | bytes 147464 | tf_op jit(solution)/shard_map/ppermute | solution.py:334
  48.6 0.0 collective-permute-start.8
  48.6 2.4 %collective-permute-start.7 = (bf16[64,384]{1,0:T(8,128)(2,1)S(1)}, bf16[64,384]{1,0:T(8,128)(2,1)S(1)}, u32[]{:S(2)}, u32[]{:S(2)}) collective-permute-start(bf16[64,384]{1,0:T(8,128)(2,1)S(1)} %shard_map.146.refs_0_), channel_id=1, source_target_pairs={{0,8},{8,0},{1,9},{9,1},{2,10},{10,2},{3,11},{11,3},{4,12},{12,4},... | collective-permute-start | bytes 147464 | tf_op jit(solution)/shard_map/ppermute | solution.py:335
  51.0 0.0 collective-permute-done.12.refs_6_
  51.0 1.5 %collective-permute-start.13 = (bf16[64,384]{1,0:T(8,128)(2,1)S(1)}, bf16[64,384]{1,0:T(8,128)(2,1)S(1)}, u32[]{:S(2)}, u32[]{:S(2)}) collective-permute-start(bf16[64,384]{1,0:T(8,128)(2,1)S(1)} %collective-permute-done.12.refs_6_), channel_id=1, source_target_pairs={{0,4},{4,0},{1,5},{5,1},{2,6},{6,2},{3,7},{7,3},{8,12},{12,8},{9,1... | collective-permute-start | bytes 147464 | tf_op jit(solution)/shard_map/ppermute | solution.py:293
  52.4 0.0 collective-permute-done.10.refs_4_
  52.4 0.8 %collective-permute-start.11 = (bf16[64,384]{1,0:T(8,128)(2,1)S(1)}, bf16[64,384]{1,0:T(8,128)(2,1)S(1)}, u32[]{:S(2)}, u32[]{:S(2)}) collective-permute-start(bf16[64,384]{1,0:T(8,128)(2,1)S(1)} %collective-permute-done.10.refs_4_), channel_id=1, source_target_pairs={{0,4},{4,0},{1,5},{5,1},{2,6},{6,2},{3,7},{7,3},{8,12},{12,8},{9,1... | collective-permute-start | bytes 147464 | tf_op jit(solution)/shard_map/ppermute | solution.py:293
  53.2 0.0 collective-permute-done.8.refs_2_
  53.2 0.6 %collective-permute-start.9 = (bf16[64,384]{1,0:T(8,128)(2,1)S(1)}, bf16[64,384]{1,0:T(8,128)(2,1)S(1)}, u32[]{:S(2)}, u32[]{:S(2)}) collective-permute-start(bf16[64,384]{1,0:T(8,128)(2,1)S(1)} %collective-permute-done.8.refs_2_), channel_id=1, source_target_pairs={{0,4},{4,0},{1,5},{5,1},{2,6},{6,2},{3,7},{7,3},{8,12},{12,8},{9,1... | collective-permute-start | bytes 147464 | tf_op jit(solution)/shard_map/ppermute | solution.py:293
  53.8 0.0 collective-permute-done.7.refs_1_
  53.8 0.0 collective-permute-done.13.refs_7_
  53.8 0.3 collective-permute-done.11.refs_5_
  54.1 0.6 %collective-permute-done.9.refs_3_ = bf16[64,384]{1,0:T(8,128)(2,1)S(1)} collective-permute-done((bf16[64,384]{1,0:T(8,128)(2,1)S(1)}, bf16[64,384]{1,0:T(8,128)(2,1)S(1)}, u32[]{:S(2)}, u32[]{:S(2)}) %collective-permute-start.9) | collective-permute-done | bytes 49184 | tf_op jit(solution)/shard_map/ppermute | solution.py:293
  54.7 0.0 copy-done.5
  54.7 0.0 copy-done.7
  54.7 2.5 %shard_map.147 = (bf16[256,384]{1,0:T(8,128)(2,1)}, bf16[512,384]{1,0:T(8,128)(2,1)}) custom-call(bf16[256,384]{1,0:T(8,128)(2,1)S(1)} %get-tuple-element.13.updated_ref, bf16[256,384]{1,0:T(8,128)(2,1)S(1)} %get-tuple-element.15.refs_0_.query_ref, bf16[128,128]{1,0:T(8,128)(2,1)S(1)} %get-tuple-element.16.swap_part_ref, ...), custom_call_target="tpu_custom_call" | custom-call | tf_op jit(solution)/shard_map/pallas_call | solution.py:284
  (3 shorter events, 0.0 us)
Async XLA Ops:
  0.6 6.1 %copy-start = (bf16[64,8,384]{2,1,0:T(8,128)(2,1)S(1)}, bf16[64,8,384]{2,1,0:T(8,128)(2,1)}, u32[]{:S(2)}) copy-start(bf16[64,8,384]{2,1,0:T(8,128)(2,1)} %param.15) | copy-start | bytes 1179652
  0.6 6.2 %copy-start.4 = (bf16[32,8,384]{2,1,0:T(8,128)(2,1)S(1)}, bf16[32,8,384]{2,1,0:T(8,128)(2,1)}, u32[]{:S(2)}) copy-start(bf16[32,8,384]{2,1,0:T(8,128)(2,1)} %param.13) | copy-start | bytes 589828
  0.7 9.1 %collective-permute-start = (bf16[256,384]{1,0:T(8,128)(2,1)}, bf16[256,384]{1,0:T(8,128)(2,1)S(1)}, u32[]{:S(2)}, u32[]{:S(2)}) collective-permute-start(bf16[256,384]{1,0:T(8,128)(2,1)} %bitcast.11), channel_id=1, source_target_pairs={{0,2},{1,3},{2,0},{3,1},{4,6},{5,7},{6,4},{7,5},{8,10},{9,11},{10,... | collective-permute-start | bytes 589832 | tf_op jit(solution)/shard_map/ppermute | solution.py:293
  4.5 9.3 %collective-permute-start.2 = (bf16[256,384]{1,0:T(8,128)(2,1)}, bf16[256,384]{1,0:T(8,128)(2,1)S(1)}, u32[]{:S(2)}, u32[]{:S(2)}) collective-permute-start(bf16[256,384]{1,0:T(8,128)(2,1)} %bitcast.12), channel_id=1, source_target_pairs={{0,3},{1,0},{2,1},{3,2},{4,7},{5,4},{6,5},{7,6},{8,11},{9,8},{10,9... | collective-permute-start | bytes 589832 | tf_op jit(solution)/shard_map/ppermute | solution.py:293
  5.3 9.2 %collective-permute-start.1 = (bf16[256,384]{1,0:T(8,128)(2,1)}, bf16[256,384]{1,0:T(8,128)(2,1)S(1)}, u32[]{:S(2)}, u32[]{:S(2)}) collective-permute-start(bf16[256,384]{1,0:T(8,128)(2,1)} %bitcast.13), channel_id=1, source_target_pairs={{0,1},{1,2},{2,3},{3,0},{4,5},{5,6},{6,7},{7,4},{8,9},{9,10},{10,1... | collective-permute-start | bytes 589832 | tf_op jit(solution)/shard_map/ppermute | solution.py:293
  6.9 1.2 %copy-start.1 = (bf16[384,1152]{1,0:T(8,128)(2,1)S(1)}, bf16[384,1152]{1,0:T(8,128)(2,1)}, u32[]{:S(2)}) copy-start(bf16[384,1152]{1,0:T(8,128)(2,1)} %refs_6_.2) | copy-start | bytes 2654212
  8.0 1.0 %copy-start.9 = (bf16[384,384]{1,0:T(8,128)(2,1)S(1)}, bf16[384,384]{1,0:T(8,128)(2,1)}, u32[]{:S(2)}) copy-start(bf16[384,384]{1,0:T(8,128)(2,1)} %virt_q_ref.1) | copy-start | bytes 884740
  9.0 1.2 %copy-start.2 = (bf16[384,1152]{1,0:T(8,128)(2,1)S(1)}, bf16[384,1152]{1,0:T(8,128)(2,1)}, u32[]{:S(2)}) copy-start(bf16[384,1152]{1,0:T(8,128)(2,1)} %refs_6_.2) | copy-start | bytes 2654212
  9.7 4.8 %copy-start.10 = (bf16[384,384]{1,0:T(8,128)(2,1)S(1)}, bf16[384,384]{1,0:T(8,128)(2,1)}, u32[]{:S(2)}) copy-start(bf16[384,384]{1,0:T(8,128)(2,1)} %refs_7_.2) | copy-start | bytes 884740
  14.5 12.5 %copy-start.6 = (bf16[384,768]{1,0:T(8,128)(2,1)S(1)}, bf16[384,768]{1,0:T(8,128)(2,1)}, u32[]{:S(2)}) copy-start(bf16[384,768]{1,0:T(8,128)(2,1)} %virt_kv_ref.1) | copy-start | bytes 1769476
  16.6 24.9 %copy-start.8 = (bf16[384,384]{1,0:T(8,128)(2,1)S(1)}, bf16[384,384]{1,0:T(8,128)(2,1)}, u32[]{:S(2)}) copy-start(bf16[384,384]{1,0:T(8,128)(2,1)} %back_q_ref.1) | copy-start | bytes 884740
  27.0 17.2 %copy-start.3 = (bf16[384,1152]{1,0:T(8,128)(2,1)S(1)}, bf16[384,1152]{1,0:T(8,128)(2,1)}, u32[]{:S(2)}) copy-start(bf16[384,1152]{1,0:T(8,128)(2,1)} %refs_7_.3) | copy-start | bytes 2654212
  27.7 3.9 %collective-permute-start.3 = (bf16[64,512]{1,0:T(8,128)(2,1)S(1)}, bf16[64,512]{1,0:T(8,128)(2,1)S(1)}, u32[]{:S(2)}, u32[]{:S(2)}) collective-permute-start(bf16[64,512]{1,0:T(8,128)(2,1)S(1)} %shard_map.144.a_ref), channel_id=1, source_target_pairs={{0,4},{4,0},{1,5},{5,1},{2,6},{6,2},{3,7},{7,3},{8,12},{12,8},{9,1... | collective-permute-start | bytes 196616 | tf_op jit(solution)/shard_map/ppermute | solution.py:293
  31.6 12.5 %copy-start.12 = (bf16[384,384]{1,0:T(8,128)(2,1)S(1)}, bf16[384,384]{1,0:T(8,128)(2,1)}, u32[]{:S(2)}) copy-start(bf16[384,384]{1,0:T(8,128)(2,1)} %refs_8_.2) | copy-start | bytes 884740
  31.9 12.2 %copy-start.11 = (bf16[384,384]{1,0:T(8,128)(2,1)S(1)}, bf16[384,384]{1,0:T(8,128)(2,1)}, u32[]{:S(2)}) copy-start(bf16[384,384]{1,0:T(8,128)(2,1)} %refs_6_.3) | copy-start | bytes 884740
  31.9 7.1 %collective-permute-start.4 = (bf16[64,512]{1,0:T(8,128)(2,1)S(1)}, bf16[64,512]{1,0:T(8,128)(2,1)S(1)}, u32[]{:S(2)}, u32[]{:S(2)}) collective-permute-start(bf16[64,512]{1,0:T(8,128)(2,1)S(1)} %shard_map.145.refs_1_), channel_id=1, source_target_pairs={{0,32},{4,52},{16,48},{20,36},{32,0},{36,20},{48,16},{52,4},{1,33}... | collective-permute-start | bytes 196616 | tf_op jit(solution)/shard_map/ppermute | solution.py:325
  37.1 7.0 %collective-permute-start.6 = (bf16[64,512]{1,0:T(8,128)(2,1)S(1)}, bf16[64,512]{1,0:T(8,128)(2,1)S(1)}, u32[]{:S(2)}, u32[]{:S(2)}) collective-permute-start(bf16[64,512]{1,0:T(8,128)(2,1)S(1)} %shard_map.145.refs_1_), channel_id=1, source_target_pairs={{0,16},{16,0},{32,48},{48,32},{1,17},{17,1},{33,49},{49,33},{2,18}... | collective-permute-start | bytes 196616 | tf_op jit(solution)/shard_map/ppermute | solution.py:326
  39.0 5.1 %collective-permute-start.5 = (bf16[64,512]{1,0:T(8,128)(2,1)S(1)}, bf16[64,512]{1,0:T(8,128)(2,1)S(1)}, u32[]{:S(2)}, u32[]{:S(2)}) collective-permute-start(bf16[64,512]{1,0:T(8,128)(2,1)S(1)} %collective-permute-done.4.refs_2_), channel_id=1, source_target_pairs={{0,4},{4,0},{1,5},{5,1},{2,6},{6,2},{3,7},{7,3},{8,12},{12,8},{9,1... | collective-permute-start | bytes 196616 | tf_op jit(solution)/shard_map/ppermute | solution.py:293
  44.2 10.5 %copy-start.5 = (bf16[384,768]{1,0:T(8,128)(2,1)S(1)}, bf16[384,768]{1,0:T(8,128)(2,1)}, u32[]{:S(2)}) copy-start(bf16[384,768]{1,0:T(8,128)(2,1)} %refs_8_.3) | copy-start | bytes 1769476
  44.2 10.5 %copy-start.7 = (bf16[384,384]{1,0:T(8,128)(2,1)S(1)}, bf16[384,384]{1,0:T(8,128)(2,1)}, u32[]{:S(2)}) copy-start(bf16[384,384]{1,0:T(8,128)(2,1)} %refs_9_.1) | copy-start | bytes 884740
  45.6 5.4 %collective-permute-start.12 = (bf16[64,384]{1,0:T(8,128)(2,1)S(1)}, bf16[64,384]{1,0:T(8,128)(2,1)S(1)}, u32[]{:S(2)}, u32[]{:S(2)}) collective-permute-start(bf16[64,384]{1,0:T(8,128)(2,1)S(1)} %shard_map.146.refs_0_), channel_id=1, source_target_pairs={{0,192},{4,204},{8,200},{12,196},{64,128},{68,140},{72,136},{76,13... | collective-permute-start | bytes 147464 | tf_op jit(solution)/shard_map/ppermute | solution.py:334
  45.7 6.8 %collective-permute-start.10 = (bf16[64,384]{1,0:T(8,128)(2,1)S(1)}, bf16[64,384]{1,0:T(8,128)(2,1)S(1)}, u32[]{:S(2)}, u32[]{:S(2)}) collective-permute-start(bf16[64,384]{1,0:T(8,128)(2,1)S(1)} %shard_map.146.refs_0_), channel_id=1, source_target_pairs={{0,128},{4,140},{8,136},{12,132},{64,192},{68,204},{72,200},{76,19... | collective-permute-start | bytes 147464 | tf_op jit(solution)/shard_map/ppermute | solution.py:334
  48.6 4.6 %collective-permute-start.8 = (bf16[64,384]{1,0:T(8,128)(2,1)S(1)}, bf16[64,384]{1,0:T(8,128)(2,1)S(1)}, u32[]{:S(2)}, u32[]{:S(2)}) collective-permute-start(bf16[64,384]{1,0:T(8,128)(2,1)S(1)} %shard_map.146.refs_0_), channel_id=1, source_target_pairs={{0,64},{4,76},{8,72},{12,68},{64,0},{68,12},{72,8},{76,4},{128,192... | collective-permute-start | bytes 147464 | tf_op jit(solution)/shard_map/ppermute | solution.py:334
  48.6 5.2 %collective-permute-start.7 = (bf16[64,384]{1,0:T(8,128)(2,1)S(1)}, bf16[64,384]{1,0:T(8,128)(2,1)S(1)}, u32[]{:S(2)}, u32[]{:S(2)}) collective-permute-start(bf16[64,384]{1,0:T(8,128)(2,1)S(1)} %shard_map.146.refs_0_), channel_id=1, source_target_pairs={{0,8},{8,0},{1,9},{9,1},{2,10},{10,2},{3,11},{11,3},{4,12},{12,4},... | collective-permute-start | bytes 147464 | tf_op jit(solution)/shard_map/ppermute | solution.py:335
  51.0 2.8 %collective-permute-start.13 = (bf16[64,384]{1,0:T(8,128)(2,1)S(1)}, bf16[64,384]{1,0:T(8,128)(2,1)S(1)}, u32[]{:S(2)}, u32[]{:S(2)}) collective-permute-start(bf16[64,384]{1,0:T(8,128)(2,1)S(1)} %collective-permute-done.12.refs_6_), channel_id=1, source_target_pairs={{0,4},{4,0},{1,5},{5,1},{2,6},{6,2},{3,7},{7,3},{8,12},{12,8},{9,1... | collective-permute-start | bytes 147464 | tf_op jit(solution)/shard_map/ppermute | solution.py:293
  52.4 1.7 %collective-permute-start.11 = (bf16[64,384]{1,0:T(8,128)(2,1)S(1)}, bf16[64,384]{1,0:T(8,128)(2,1)S(1)}, u32[]{:S(2)}, u32[]{:S(2)}) collective-permute-start(bf16[64,384]{1,0:T(8,128)(2,1)S(1)} %collective-permute-done.10.refs_4_), channel_id=1, source_target_pairs={{0,4},{4,0},{1,5},{5,1},{2,6},{6,2},{3,7},{7,3},{8,12},{12,8},{9,1... | collective-permute-start | bytes 147464 | tf_op jit(solution)/shard_map/ppermute | solution.py:293
  53.2 1.5 %collective-permute-start.9 = (bf16[64,384]{1,0:T(8,128)(2,1)S(1)}, bf16[64,384]{1,0:T(8,128)(2,1)S(1)}, u32[]{:S(2)}, u32[]{:S(2)}) collective-permute-start(bf16[64,384]{1,0:T(8,128)(2,1)S(1)} %collective-permute-done.8.refs_2_), channel_id=1, source_target_pairs={{0,4},{4,0},{1,5},{5,1},{2,6},{6,2},{3,7},{7,3},{8,12},{12,8},{9,1... | collective-permute-start | bytes 147464 | tf_op jit(solution)/shard_map/ppermute | solution.py:293

commit v6 on v5

--- a/solution.py
+++ b/solution.py
@@ -15,6 +15,7 @@
 STEPS = (2, 1, 3)
 EARLY = 1
 GATHER_STEPS = (4, 2, 6)
+FIRST_PLACES = (0, 1, 6, 7)
 MARK = 64.0
 BF = jnp.bfloat16
 F32 = jnp.float32
@@ -258,23 +259,40 @@
     out_ref[...] = matmul(ordered, back_q_ref[...]).astype(BF)
 
 
-def back_kernel(updated_ref, query_ref, swap_part_ref, swap_ref, *refs):
+def attend_pieces(places, tracks, query_ref, piece_refs, back_kv_ref):
+    count, width = piece_refs[0].shape
+    flat = jnp.concatenate([ref[...] for ref in piece_refs], axis=0)
+    pair = matmul(normalize(flat), back_kv_ref[...]).astype(BF)
+    items = []
+    for k, place in enumerate(places):
+        span = slice(k * count, (k + 1) * count)
+        queries = query_ref[place * tracks : (place + 1) * tracks]
+        items.append((queries, pair[span, :width], pair[span, width:], None))
+    return attend(items, width)
+
+
+def front_kernel(query_ref, *refs):
+    *piece_refs, back_kv_ref, out_ref = refs
+    tracks = out_ref.shape[0] // len(FIRST_PLACES)
+    out_ref[...] = jnp.concatenate(
+        attend_pieces(FIRST_PLACES, tracks, query_ref, piece_refs, back_kv_ref), axis=0
+    )
+
+
+def back_kernel(updated_ref, query_ref, swap_part_ref, swap_ref, front_ref, *refs):
     *piece_refs, back_kv_ref, back_out_ref, out_ref, virtual_out_ref = refs
     frames = len(piece_refs)
-    count, width = piece_refs[0].shape
+    count = piece_refs[0].shape[0]
     tracks = updated_ref.shape[0] // frames
     step = swap_part_ref.shape[0] // frames
     for start in range(0, count, step):
         block = jnp.concatenate([ref[start : start + step] for ref in piece_refs], axis=0)
         virtual_out_ref[start * frames : (start + step) * frames] = matmul(swap_part_ref[...], block).astype(BF)
-    flat = jnp.concatenate([ref[...] for ref in piece_refs], axis=0)
-    pair = matmul(normalize(flat), back_kv_ref[...]).astype(BF)
-    items = []
-    for place in range(frames):
-        span = slice(place * count, (place + 1) * count)
-        queries = query_ref[place * tracks : (place + 1) * tracks]
-        items.append((queries, pair[span, :width], pair[span, width:], None))
-    mixed = jnp.concatenate(attend(items, width), axis=0)
+    rest = [place for place in range(frames) if place not in FIRST_PLACES]
+    mixed = dict(zip(rest, attend_pieces(rest, tracks, query_ref, [piece_refs[k] for k in rest], back_kv_ref)))
+    for k, place in enumerate(FIRST_PLACES):
+        mixed[place] = front_ref[k * tracks : (k + 1) * tracks]
+    mixed = jnp.concatenate([mixed[place] for place in range(frames)], axis=0)
     by_track = matmul(swap_ref[...], mixed).astype(BF)
     out_ref[...] = (updated_ref[...].astype(F32) + matmul(by_track, back_out_ref[...])).astype(BF)
 
@@ -335,10 +353,14 @@
     pieces[1] = lax.ppermute(frame_out, "zl", [(0, 1), (1, 0)])
     for k in GATHER_STEPS:
         pieces[k + 1] = shift(pieces[k], "c", 2, 1)
+    (front,) = call(
+        front_kernel, [((len(FIRST_PLACES) * tracks, width), BF)],
+        query, *[pieces[place] for place in FIRST_PLACES], back_kv,
+    )
     tracks_out, virtual_out = call(
         back_kernel,
         [((rows, width), BF), ((count * frames, width), BF)],
-        updated, query, swap_part, swap, *pieces, back_kv, back_out,
+        updated, query, swap_part, swap, front, *pieces, back_kv, back_out,
     )
     return tracks_out.reshape(tokens.shape), virtual_out.reshape(virtual.shape)
 

time: 57.4 us -> 57.2 us (level)
  waiting for transfers between devices: 8.2 us -> 7.33 us
    ppermute x8, waiting for transfers between devices: 5.59 us -> 4.72 us  [shift(): lax.ppermute(value, axis, [(i, (i + step) % count) for i in range(count)])]
    pallas_call x8 -> x9, Pallas kernels: 9.07 us -> 9.63 us  [call(): pl.pallas_call(kernel, out_shape=[jax.ShapeDtypeStruct(shape, dtype) for...]
  transfers between devices with their start and end apart: 14 -> 14, of which waited for: 7 -> 5; matrix products, arithmetic and copies ran while one was open for 2% -> 2% of each run, Pallas kernels for 4% -> 5%
where the time goes in v6:
time: 57.2 us; the launch traced here: 56.9 us
  starting transfers between devices  25.2 us (44%)
  blocking collectives  10.4 us (18%)
  Pallas kernels  9.63 us (17%)
  waiting for transfers between devices  7.33 us (13%)
  local copies, waits for them, and re-layouts  3.49 us (6%)
  between operations  0.84 us (1%)
    ppermute x8, starting transfers between devices, shift(): lax.ppermute(value, axis, [(i, (i + step) % count) for i in range(count)])  13.4 us
    all_to_all x1, blocking collectives, on_device(): lax.all_to_all(send.reshape(frames, tracks, width), ('x', 'zl'), 0, 0)  10.4 us
    pallas_call x9, Pallas kernels, call(): pl.pallas_call(kernel, out_shape=[jax.ShapeDtypeStruct(shape, dtype) for...  9.63 us
    ppermute x1, starting transfers between devices, on_device(): fetched = lax.ppermute(partial, ('zh', 'c'), split_pairs)  5.21 us
    ppermute x8, waiting for transfers between devices, shift(): lax.ppermute(value, axis, [(i, (i + step) % count) for i in range(count)])  4.72 us
    unnamed x28, local copies, waits for them, and re-layouts  3.38 us
    ppermute x3, starting transfers between devices, on_device(): pieces[k] = lax.ppermute(frame_out, ('x', 'zl', 'c'), pairs)  3.03 us
    ppermute x1, starting transfers between devices, on_device(): pieces[1] = lax.ppermute(frame_out, 'zl', [(0, 1), (1, 0)])  2.38 us
  transfers between devices with their start and end apart: 14, of which 5 were waited for; matrix products, arithmetic and copies ran while one was open for 2% of the time, Pallas kernels for 5%

profile of v6, /device:TPU:1, one launch (start us, length us, event | category | flops | bytes accessed | tf_op | source)
XLA Modules:
  0.0 56.9 jit_solution(6793472992580253654)
XLA Ops:
  0.6 0.0 copy-start
  0.6 0.0 copy-start.5
  0.7 3.8 %collective-permute-start = (bf16[256,384]{1,0:T(8,128)(2,1)}, bf16[256,384]{1,0:T(8,128)(2,1)S(1)}, u32[]{:S(2)}, u32[]{:S(2)}) collective-permute-start(bf16[256,384]{1,0:T(8,128)(2,1)} %bitcast.11), channel_id=1, source_target_pairs={{0,2},{1,3},{2,0},{3,1},{4,6},{5,7},{6,4},{7,5},{8,10},{9,11},{10,... | collective-permute-start | bytes 589832 | tf_op jit(solution)/shard_map/ppermute | solution.py:311
  4.5 0.8 %collective-permute-start.2 = (bf16[256,384]{1,0:T(8,128)(2,1)}, bf16[256,384]{1,0:T(8,128)(2,1)S(1)}, u32[]{:S(2)}, u32[]{:S(2)}) collective-permute-start(bf16[256,384]{1,0:T(8,128)(2,1)} %bitcast.12), channel_id=1, source_target_pairs={{0,3},{1,0},{2,1},{3,2},{4,7},{5,4},{6,5},{7,6},{8,11},{9,8},{10,9... | collective-permute-start | bytes 589832 | tf_op jit(solution)/shard_map/ppermute | solution.py:311
  5.3 0.7 %collective-permute-start.1 = (bf16[256,384]{1,0:T(8,128)(2,1)}, bf16[256,384]{1,0:T(8,128)(2,1)S(1)}, u32[]{:S(2)}, u32[]{:S(2)}) collective-permute-start(bf16[256,384]{1,0:T(8,128)(2,1)} %bitcast.13), channel_id=1, source_target_pairs={{0,1},{1,2},{2,3},{3,0},{4,5},{5,6},{6,7},{7,4},{8,9},{9,10},{10,1... | collective-permute-start | bytes 589832 | tf_op jit(solution)/shard_map/ppermute | solution.py:311
  6.0 0.8 %copy.17.refs_5_ = s32[32,8]{1,0:T(8,128)S(1)} copy(s32[32,8]{0,1:T(8,128)} %param.14) | data formatting | bytes 2048 | tf_op args[1]
  6.7 0.0 copy-done
  6.7 0.1 constant_dynamic-slice_fusion
  6.8 0.0 copy-done.5
  6.9 0.0 copy-start.1
  6.9 1.2 %copy-done.1 = bf16[384,1152]{1,0:T(8,128)(2,1)S(1)} copy-done((bf16[384,1152]{1,0:T(8,128)(2,1)S(1)}, bf16[384,1152]{1,0:T(8,128)(2,1)}, u32[]{:S(2)}) %copy-start.1) | copy-done | bytes 884760
  8.0 0.0 copy-start.8
  8.0 1.0 %copy-done.8 = bf16[384,384]{1,0:T(8,128)(2,1)S(1)} copy-done((bf16[384,384]{1,0:T(8,128)(2,1)S(1)}, bf16[384,384]{1,0:T(8,128)(2,1)}, u32[]{:S(2)}) %copy-start.8) | copy-done | bytes 294936
  9.0 0.0 copy-start.2
  9.0 0.7 %shard_map.140 = (bf16[256,1152]{1,0:T(8,128)(2,1)S(1)}, bf16[64,384]{1,0:T(8,128)(2,1)S(1)}) custom-call(bf16[256,384]{1,0:T(8,128)(2,1)S(1)} %bitcast.14, bf16[64,384]{1,0:T(8,128)(2,1)S(1)} %bitcast.16, bf16[384,1152]{1,0:T(8,128)(2,1)S(1)} %copy-done.1, bf16[384,384]{1,0:T(8,128)(2,1)S(1)} %copy-done.8), custom_call_target="tpu_custom_call" | custom-call | tf_op jit(solution)/shard_map/pallas_call | solution.py:302
  9.7 0.0 copy-start.9
  9.7 0.0 collective-permute-done.tokens_ref
  9.7 0.4 copy-done.2
  10.2 0.5 shard_map.141.refs_2_
  10.7 3.0 %collective-permute-done.2.refs_4_ = bf16[256,384]{1,0:T(8,128)(2,1)S(1)} collective-permute-done((bf16[256,384]{1,0:T(8,128)(2,1)}, bf16[256,384]{1,0:T(8,128)(2,1)S(1)}, u32[]{:S(2)}, u32[]{:S(2)}) %collective-permute-start.2) | collective-permute-done | bytes 196640 | tf_op jit(solution)/shard_map/ppermute | solution.py:311
  13.8 0.8 %collective-permute-done.1.refs_3_ = bf16[256,384]{1,0:T(8,128)(2,1)S(1)} collective-permute-done((bf16[256,384]{1,0:T(8,128)(2,1)}, bf16[256,384]{1,0:T(8,128)(2,1)S(1)}, u32[]{:S(2)}, u32[]{:S(2)}) %collective-permute-start.1) | collective-permute-done | bytes 196640 | tf_op jit(solution)/shard_map/ppermute | solution.py:311
  14.5 0.0 copy-done.9
  14.5 2.1 %shard_map.142 = (bf16[256,384]{1,0:T(8,128)(2,1)S(1)}, bf16[256,384]{1,0:T(8,128)(2,1)S(1)}, bf16[256,384]{1,0:T(8,128)(2,1)S(1)}) custom-call(bf16[256,384]{1,0:T(8,128)(2,1)S(1)} %bitcast.15, bf16[256,1152]{1,0:T(8,128)(2,1)S(1)} %get-tuple-element.12.refs_1_, bf16[256,768]{1,0:T(8,128)(2,1)S(1)} %shard_map.141.refs_2_, ...), custom_call_target="tpu_custom_call" | custom-call | tf_op jit(solution)/shard_map/pallas_call | solution.py:302
  16.6 0.0 copy-start.7
  16.6 10.4 %all_to_all.5 = bf16[8,32,384]{2,1,0:T(8,128)(2,1)S(1)} all-to-all(bf16[8,32,384]{2,1,0:T(8,128)(2,1)S(1)} %bitcast.18), channel_id=1, replica_groups=mesh['x'=4,'zh'=4,'zl'=2,'c'=2,'y'=4] {'x','zl'}, dimensions={0} | all-to-all | bytes 393216 | tf_op jit(solution)/shard_map/all_to_all | solution.py:335
  27.0 0.0 copy-done.6
  27.0 0.7 %shard_map.144.a_ref = bf16[64,512]{1,0:T(8,128)(2,1)S(1)} custom-call(bf16[256,384]{1,0:T(8,128)(2,1)S(1)} %bitcast.10, bf16[64,384]{1,0:T(8,128)(2,1)S(1)} %get-tuple-element.19.query_ref, bf16[384,768]{1,0:T(8,128)(2,1)S(1)} %copy-done.6), custom_call_target="tpu_custom_call" | custom-call | tf_op jit(solution)/shard_map/pallas_call | solution.py:302
  27.7 3.0 %collective-permute-start.3 = (bf16[64,512]{1,0:T(8,128)(2,1)S(1)}, bf16[64,512]{1,0:T(8,128)(2,1)S(1)}, u32[]{:S(2)}, u32[]{:S(2)}) collective-permute-start(bf16[64,512]{1,0:T(8,128)(2,1)S(1)} %shard_map.144.a_ref), channel_id=1, source_target_pairs={{0,4},{4,0},{1,5},{5,1},{2,6},{6,2},{3,7},{7,3},{8,12},{12,8},{9,1... | collective-permute-start | bytes 196616 | tf_op jit(solution)/shard_map/ppermute | solution.py:311
  30.7 0.9 %collective-permute-done.3.b_ref = bf16[64,512]{1,0:T(8,128)(2,1)S(1)} collective-permute-done((bf16[64,512]{1,0:T(8,128)(2,1)S(1)}, bf16[64,512]{1,0:T(8,128)(2,1)S(1)}, u32[]{:S(2)}, u32[]{:S(2)}) %collective-permute-start.3) | collective-permute-done | bytes 65568 | tf_op jit(solution)/shard_map/ppermute | solution.py:311
  31.6 0.3 shard_map.145.refs_1_
  31.9 0.0 copy-start.10
  31.9 5.2 %collective-permute-start.4 = (bf16[64,512]{1,0:T(8,128)(2,1)S(1)}, bf16[64,512]{1,0:T(8,128)(2,1)S(1)}, u32[]{:S(2)}, u32[]{:S(2)}) collective-permute-start(bf16[64,512]{1,0:T(8,128)(2,1)S(1)} %shard_map.145.refs_1_), channel_id=1, source_target_pairs={{0,32},{4,52},{16,48},{20,36},{32,0},{36,20},{48,16},{52,4},{1,33}... | collective-permute-start | bytes 196616 | tf_op jit(solution)/shard_map/ppermute | solution.py:343
  37.1 1.2 %collective-permute-start.6 = (bf16[64,512]{1,0:T(8,128)(2,1)S(1)}, bf16[64,512]{1,0:T(8,128)(2,1)S(1)}, u32[]{:S(2)}, u32[]{:S(2)}) collective-permute-start(bf16[64,512]{1,0:T(8,128)(2,1)S(1)} %shard_map.145.refs_1_), channel_id=1, source_target_pairs={{0,16},{16,0},{32,48},{48,32},{1,17},{17,1},{33,49},{49,33},{2,18}... | collective-permute-start | bytes 196616 | tf_op jit(solution)/shard_map/ppermute | solution.py:344
  38.3 0.7 %collective-permute-done.4.refs_2_ = bf16[64,512]{1,0:T(8,128)(2,1)S(1)} collective-permute-done((bf16[64,512]{1,0:T(8,128)(2,1)S(1)}, bf16[64,512]{1,0:T(8,128)(2,1)S(1)}, u32[]{:S(2)}, u32[]{:S(2)}) %collective-permute-start.4) | collective-permute-done | bytes 65568 | tf_op jit(solution)/shard_map/ppermute | solution.py:343
  39.0 2.3 %collective-permute-start.5 = (bf16[64,512]{1,0:T(8,128)(2,1)S(1)}, bf16[64,512]{1,0:T(8,128)(2,1)S(1)}, u32[]{:S(2)}, u32[]{:S(2)}) collective-permute-start(bf16[64,512]{1,0:T(8,128)(2,1)S(1)} %collective-permute-done.4.refs_2_), channel_id=1, source_target_pairs={{0,4},{4,0},{1,5},{5,1},{2,6},{6,2},{3,7},{7,3},{8,12},{12,8},{9,1... | collective-permute-start | bytes 196616 | tf_op jit(solution)/shard_map/ppermute | solution.py:311
  41.4 0.1 pad_add_fusion.place_ref
  41.4 0.0 copy-done.7
  41.4 0.8 %shard_map.143 = (bf16[256,384]{1,0:T(8,128)(2,1)S(1)}, bf16[128,128]{1,0:T(8,128)(2,1)S(1)}, bf16[256,256]{1,0:T(8,128)(2,1)S(1)}) custom-call(s32[2]{0:T(128)S(1)} %pad_add_fusion.place_ref, bf16[256,384]{1,0:T(8,128)(2,1)S(1)} %get-tuple-element.14.normed_ref, bf16[384,384]{1,0:T(8,128)(2,1)S(1)} %copy-done.7), custom_call_target="tpu_custom_call" | custom-call | tf_op jit(solution)/shard_map/pallas_call | solution.py:302
  42.3 1.9 %collective-permute-done.6.refs_4_ = bf16[64,512]{1,0:T(8,128)(2,1)S(1)} collective-permute-done((bf16[64,512]{1,0:T(8,128)(2,1)S(1)}, bf16[64,512]{1,0:T(8,128)(2,1)S(1)}, u32[]{:S(2)}, u32[]{:S(2)}) %collective-permute-start.6) | collective-permute-done | bytes 65568 | tf_op jit(solution)/shard_map/ppermute | solution.py:344
  44.1 0.0 collective-permute-done.5.refs_3_
  44.1 0.0 copy-done.4
  44.1 0.0 copy-done.11
  44.1 0.0 copy-done.10
  44.2 0.0 copy-start.3
  44.2 1.4 %shard_map.146.refs_0_ = bf16[64,384]{1,0:T(8,128)(2,1)S(1)} custom-call(bf16[256,384]{1,0:T(8,128)(2,1)S(1)} %get-tuple-element.15.refs_0_.query_ref, bf16[64,512]{1,0:T(8,128)(2,1)S(1)} %shard_map.145.refs_1_, bf16[64,512]{1,0:T(8,128)(2,1)S(1)} %collective-permute-done.4.refs_2_, bf16[64,512]{1,0:T(8,128)(2,1)S(1)} %collective-permute-done.5.refs_3_, ...), custom_call_target="tpu_custom_call" | custom-call | tf_op jit(solution)/shard_map/pallas_call | solution.py:302
  45.6 0.0 copy-start.12
  45.6 0.1 collective-permute-start.8
  45.7 2.9 %collective-permute-start.12 = (bf16[64,384]{1,0:T(8,128)(2,1)S(1)}, bf16[64,384]{1,0:T(8,128)(2,1)S(1)}, u32[]{:S(2)}, u32[]{:S(2)}) collective-permute-start(bf16[64,384]{1,0:T(8,128)(2,1)S(1)} %shard_map.146.refs_0_), channel_id=1, source_target_pairs={{0,128},{4,140},{8,136},{12,132},{64,192},{68,204},{72,200},{76,19... | collective-permute-start | bytes 147464 | tf_op jit(solution)/shard_map/ppermute | solution.py:352
  48.6 0.0 collective-permute-start.10
  48.6 2.4 %collective-permute-start.7 = (bf16[64,384]{1,0:T(8,128)(2,1)S(1)}, bf16[64,384]{1,0:T(8,128)(2,1)S(1)}, u32[]{:S(2)}, u32[]{:S(2)}) collective-permute-start(bf16[64,384]{1,0:T(8,128)(2,1)S(1)} %shard_map.146.refs_0_), channel_id=1, source_target_pairs={{0,8},{8,0},{1,9},{9,1},{2,10},{10,2},{3,11},{11,3},{4,12},{12,4},... | collective-permute-start | bytes 147464 | tf_op jit(solution)/shard_map/ppermute | solution.py:353
  51.0 0.0 collective-permute-done.8.refs_2_.refs_6_
  51.0 1.5 %collective-permute-start.9 = (bf16[64,384]{1,0:T(8,128)(2,1)S(1)}, bf16[64,384]{1,0:T(8,128)(2,1)S(1)}, u32[]{:S(2)}, u32[]{:S(2)}) collective-permute-start(bf16[64,384]{1,0:T(8,128)(2,1)S(1)} %collective-permute-done.8.refs_2_.refs_6_), channel_id=1, source_target_pairs={{0,4},{4,0},{1,5},{5,1},{2,6},{6,2},{3,7},{7,3},{8,12},{12,8},{9,1... | collective-permute-start | bytes 147464 | tf_op jit(solution)/shard_map/ppermute | solution.py:311
  52.4 0.0 collective-permute-done.12.refs_4_
  52.5 0.8 %collective-permute-start.13 = (bf16[64,384]{1,0:T(8,128)(2,1)S(1)}, bf16[64,384]{1,0:T(8,128)(2,1)S(1)}, u32[]{:S(2)}, u32[]{:S(2)}) collective-permute-start(bf16[64,384]{1,0:T(8,128)(2,1)S(1)} %collective-permute-done.12.refs_4_), channel_id=1, source_target_pairs={{0,4},{4,0},{1,5},{5,1},{2,6},{6,2},{3,7},{7,3},{8,12},{12,8},{9,1... | collective-permute-start | bytes 147464 | tf_op jit(solution)/shard_map/ppermute | solution.py:311
  53.2 0.0 collective-permute-done.10.refs_2_
  53.2 0.6 %collective-permute-start.11 = (bf16[64,384]{1,0:T(8,128)(2,1)S(1)}, bf16[64,384]{1,0:T(8,128)(2,1)S(1)}, u32[]{:S(2)}, u32[]{:S(2)}) collective-permute-start(bf16[64,384]{1,0:T(8,128)(2,1)S(1)} %collective-permute-done.10.refs_2_), channel_id=1, source_target_pairs={{0,4},{4,0},{1,5},{5,1},{2,6},{6,2},{3,7},{7,3},{8,12},{12,8},{9,1... | collective-permute-start | bytes 147464 | tf_op jit(solution)/shard_map/ppermute | solution.py:311
  53.8 0.0 collective-permute-done.7.refs_1_
  53.8 0.0 collective-permute-done.9.refs_3_.refs_7_
  53.8 0.0 copy-done.3
  53.8 1.0 %shard_map.147.front_ref = bf16[128,384]{1,0:T(8,128)(2,1)S(1)} custom-call(bf16[256,384]{1,0:T(8,128)(2,1)S(1)} %get-tuple-element.15.refs_0_.query_ref, bf16[64,384]{1,0:T(8,128)(2,1)S(1)} %shard_map.146.refs_0_, bf16[64,384]{1,0:T(8,128)(2,1)S(1)} %collective-permute-done.7.refs_1_, bf16[64,384]{1,0:T(8,128)(2,1)S(1)} %collective-permute-done.8.refs_2_.refs_6_, ...), custom_call_target="tpu_custom_call" | custom-call | tf_op jit(solution)/shard_map/pallas_call | solution.py:302
  54.8 0.0 collective-permute-done.13.refs_5_
  54.8 0.0 collective-permute-done.11.refs_3_
  54.8 0.0 copy-done.12
  54.8 2.1 %shard_map.148 = (bf16[256,384]{1,0:T(8,128)(2,1)}, bf16[512,384]{1,0:T(8,128)(2,1)}) custom-call(bf16[256,384]{1,0:T(8,128)(2,1)S(1)} %get-tuple-element.13.updated_ref, bf16[256,384]{1,0:T(8,128)(2,1)S(1)} %get-tuple-element.15.refs_0_.query_ref, bf16[128,128]{1,0:T(8,128)(2,1)S(1)} %get-tuple-element.16.swap_part_ref, ...), custom_call_target="tpu_custom_call" | custom-call | tf_op jit(solution)/shard_map/pallas_call | solution.py:302
  (4 shorter events, 0.0 us)
Async XLA Ops:
  0.6 6.1 %copy-start = (bf16[64,8,384]{2,1,0:T(8,128)(2,1)S(1)}, bf16[64,8,384]{2,1,0:T(8,128)(2,1)}, u32[]{:S(2)}) copy-start(bf16[64,8,384]{2,1,0:T(8,128)(2,1)} %param.15) | copy-start | bytes 1179652
  0.6 6.2 %copy-start.5 = (bf16[32,8,384]{2,1,0:T(8,128)(2,1)S(1)}, bf16[32,8,384]{2,1,0:T(8,128)(2,1)}, u32[]{:S(2)}) copy-start(bf16[32,8,384]{2,1,0:T(8,128)(2,1)} %param.13) | copy-start | bytes 589828
  0.7 9.1 %collective-permute-start = (bf16[256,384]{1,0:T(8,128)(2,1)}, bf16[256,384]{1,0:T(8,128)(2,1)S(1)}, u32[]{:S(2)}, u32[]{:S(2)}) collective-permute-start(bf16[256,384]{1,0:T(8,128)(2,1)} %bitcast.11), channel_id=1, source_target_pairs={{0,2},{1,3},{2,0},{3,1},{4,6},{5,7},{6,4},{7,5},{8,10},{9,11},{10,... | collective-permute-start | bytes 589832 | tf_op jit(solution)/shard_map/ppermute | solution.py:311
  4.5 9.3 %collective-permute-start.2 = (bf16[256,384]{1,0:T(8,128)(2,1)}, bf16[256,384]{1,0:T(8,128)(2,1)S(1)}, u32[]{:S(2)}, u32[]{:S(2)}) collective-permute-start(bf16[256,384]{1,0:T(8,128)(2,1)} %bitcast.12), channel_id=1, source_target_pairs={{0,3},{1,0},{2,1},{3,2},{4,7},{5,4},{6,5},{7,6},{8,11},{9,8},{10,9... | collective-permute-start | bytes 589832 | tf_op jit(solution)/shard_map/ppermute | solution.py:311
  5.3 9.2 %collective-permute-start.1 = (bf16[256,384]{1,0:T(8,128)(2,1)}, bf16[256,384]{1,0:T(8,128)(2,1)S(1)}, u32[]{:S(2)}, u32[]{:S(2)}) collective-permute-start(bf16[256,384]{1,0:T(8,128)(2,1)} %bitcast.13), channel_id=1, source_target_pairs={{0,1},{1,2},{2,3},{3,0},{4,5},{5,6},{6,7},{7,4},{8,9},{9,10},{10,1... | collective-permute-start | bytes 589832 | tf_op jit(solution)/shard_map/ppermute | solution.py:311
  6.9 1.2 %copy-start.1 = (bf16[384,1152]{1,0:T(8,128)(2,1)S(1)}, bf16[384,1152]{1,0:T(8,128)(2,1)}, u32[]{:S(2)}) copy-start(bf16[384,1152]{1,0:T(8,128)(2,1)} %refs_6_.2) | copy-start | bytes 2654212
  8.0 1.0 %copy-start.8 = (bf16[384,384]{1,0:T(8,128)(2,1)S(1)}, bf16[384,384]{1,0:T(8,128)(2,1)}, u32[]{:S(2)}) copy-start(bf16[384,384]{1,0:T(8,128)(2,1)} %virt_q_ref.1) | copy-start | bytes 884740
  9.0 1.2 %copy-start.2 = (bf16[384,1152]{1,0:T(8,128)(2,1)S(1)}, bf16[384,1152]{1,0:T(8,128)(2,1)}, u32[]{:S(2)}) copy-start(bf16[384,1152]{1,0:T(8,128)(2,1)} %refs_6_.2) | copy-start | bytes 2654212
  9.7 4.8 %copy-start.9 = (bf16[384,384]{1,0:T(8,128)(2,1)S(1)}, bf16[384,384]{1,0:T(8,128)(2,1)}, u32[]{:S(2)}) copy-start(bf16[384,384]{1,0:T(8,128)(2,1)} %refs_7_.2) | copy-start | bytes 884740
  14.5 12.5 %copy-start.6 = (bf16[384,768]{1,0:T(8,128)(2,1)S(1)}, bf16[384,768]{1,0:T(8,128)(2,1)}, u32[]{:S(2)}) copy-start(bf16[384,768]{1,0:T(8,128)(2,1)} %virt_kv_ref.1) | copy-start | bytes 1769476
  16.6 24.9 %copy-start.7 = (bf16[384,384]{1,0:T(8,128)(2,1)S(1)}, bf16[384,384]{1,0:T(8,128)(2,1)}, u32[]{:S(2)}) copy-start(bf16[384,384]{1,0:T(8,128)(2,1)} %back_q_ref.1) | copy-start | bytes 884740
  27.0 17.2 %copy-start.4 = (bf16[384,1152]{1,0:T(8,128)(2,1)S(1)}, bf16[384,1152]{1,0:T(8,128)(2,1)}, u32[]{:S(2)}) copy-start(bf16[384,1152]{1,0:T(8,128)(2,1)} %refs_7_.3) | copy-start | bytes 2654212
  27.7 3.9 %collective-permute-start.3 = (bf16[64,512]{1,0:T(8,128)(2,1)S(1)}, bf16[64,512]{1,0:T(8,128)(2,1)S(1)}, u32[]{:S(2)}, u32[]{:S(2)}) collective-permute-start(bf16[64,512]{1,0:T(8,128)(2,1)S(1)} %shard_map.144.a_ref), channel_id=1, source_target_pairs={{0,4},{4,0},{1,5},{5,1},{2,6},{6,2},{3,7},{7,3},{8,12},{12,8},{9,1... | collective-permute-start | bytes 196616 | tf_op jit(solution)/shard_map/ppermute | solution.py:311
  31.6 12.5 %copy-start.11 = (bf16[384,384]{1,0:T(8,128)(2,1)S(1)}, bf16[384,384]{1,0:T(8,128)(2,1)}, u32[]{:S(2)}) copy-start(bf16[384,384]{1,0:T(8,128)(2,1)} %refs_8_.2) | copy-start | bytes 884740
  31.9 12.2 %copy-start.10 = (bf16[384,384]{1,0:T(8,128)(2,1)S(1)}, bf16[384,384]{1,0:T(8,128)(2,1)}, u32[]{:S(2)}) copy-start(bf16[384,384]{1,0:T(8,128)(2,1)} %refs_6_.3) | copy-start | bytes 884740
  31.9 7.1 %collective-permute-start.4 = (bf16[64,512]{1,0:T(8,128)(2,1)S(1)}, bf16[64,512]{1,0:T(8,128)(2,1)S(1)}, u32[]{:S(2)}, u32[]{:S(2)}) collective-permute-start(bf16[64,512]{1,0:T(8,128)(2,1)S(1)} %shard_map.145.refs_1_), channel_id=1, source_target_pairs={{0,32},{4,52},{16,48},{20,36},{32,0},{36,20},{48,16},{52,4},{1,33}... | collective-permute-start | bytes 196616 | tf_op jit(solution)/shard_map/ppermute | solution.py:343
  37.1 7.0 %collective-permute-start.6 = (bf16[64,512]{1,0:T(8,128)(2,1)S(1)}, bf16[64,512]{1,0:T(8,128)(2,1)S(1)}, u32[]{:S(2)}, u32[]{:S(2)}) collective-permute-start(bf16[64,512]{1,0:T(8,128)(2,1)S(1)} %shard_map.145.refs_1_), channel_id=1, source_target_pairs={{0,16},{16,0},{32,48},{48,32},{1,17},{17,1},{33,49},{49,33},{2,18}... | collective-permute-start | bytes 196616 | tf_op jit(solution)/shard_map/ppermute | solution.py:344
  39.0 5.1 %collective-permute-start.5 = (bf16[64,512]{1,0:T(8,128)(2,1)S(1)}, bf16[64,512]{1,0:T(8,128)(2,1)S(1)}, u32[]{:S(2)}, u32[]{:S(2)}) collective-permute-start(bf16[64,512]{1,0:T(8,128)(2,1)S(1)} %collective-permute-done.4.refs_2_), channel_id=1, source_target_pairs={{0,4},{4,0},{1,5},{5,1},{2,6},{6,2},{3,7},{7,3},{8,12},{12,8},{9,1... | collective-permute-start | bytes 196616 | tf_op jit(solution)/shard_map/ppermute | solution.py:311
  44.2 9.7 %copy-start.3 = (bf16[384,768]{1,0:T(8,128)(2,1)S(1)}, bf16[384,768]{1,0:T(8,128)(2,1)}, u32[]{:S(2)}) copy-start(bf16[384,768]{1,0:T(8,128)(2,1)} %refs_8_.3) | copy-start | bytes 1769476
  45.6 9.3 %copy-start.12 = (bf16[384,384]{1,0:T(8,128)(2,1)S(1)}, bf16[384,384]{1,0:T(8,128)(2,1)}, u32[]{:S(2)}) copy-start(bf16[384,384]{1,0:T(8,128)(2,1)} %refs_9_.1) | copy-start | bytes 884740
  45.6 5.4 %collective-permute-start.8 = (bf16[64,384]{1,0:T(8,128)(2,1)S(1)}, bf16[64,384]{1,0:T(8,128)(2,1)S(1)}, u32[]{:S(2)}, u32[]{:S(2)}) collective-permute-start(bf16[64,384]{1,0:T(8,128)(2,1)S(1)} %shard_map.146.refs_0_), channel_id=1, source_target_pairs={{0,192},{4,204},{8,200},{12,196},{64,128},{68,140},{72,136},{76,13... | collective-permute-start | bytes 147464 | tf_op jit(solution)/shard_map/ppermute | solution.py:352
  45.7 6.8 %collective-permute-start.12 = (bf16[64,384]{1,0:T(8,128)(2,1)S(1)}, bf16[64,384]{1,0:T(8,128)(2,1)S(1)}, u32[]{:S(2)}, u32[]{:S(2)}) collective-permute-start(bf16[64,384]{1,0:T(8,128)(2,1)S(1)} %shard_map.146.refs_0_), channel_id=1, source_target_pairs={{0,128},{4,140},{8,136},{12,132},{64,192},{68,204},{72,200},{76,19... | collective-permute-start | bytes 147464 | tf_op jit(solution)/shard_map/ppermute | solution.py:352
  48.6 4.6 %collective-permute-start.10 = (bf16[64,384]{1,0:T(8,128)(2,1)S(1)}, bf16[64,384]{1,0:T(8,128)(2,1)S(1)}, u32[]{:S(2)}, u32[]{:S(2)}) collective-permute-start(bf16[64,384]{1,0:T(8,128)(2,1)S(1)} %shard_map.146.refs_0_), channel_id=1, source_target_pairs={{0,64},{4,76},{8,72},{12,68},{64,0},{68,12},{72,8},{76,4},{128,192... | collective-permute-start | bytes 147464 | tf_op jit(solution)/shard_map/ppermute | solution.py:352
  48.6 5.2 %collective-permute-start.7 = (bf16[64,384]{1,0:T(8,128)(2,1)S(1)}, bf16[64,384]{1,0:T(8,128)(2,1)S(1)}, u32[]{:S(2)}, u32[]{:S(2)}) collective-permute-start(bf16[64,384]{1,0:T(8,128)(2,1)S(1)} %shard_map.146.refs_0_), channel_id=1, source_target_pairs={{0,8},{8,0},{1,9},{9,1},{2,10},{10,2},{3,11},{11,3},{4,12},{12,4},... | collective-permute-start | bytes 147464 | tf_op jit(solution)/shard_map/ppermute | solution.py:353
  51.0 2.8 %collective-permute-start.9 = (bf16[64,384]{1,0:T(8,128)(2,1)S(1)}, bf16[64,384]{1,0:T(8,128)(2,1)S(1)}, u32[]{:S(2)}, u32[]{:S(2)}) collective-permute-start(bf16[64,384]{1,0:T(8,128)(2,1)S(1)} %collective-permute-done.8.refs_2_.refs_6_), channel_id=1, source_target_pairs={{0,4},{4,0},{1,5},{5,1},{2,6},{6,2},{3,7},{7,3},{8,12},{12,8},{9,1... | collective-permute-start | bytes 147464 | tf_op jit(solution)/shard_map/ppermute | solution.py:311
  52.5 2.3 %collective-permute-start.13 = (bf16[64,384]{1,0:T(8,128)(2,1)S(1)}, bf16[64,384]{1,0:T(8,128)(2,1)S(1)}, u32[]{:S(2)}, u32[]{:S(2)}) collective-permute-start(bf16[64,384]{1,0:T(8,128)(2,1)S(1)} %collective-permute-done.12.refs_4_), channel_id=1, source_target_pairs={{0,4},{4,0},{1,5},{5,1},{2,6},{6,2},{3,7},{7,3},{8,12},{12,8},{9,1... | collective-permute-start | bytes 147464 | tf_op jit(solution)/shard_map/ppermute | solution.py:311
  53.2 1.6 %collective-permute-start.11 = (bf16[64,384]{1,0:T(8,128)(2,1)S(1)}, bf16[64,384]{1,0:T(8,128)(2,1)S(1)}, u32[]{:S(2)}, u32[]{:S(2)}) collective-permute-start(bf16[64,384]{1,0:T(8,128)(2,1)S(1)} %collective-permute-done.10.refs_2_), channel_id=1, source_target_pairs={{0,4},{4,0},{1,5},{5,1},{2,6},{6,2},{3,7},{7,3},{8,12},{12,8},{9,1... | collective-permute-start | bytes 147464 | tf_op jit(solution)/shard_map/ppermute | solution.py:311

commit v7 on v6

--- a/solution.py
+++ b/solution.py
@@ -100,7 +100,17 @@
     return jnp.where(col == source, 1.0, 0.0).astype(BF)
 
 
-def own_kernel(tokens_ref, virtual_ref, time_qkv_ref, virt_q_ref, qkv_ref, query_ref):
+def own_kernel(
+    tokens_ref, virtual_ref, visible_ref, time_qkv_ref, virt_q_ref, qkv_ref, query_ref, by_frame_ref, seen_ref
+):
+    rows = tokens_ref.shape[0]
+    tracks, frames = visible_ref.shape
+    by_frame_ref[...] = swap_matrix(frames, tracks)
+    pick = jnp.where((iota((rows, tracks), 0) & (tracks - 1)) == iota((rows, tracks), 1), 1.0, 0.0).astype(BF)
+    spread = matmul(pick, visible_ref[...].astype(F32).astype(BF))
+    here = iota((rows, frames), 0) // tracks == iota((rows, frames), 1)
+    seen = jnp.sum(jnp.where(here, spread, 0.0), -1, keepdims=True)
+    seen_ref[...] = jnp.broadcast_to(seen, seen_ref.shape)
     qkv_ref[...] = matmul(normalize(tokens_ref[...]), time_qkv_ref[...]).astype(BF)
     query_ref[...] = matmul(normalize(virtual_ref[...]), virt_q_ref[...]).astype(BF)
 
@@ -114,9 +124,8 @@
     frames, group, early, tokens_ref, qkv_ref, *refs
 ):
     piece_refs = refs[:3]
-    visible_ref, time_qkv_ref, time_out_ref, updated_ref, send_ref, normed_ref = refs[3:]
+    by_frame_ref, seen_ref, time_qkv_ref, time_out_ref, updated_ref, send_ref, normed_ref = refs[3:]
     rows, width = tokens_ref.shape
-    tracks = rows // frames
     size = group * frames
     pairs = [qkv_ref[:, width:]] + [ref[...] for ref in piece_refs[:early]]
     pairs += [matmul(normalize(ref[...]), time_qkv_ref[:, width:]).astype(BF) for ref in piece_refs[early:]]
@@ -131,11 +140,8 @@
     mixed = jnp.concatenate(attend(items, width), axis=0)
     updated = (tokens_ref[...].astype(F32) + matmul(mixed, time_out_ref[...])).astype(BF)
     updated_ref[...] = updated
-    normed = matmul(swap_matrix(frames, tracks), normalize(updated))
-    pick = jnp.where((iota((rows, tracks), 0) & (tracks - 1)) == iota((rows, tracks), 1), 1.0, 0.0).astype(BF)
-    spread = matmul(pick, visible_ref[...].astype(F32).astype(BF))
-    here = iota((rows, frames), 0) // tracks == iota((rows, frames), 1)
-    seen = jnp.sum(jnp.where(here, spread, 0.0), -1, keepdims=True) > 0.5
+    normed = matmul(by_frame_ref[...], normalize(updated))
+    seen = seen_ref[:, :1] > 0.5
     send_ref[...] = jnp.where(seen, normed, MARK).astype(BF)
     normed_ref[...] = normed.astype(BF)
 
@@ -322,15 +328,17 @@
     others = [shift(flat, "y", 4, step) for step in STEPS]
     frame = lax.axis_index("x") * 2 + lax.axis_index("zl")
     mine = lax.dynamic_slice_in_dim(virtual, frame, 1, axis=1).reshape(count, width)
-    qkv, virt_query = call(
-        own_kernel, [((rows, 3 * width), BF), ((count, width), BF)], flat, mine, time_qkv, virt_q
+    qkv, virt_query, by_frame, seen = call(
+        own_kernel,
+        [((rows, 3 * width), BF), ((count, width), BF), ((rows, rows), BF), ((rows, 128), F32)],
+        flat, mine, visible, time_qkv, virt_q,
     )
     for k in range(EARLY):
         (others[k],) = call(pair_kernel, [((rows, 2 * width), BF)], others[k], time_qkv)
     updated, send, normed = call(
         lambda *refs: time_kernel(frames, GROUP, EARLY, *refs),
         [((rows, width), BF)] * 3,
-        flat, qkv, *others, visible, time_qkv, time_out,
+        flat, qkv, *others, by_frame, seen, time_qkv, time_out,
     )
     got = lax.all_to_all(send.reshape(frames, tracks, width), ("x", "zl"), 0, 0).reshape(rows, width)
     (partial,) = call(partial_kernel, [((count, width + 128), BF)], got, virt_query, virt_kv)

time: 57.2 us -> 57 us (level)
  no operation moved by 1% of the time
where the time goes in v7:
time: 57 us; the launch traced here: 56.8 us
  starting transfers between devices  25.2 us (44%)
  blocking collectives  10.4 us (18%)
  Pallas kernels  9.48 us (17%)
  waiting for transfers between devices  7.33 us (13%)
  local copies, waits for them, and re-layouts  3.49 us (6%)
  between operations  0.85 us (1%)
    ppermute x8, starting transfers between devices, shift(): lax.ppermute(value, axis, [(i, (i + step) % count) for i in range(count)])  13.4 us
    all_to_all x1, blocking collectives, on_device(): lax.all_to_all(send.reshape(frames, tracks, width), ('x', 'zl'), 0, 0)  10.4 us
    pallas_call x9, Pallas kernels, call(): pl.pallas_call(kernel, out_shape=[jax.ShapeDtypeStruct(shape, dtype) for...  9.48 us
    ppermute x1, starting transfers between devices, on_device(): fetched = lax.ppermute(partial, ('zh', 'c'), split_pairs)  5.21 us
    ppermute x8, waiting for transfers between devices, shift(): lax.ppermute(value, axis, [(i, (i + step) % count) for i in range(count)])  4.72 us
    unnamed x28, local copies, waits for them, and re-layouts  3.38 us
    ppermute x3, starting transfers between devices, on_device(): pieces[k] = lax.ppermute(frame_out, ('x', 'zl', 'c'), pairs)  3.03 us
    ppermute x1, starting transfers between devices, on_device(): pieces[1] = lax.ppermute(frame_out, 'zl', [(0, 1), (1, 0)])  2.38 us
  transfers between devices with their start and end apart: 14, of which 5 were waited for; matrix products, arithmetic and copies ran while one was open for 2% of the time, Pallas kernels for 5%

profile of v7, /device:TPU:1, one launch (start us, length us, event | category | flops | bytes accessed | tf_op | source)
XLA Modules:
  0.0 56.8 jit_solution(2749751152906450819)
XLA Ops:
  0.6 0.0 copy-start
  0.6 0.0 copy-start.5
  0.7 3.8 %collective-permute-start = (bf16[256,384]{1,0:T(8,128)(2,1)}, bf16[256,384]{1,0:T(8,128)(2,1)S(1)}, u32[]{:S(2)}, u32[]{:S(2)}) collective-permute-start(bf16[256,384]{1,0:T(8,128)(2,1)} %bitcast.11), channel_id=1, source_target_pairs={{0,2},{1,3},{2,0},{3,1},{4,6},{5,7},{6,4},{7,5},{8,10},{9,11},{10,... | collective-permute-start | bytes 589832 | tf_op jit(solution)/shard_map/ppermute | solution.py:317
  4.5 0.8 %collective-permute-start.2 = (bf16[256,384]{1,0:T(8,128)(2,1)}, bf16[256,384]{1,0:T(8,128)(2,1)S(1)}, u32[]{:S(2)}, u32[]{:S(2)}) collective-permute-start(bf16[256,384]{1,0:T(8,128)(2,1)} %bitcast.12), channel_id=1, source_target_pairs={{0,3},{1,0},{2,1},{3,2},{4,7},{5,4},{6,5},{7,6},{8,11},{9,8},{10,9... | collective-permute-start | bytes 589832 | tf_op jit(solution)/shard_map/ppermute | solution.py:317
  5.3 0.7 %collective-permute-start.1 = (bf16[256,384]{1,0:T(8,128)(2,1)}, bf16[256,384]{1,0:T(8,128)(2,1)S(1)}, u32[]{:S(2)}, u32[]{:S(2)}) collective-permute-start(bf16[256,384]{1,0:T(8,128)(2,1)} %bitcast.13), channel_id=1, source_target_pairs={{0,1},{1,2},{2,3},{3,0},{4,5},{5,6},{6,7},{7,4},{8,9},{9,10},{10,1... | collective-permute-start | bytes 589832 | tf_op jit(solution)/shard_map/ppermute | solution.py:317
  6.0 0.8 %copy.17.visible_ref = s32[32,8]{1,0:T(8,128)S(1)} copy(s32[32,8]{0,1:T(8,128)} %param.14) | data formatting | bytes 2048 | tf_op args[1]
  6.7 0.0 copy-done
  6.7 0.1 constant_dynamic-slice_fusion
  6.8 0.0 copy-done.5
  6.9 0.0 copy-start.1
  6.9 1.2 %copy-done.1 = bf16[384,1152]{1,0:T(8,128)(2,1)S(1)} copy-done((bf16[384,1152]{1,0:T(8,128)(2,1)S(1)}, bf16[384,1152]{1,0:T(8,128)(2,1)}, u32[]{:S(2)}) %copy-start.1) | copy-done | bytes 884760
  8.0 0.0 copy-start.9
  8.0 1.0 %copy-done.9 = bf16[384,384]{1,0:T(8,128)(2,1)S(1)} copy-done((bf16[384,384]{1,0:T(8,128)(2,1)S(1)}, bf16[384,384]{1,0:T(8,128)(2,1)}, u32[]{:S(2)}) %copy-start.9) | copy-done | bytes 294936
  9.0 0.0 copy-start.2
  9.0 0.7 %shard_map.140 = (bf16[256,1152]{1,0:T(8,128)(2,1)S(1)}, bf16[64,384]{1,0:T(8,128)(2,1)S(1)}, bf16[256,256]{1,0:T(8,128)(2,1)S(1)}, f32[256,128]{1,0:T(8,128)S(1)}) custom-call(bf16[256,384]{1,0:T(8,128)(2,1)S(1)} %bitcast.14, bf16[64,384]{1,0:T(8,128)(2,1)S(1)} %bitcast.16, s32[32,8]{1,0:T(8,128)S(1)} %copy.17.visible_ref, bf16[384,1152]{1,0:T(8,128)(2,1)S(1)} %copy-done.1, ...), custom_call_target="tpu_custom_call" | custom-call | tf_op jit(solution)/shard_map/pallas_call | solution.py:308
  9.7 0.0 copy-start.7
  9.7 0.0 collective-permute-done.tokens_ref
  9.7 0.4 copy-done.2
  10.2 0.5 shard_map.141.refs_2_
  10.7 3.0 %collective-permute-done.2.refs_4_ = bf16[256,384]{1,0:T(8,128)(2,1)S(1)} collective-permute-done((bf16[256,384]{1,0:T(8,128)(2,1)}, bf16[256,384]{1,0:T(8,128)(2,1)S(1)}, u32[]{:S(2)}, u32[]{:S(2)}) %collective-permute-start.2) | collective-permute-done | bytes 196640 | tf_op jit(solution)/shard_map/ppermute | solution.py:317
  13.8 0.8 %collective-permute-done.1.refs_3_ = bf16[256,384]{1,0:T(8,128)(2,1)S(1)} collective-permute-done((bf16[256,384]{1,0:T(8,128)(2,1)}, bf16[256,384]{1,0:T(8,128)(2,1)S(1)}, u32[]{:S(2)}, u32[]{:S(2)}) %collective-permute-start.1) | collective-permute-done | bytes 196640 | tf_op jit(solution)/shard_map/ppermute | solution.py:317
  14.5 0.0 copy-done.7
  14.5 1.9 %shard_map.142 = (bf16[256,384]{1,0:T(8,128)(2,1)S(1)}, bf16[256,384]{1,0:T(8,128)(2,1)S(1)}, bf16[256,384]{1,0:T(8,128)(2,1)S(1)}) custom-call(bf16[256,384]{1,0:T(8,128)(2,1)S(1)} %bitcast.15, bf16[256,1152]{1,0:T(8,128)(2,1)S(1)} %get-tuple-element.14.refs_1_, bf16[256,768]{1,0:T(8,128)(2,1)S(1)} %shard_map.141.refs_2_, ...), custom_call_target="tpu_custom_call" | custom-call | tf_op jit(solution)/shard_map/pallas_call | solution.py:308
  16.4 0.0 copy-start.8
  16.4 10.4 %all_to_all.5 = bf16[8,32,384]{2,1,0:T(8,128)(2,1)S(1)} all-to-all(bf16[8,32,384]{2,1,0:T(8,128)(2,1)S(1)} %bitcast.18), channel_id=1, replica_groups=mesh['x'=4,'zh'=4,'zl'=2,'c'=2,'y'=4] {'x','zl'}, dimensions={0} | all-to-all | bytes 393216 | tf_op jit(solution)/shard_map/all_to_all | solution.py:343
  26.8 0.0 copy-done.6
  26.8 0.7 %shard_map.144.a_ref = bf16[64,512]{1,0:T(8,128)(2,1)S(1)} custom-call(bf16[256,384]{1,0:T(8,128)(2,1)S(1)} %bitcast.10, bf16[64,384]{1,0:T(8,128)(2,1)S(1)} %get-tuple-element.23.query_ref, bf16[384,768]{1,0:T(8,128)(2,1)S(1)} %copy-done.6), custom_call_target="tpu_custom_call" | custom-call | tf_op jit(solution)/shard_map/pallas_call | solution.py:308
  27.6 3.0 %collective-permute-start.3 = (bf16[64,512]{1,0:T(8,128)(2,1)S(1)}, bf16[64,512]{1,0:T(8,128)(2,1)S(1)}, u32[]{:S(2)}, u32[]{:S(2)}) collective-permute-start(bf16[64,512]{1,0:T(8,128)(2,1)S(1)} %shard_map.144.a_ref), channel_id=1, source_target_pairs={{0,4},{4,0},{1,5},{5,1},{2,6},{6,2},{3,7},{7,3},{8,12},{12,8},{9,1... | collective-permute-start | bytes 196616 | tf_op jit(solution)/shard_map/ppermute | solution.py:317
  30.5 0.9 %collective-permute-done.3.b_ref = bf16[64,512]{1,0:T(8,128)(2,1)S(1)} collective-permute-done((bf16[64,512]{1,0:T(8,128)(2,1)S(1)}, bf16[64,512]{1,0:T(8,128)(2,1)S(1)}, u32[]{:S(2)}, u32[]{:S(2)}) %collective-permute-start.3) | collective-permute-done | bytes 65568 | tf_op jit(solution)/shard_map/ppermute | solution.py:317
  31.4 0.3 shard_map.145.refs_1_
  31.8 0.0 copy-start.10
  31.8 5.2 %collective-permute-start.4 = (bf16[64,512]{1,0:T(8,128)(2,1)S(1)}, bf16[64,512]{1,0:T(8,128)(2,1)S(1)}, u32[]{:S(2)}, u32[]{:S(2)}) collective-permute-start(bf16[64,512]{1,0:T(8,128)(2,1)S(1)} %shard_map.145.refs_1_), channel_id=1, source_target_pairs={{0,32},{4,52},{16,48},{20,36},{32,0},{36,20},{48,16},{52,4},{1,33}... | collective-permute-start | bytes 196616 | tf_op jit(solution)/shard_map/ppermute | solution.py:351
  37.0 1.2 %collective-permute-start.6 = (bf16[64,512]{1,0:T(8,128)(2,1)S(1)}, bf16[64,512]{1,0:T(8,128)(2,1)S(1)}, u32[]{:S(2)}, u32[]{:S(2)}) collective-permute-start(bf16[64,512]{1,0:T(8,128)(2,1)S(1)} %shard_map.145.refs_1_), channel_id=1, source_target_pairs={{0,16},{16,0},{32,48},{48,32},{1,17},{17,1},{33,49},{49,33},{2,18}... | collective-permute-start | bytes 196616 | tf_op jit(solution)/shard_map/ppermute | solution.py:352
  38.2 0.7 %collective-permute-done.4.refs_2_ = bf16[64,512]{1,0:T(8,128)(2,1)S(1)} collective-permute-done((bf16[64,512]{1,0:T(8,128)(2,1)S(1)}, bf16[64,512]{1,0:T(8,128)(2,1)S(1)}, u32[]{:S(2)}, u32[]{:S(2)}) %collective-permute-start.4) | collective-permute-done | bytes 65568 | tf_op jit(solution)/shard_map/ppermute | solution.py:351
  38.9 2.3 %collective-permute-start.5 = (bf16[64,512]{1,0:T(8,128)(2,1)S(1)}, bf16[64,512]{1,0:T(8,128)(2,1)S(1)}, u32[]{:S(2)}, u32[]{:S(2)}) collective-permute-start(bf16[64,512]{1,0:T(8,128)(2,1)S(1)} %collective-permute-done.4.refs_2_), channel_id=1, source_target_pairs={{0,4},{4,0},{1,5},{5,1},{2,6},{6,2},{3,7},{7,3},{8,12},{12,8},{9,1... | collective-permute-start | bytes 196616 | tf_op jit(solution)/shard_map/ppermute | solution.py:317
  41.2 0.1 pad_add_fusion.place_ref
  41.3 0.0 copy-done.8
  41.3 0.8 %shard_map.143 = (bf16[256,384]{1,0:T(8,128)(2,1)S(1)}, bf16[128,128]{1,0:T(8,128)(2,1)S(1)}, bf16[256,256]{1,0:T(8,128)(2,1)S(1)}) custom-call(s32[2]{0:T(128)S(1)} %pad_add_fusion.place_ref, bf16[256,384]{1,0:T(8,128)(2,1)S(1)} %get-tuple-element.18.normed_ref, bf16[384,384]{1,0:T(8,128)(2,1)S(1)} %copy-done.8), custom_call_target="tpu_custom_call" | custom-call | tf_op jit(solution)/shard_map/pallas_call | solution.py:308
  42.1 1.9 %collective-permute-done.6.refs_4_ = bf16[64,512]{1,0:T(8,128)(2,1)S(1)} collective-permute-done((bf16[64,512]{1,0:T(8,128)(2,1)S(1)}, bf16[64,512]{1,0:T(8,128)(2,1)S(1)}, u32[]{:S(2)}, u32[]{:S(2)}) %collective-permute-start.6) | collective-permute-done | bytes 65568 | tf_op jit(solution)/shard_map/ppermute | solution.py:352
  44.0 0.0 collective-permute-done.5.refs_3_
  44.0 0.0 copy-done.4
  44.0 0.0 copy-done.11
  44.0 0.0 copy-done.10
  44.0 0.0 copy-start.3
  44.0 1.4 %shard_map.146.refs_0_ = bf16[64,384]{1,0:T(8,128)(2,1)S(1)} custom-call(bf16[256,384]{1,0:T(8,128)(2,1)S(1)} %get-tuple-element.19.refs_0_.query_ref, bf16[64,512]{1,0:T(8,128)(2,1)S(1)} %shard_map.145.refs_1_, bf16[64,512]{1,0:T(8,128)(2,1)S(1)} %collective-permute-done.4.refs_2_, bf16[64,512]{1,0:T(8,128)(2,1)S(1)} %collective-permute-done.5.refs_3_, ...), custom_call_target="tpu_custom_call" | custom-call | tf_op jit(solution)/shard_map/pallas_call | solution.py:308
  45.4 0.0 copy-start.12
  45.4 0.1 collective-permute-start.8
  45.5 2.9 %collective-permute-start.12 = (bf16[64,384]{1,0:T(8,128)(2,1)S(1)}, bf16[64,384]{1,0:T(8,128)(2,1)S(1)}, u32[]{:S(2)}, u32[]{:S(2)}) collective-permute-start(bf16[64,384]{1,0:T(8,128)(2,1)S(1)} %shard_map.146.refs_0_), channel_id=1, source_target_pairs={{0,128},{4,140},{8,136},{12,132},{64,192},{68,204},{72,200},{76,19... | collective-permute-start | bytes 147464 | tf_op jit(solution)/shard_map/ppermute | solution.py:360
  48.5 0.0 collective-permute-start.10
  48.5 2.4 %collective-permute-start.7 = (bf16[64,384]{1,0:T(8,128)(2,1)S(1)}, bf16[64,384]{1,0:T(8,128)(2,1)S(1)}, u32[]{:S(2)}, u32[]{:S(2)}) collective-permute-start(bf16[64,384]{1,0:T(8,128)(2,1)S(1)} %shard_map.146.refs_0_), channel_id=1, source_target_pairs={{0,8},{8,0},{1,9},{9,1},{2,10},{10,2},{3,11},{11,3},{4,12},{12,4},... | collective-permute-start | bytes 147464 | tf_op jit(solution)/shard_map/ppermute | solution.py:361
  50.8 0.0 collective-permute-done.8.refs_2_.refs_6_
  50.8 1.5 %collective-permute-start.9 = (bf16[64,384]{1,0:T(8,128)(2,1)S(1)}, bf16[64,384]{1,0:T(8,128)(2,1)S(1)}, u32[]{:S(2)}, u32[]{:S(2)}) collective-permute-start(bf16[64,384]{1,0:T(8,128)(2,1)S(1)} %collective-permute-done.8.refs_2_.refs_6_), channel_id=1, source_target_pairs={{0,4},{4,0},{1,5},{5,1},{2,6},{6,2},{3,7},{7,3},{8,12},{12,8},{9,1... | collective-permute-start | bytes 147464 | tf_op jit(solution)/shard_map/ppermute | solution.py:317
  52.3 0.0 collective-permute-done.12.refs_4_
  52.3 0.8 %collective-permute-start.13 = (bf16[64,384]{1,0:T(8,128)(2,1)S(1)}, bf16[64,384]{1,0:T(8,128)(2,1)S(1)}, u32[]{:S(2)}, u32[]{:S(2)}) collective-permute-start(bf16[64,384]{1,0:T(8,128)(2,1)S(1)} %collective-permute-done.12.refs_4_), channel_id=1, source_target_pairs={{0,4},{4,0},{1,5},{5,1},{2,6},{6,2},{3,7},{7,3},{8,12},{12,8},{9,1... | collective-permute-start | bytes 147464 | tf_op jit(solution)/shard_map/ppermute | solution.py:317
  53.1 0.0 collective-permute-done.10.refs_2_
  53.1 0.6 %collective-permute-start.11 = (bf16[64,384]{1,0:T(8,128)(2,1)S(1)}, bf16[64,384]{1,0:T(8,128)(2,1)S(1)}, u32[]{:S(2)}, u32[]{:S(2)}) collective-permute-start(bf16[64,384]{1,0:T(8,128)(2,1)S(1)} %collective-permute-done.10.refs_2_), channel_id=1, source_target_pairs={{0,4},{4,0},{1,5},{5,1},{2,6},{6,2},{3,7},{7,3},{8,12},{12,8},{9,1... | collective-permute-start | bytes 147464 | tf_op jit(solution)/shard_map/ppermute | solution.py:317
  53.6 0.0 collective-permute-done.7.refs_1_
  53.7 0.0 collective-permute-done.9.refs_3_.refs_7_
  53.7 0.0 copy-done.3
  53.7 1.0 %shard_map.147.front_ref = bf16[128,384]{1,0:T(8,128)(2,1)S(1)} custom-call(bf16[256,384]{1,0:T(8,128)(2,1)S(1)} %get-tuple-element.19.refs_0_.query_ref, bf16[64,384]{1,0:T(8,128)(2,1)S(1)} %shard_map.146.refs_0_, bf16[64,384]{1,0:T(8,128)(2,1)S(1)} %collective-permute-done.7.refs_1_, bf16[64,384]{1,0:T(8,128)(2,1)S(1)} %collective-permute-done.8.refs_2_.refs_6_, ...), custom_call_target="tpu_custom_call" | custom-call | tf_op jit(solution)/shard_map/pallas_call | solution.py:308
  54.6 0.0 collective-permute-done.13.refs_5_
  54.6 0.0 collective-permute-done.11.refs_3_
  54.7 0.0 copy-done.12
  54.7 2.1 %shard_map.148 = (bf16[256,384]{1,0:T(8,128)(2,1)}, bf16[512,384]{1,0:T(8,128)(2,1)}) custom-call(bf16[256,384]{1,0:T(8,128)(2,1)S(1)} %get-tuple-element.17.updated_ref, bf16[256,384]{1,0:T(8,128)(2,1)S(1)} %get-tuple-element.19.refs_0_.query_ref, bf16[128,128]{1,0:T(8,128)(2,1)S(1)} %get-tuple-element.20.swap_part_ref, ...), custom_call_target="tpu_custom_call" | custom-call | tf_op jit(solution)/shard_map/pallas_call | solution.py:308
  (4 shorter events, 0.0 us)
Async XLA Ops:
  0.6 6.1 %copy-start = (bf16[64,8,384]{2,1,0:T(8,128)(2,1)S(1)}, bf16[64,8,384]{2,1,0:T(8,128)(2,1)}, u32[]{:S(2)}) copy-start(bf16[64,8,384]{2,1,0:T(8,128)(2,1)} %param.15) | copy-start | bytes 1179652
  0.6 6.2 %copy-start.5 = (bf16[32,8,384]{2,1,0:T(8,128)(2,1)S(1)}, bf16[32,8,384]{2,1,0:T(8,128)(2,1)}, u32[]{:S(2)}) copy-start(bf16[32,8,384]{2,1,0:T(8,128)(2,1)} %param.13) | copy-start | bytes 589828
  0.7 9.1 %collective-permute-start = (bf16[256,384]{1,0:T(8,128)(2,1)}, bf16[256,384]{1,0:T(8,128)(2,1)S(1)}, u32[]{:S(2)}, u32[]{:S(2)}) collective-permute-start(bf16[256,384]{1,0:T(8,128)(2,1)} %bitcast.11), channel_id=1, source_target_pairs={{0,2},{1,3},{2,0},{3,1},{4,6},{5,7},{6,4},{7,5},{8,10},{9,11},{10,... | collective-permute-start | bytes 589832 | tf_op jit(solution)/shard_map/ppermute | solution.py:317
  4.5 9.3 %collective-permute-start.2 = (bf16[256,384]{1,0:T(8,128)(2,1)}, bf16[256,384]{1,0:T(8,128)(2,1)S(1)}, u32[]{:S(2)}, u32[]{:S(2)}) collective-permute-start(bf16[256,384]{1,0:T(8,128)(2,1)} %bitcast.12), channel_id=1, source_target_pairs={{0,3},{1,0},{2,1},{3,2},{4,7},{5,4},{6,5},{7,6},{8,11},{9,8},{10,9... | collective-permute-start | bytes 589832 | tf_op jit(solution)/shard_map/ppermute | solution.py:317
  5.3 9.2 %collective-permute-start.1 = (bf16[256,384]{1,0:T(8,128)(2,1)}, bf16[256,384]{1,0:T(8,128)(2,1)S(1)}, u32[]{:S(2)}, u32[]{:S(2)}) collective-permute-start(bf16[256,384]{1,0:T(8,128)(2,1)} %bitcast.13), channel_id=1, source_target_pairs={{0,1},{1,2},{2,3},{3,0},{4,5},{5,6},{6,7},{7,4},{8,9},{9,10},{10,1... | collective-permute-start | bytes 589832 | tf_op jit(solution)/shard_map/ppermute | solution.py:317
  6.9 1.2 %copy-start.1 = (bf16[384,1152]{1,0:T(8,128)(2,1)S(1)}, bf16[384,1152]{1,0:T(8,128)(2,1)}, u32[]{:S(2)}) copy-start(bf16[384,1152]{1,0:T(8,128)(2,1)} %refs_7_.2) | copy-start | bytes 2654212
  8.0 1.0 %copy-start.9 = (bf16[384,384]{1,0:T(8,128)(2,1)S(1)}, bf16[384,384]{1,0:T(8,128)(2,1)}, u32[]{:S(2)}) copy-start(bf16[384,384]{1,0:T(8,128)(2,1)} %virt_q_ref.1) | copy-start | bytes 884740
  9.0 1.2 %copy-start.2 = (bf16[384,1152]{1,0:T(8,128)(2,1)S(1)}, bf16[384,1152]{1,0:T(8,128)(2,1)}, u32[]{:S(2)}) copy-start(bf16[384,1152]{1,0:T(8,128)(2,1)} %refs_7_.2) | copy-start | bytes 2654212
  9.7 4.8 %copy-start.7 = (bf16[384,384]{1,0:T(8,128)(2,1)S(1)}, bf16[384,384]{1,0:T(8,128)(2,1)}, u32[]{:S(2)}) copy-start(bf16[384,384]{1,0:T(8,128)(2,1)} %refs_8_.3) | copy-start | bytes 884740
  14.5 12.3 %copy-start.6 = (bf16[384,768]{1,0:T(8,128)(2,1)S(1)}, bf16[384,768]{1,0:T(8,128)(2,1)}, u32[]{:S(2)}) copy-start(bf16[384,768]{1,0:T(8,128)(2,1)} %virt_kv_ref.1) | copy-start | bytes 1769476
  16.4 24.9 %copy-start.8 = (bf16[384,384]{1,0:T(8,128)(2,1)S(1)}, bf16[384,384]{1,0:T(8,128)(2,1)}, u32[]{:S(2)}) copy-start(bf16[384,384]{1,0:T(8,128)(2,1)} %back_q_ref.1) | copy-start | bytes 884740
  26.8 17.2 %copy-start.4 = (bf16[384,1152]{1,0:T(8,128)(2,1)S(1)}, bf16[384,1152]{1,0:T(8,128)(2,1)}, u32[]{:S(2)}) copy-start(bf16[384,1152]{1,0:T(8,128)(2,1)} %refs_7_.3) | copy-start | bytes 2654212
  27.6 3.9 %collective-permute-start.3 = (bf16[64,512]{1,0:T(8,128)(2,1)S(1)}, bf16[64,512]{1,0:T(8,128)(2,1)S(1)}, u32[]{:S(2)}, u32[]{:S(2)}) collective-permute-start(bf16[64,512]{1,0:T(8,128)(2,1)S(1)} %shard_map.144.a_ref), channel_id=1, source_target_pairs={{0,4},{4,0},{1,5},{5,1},{2,6},{6,2},{3,7},{7,3},{8,12},{12,8},{9,1... | collective-permute-start | bytes 196616 | tf_op jit(solution)/shard_map/ppermute | solution.py:317
  31.4 12.5 %copy-start.11 = (bf16[384,384]{1,0:T(8,128)(2,1)S(1)}, bf16[384,384]{1,0:T(8,128)(2,1)}, u32[]{:S(2)}) copy-start(bf16[384,384]{1,0:T(8,128)(2,1)} %refs_8_.4) | copy-start | bytes 884740
  31.8 12.2 %copy-start.10 = (bf16[384,384]{1,0:T(8,128)(2,1)S(1)}, bf16[384,384]{1,0:T(8,128)(2,1)}, u32[]{:S(2)}) copy-start(bf16[384,384]{1,0:T(8,128)(2,1)} %refs_6_.1) | copy-start | bytes 884740
  31.8 7.1 %collective-permute-start.4 = (bf16[64,512]{1,0:T(8,128)(2,1)S(1)}, bf16[64,512]{1,0:T(8,128)(2,1)S(1)}, u32[]{:S(2)}, u32[]{:S(2)}) collective-permute-start(bf16[64,512]{1,0:T(8,128)(2,1)S(1)} %shard_map.145.refs_1_), channel_id=1, source_target_pairs={{0,32},{4,52},{16,48},{20,36},{32,0},{36,20},{48,16},{52,4},{1,33}... | collective-permute-start | bytes 196616 | tf_op jit(solution)/shard_map/ppermute | solution.py:351
  37.0 7.0 %collective-permute-start.6 = (bf16[64,512]{1,0:T(8,128)(2,1)S(1)}, bf16[64,512]{1,0:T(8,128)(2,1)S(1)}, u32[]{:S(2)}, u32[]{:S(2)}) collective-permute-start(bf16[64,512]{1,0:T(8,128)(2,1)S(1)} %shard_map.145.refs_1_), channel_id=1, source_target_pairs={{0,16},{16,0},{32,48},{48,32},{1,17},{17,1},{33,49},{49,33},{2,18}... | collective-permute-start | bytes 196616 | tf_op jit(solution)/shard_map/ppermute | solution.py:352
  38.9 5.1 %collective-permute-start.5 = (bf16[64,512]{1,0:T(8,128)(2,1)S(1)}, bf16[64,512]{1,0:T(8,128)(2,1)S(1)}, u32[]{:S(2)}, u32[]{:S(2)}) collective-permute-start(bf16[64,512]{1,0:T(8,128)(2,1)S(1)} %collective-permute-done.4.refs_2_), channel_id=1, source_target_pairs={{0,4},{4,0},{1,5},{5,1},{2,6},{6,2},{3,7},{7,3},{8,12},{12,8},{9,1... | collective-permute-start | bytes 196616 | tf_op jit(solution)/shard_map/ppermute | solution.py:317
  44.0 9.7 %copy-start.3 = (bf16[384,768]{1,0:T(8,128)(2,1)S(1)}, bf16[384,768]{1,0:T(8,128)(2,1)}, u32[]{:S(2)}) copy-start(bf16[384,768]{1,0:T(8,128)(2,1)} %refs_8_.5) | copy-start | bytes 1769476
  45.4 9.3 %copy-start.12 = (bf16[384,384]{1,0:T(8,128)(2,1)S(1)}, bf16[384,384]{1,0:T(8,128)(2,1)}, u32[]{:S(2)}) copy-start(bf16[384,384]{1,0:T(8,128)(2,1)} %refs_9_.1) | copy-start | bytes 884740
  45.4 5.4 %collective-permute-start.8 = (bf16[64,384]{1,0:T(8,128)(2,1)S(1)}, bf16[64,384]{1,0:T(8,128)(2,1)S(1)}, u32[]{:S(2)}, u32[]{:S(2)}) collective-permute-start(bf16[64,384]{1,0:T(8,128)(2,1)S(1)} %shard_map.146.refs_0_), channel_id=1, source_target_pairs={{0,192},{4,204},{8,200},{12,196},{64,128},{68,140},{72,136},{76,13... | collective-permute-start | bytes 147464 | tf_op jit(solution)/shard_map/ppermute | solution.py:360
  45.5 6.8 %collective-permute-start.12 = (bf16[64,384]{1,0:T(8,128)(2,1)S(1)}, bf16[64,384]{1,0:T(8,128)(2,1)S(1)}, u32[]{:S(2)}, u32[]{:S(2)}) collective-permute-start(bf16[64,384]{1,0:T(8,128)(2,1)S(1)} %shard_map.146.refs_0_), channel_id=1, source_target_pairs={{0,128},{4,140},{8,136},{12,132},{64,192},{68,204},{72,200},{76,19... | collective-permute-start | bytes 147464 | tf_op jit(solution)/shard_map/ppermute | solution.py:360
  48.5 4.6 %collective-permute-start.10 = (bf16[64,384]{1,0:T(8,128)(2,1)S(1)}, bf16[64,384]{1,0:T(8,128)(2,1)S(1)}, u32[]{:S(2)}, u32[]{:S(2)}) collective-permute-start(bf16[64,384]{1,0:T(8,128)(2,1)S(1)} %shard_map.146.refs_0_), channel_id=1, source_target_pairs={{0,64},{4,76},{8,72},{12,68},{64,0},{68,12},{72,8},{76,4},{128,192... | collective-permute-start | bytes 147464 | tf_op jit(solution)/shard_map/ppermute | solution.py:360
  48.5 5.2 %collective-permute-start.7 = (bf16[64,384]{1,0:T(8,128)(2,1)S(1)}, bf16[64,384]{1,0:T(8,128)(2,1)S(1)}, u32[]{:S(2)}, u32[]{:S(2)}) collective-permute-start(bf16[64,384]{1,0:T(8,128)(2,1)S(1)} %shard_map.146.refs_0_), channel_id=1, source_target_pairs={{0,8},{8,0},{1,9},{9,1},{2,10},{10,2},{3,11},{11,3},{4,12},{12,4},... | collective-permute-start | bytes 147464 | tf_op jit(solution)/shard_map/ppermute | solution.py:361
  50.8 2.8 %collective-permute-start.9 = (bf16[64,384]{1,0:T(8,128)(2,1)S(1)}, bf16[64,384]{1,0:T(8,128)(2,1)S(1)}, u32[]{:S(2)}, u32[]{:S(2)}) collective-permute-start(bf16[64,384]{1,0:T(8,128)(2,1)S(1)} %collective-permute-done.8.refs_2_.refs_6_), channel_id=1, source_target_pairs={{0,4},{4,0},{1,5},{5,1},{2,6},{6,2},{3,7},{7,3},{8,12},{12,8},{9,1... | collective-permute-start | bytes 147464 | tf_op jit(solution)/shard_map/ppermute | solution.py:317
  52.3 2.3 %collective-permute-start.13 = (bf16[64,384]{1,0:T(8,128)(2,1)S(1)}, bf16[64,384]{1,0:T(8,128)(2,1)S(1)}, u32[]{:S(2)}, u32[]{:S(2)}) collective-permute-start(bf16[64,384]{1,0:T(8,128)(2,1)S(1)} %collective-permute-done.12.refs_4_), channel_id=1, source_target_pairs={{0,4},{4,0},{1,5},{5,1},{2,6},{6,2},{3,7},{7,3},{8,12},{12,8},{9,1... | collective-permute-start | bytes 147464 | tf_op jit(solution)/shard_map/ppermute | solution.py:317
  53.1 1.6 %collective-permute-start.11 = (bf16[64,384]{1,0:T(8,128)(2,1)S(1)}, bf16[64,384]{1,0:T(8,128)(2,1)S(1)}, u32[]{:S(2)}, u32[]{:S(2)}) collective-permute-start(bf16[64,384]{1,0:T(8,128)(2,1)S(1)} %collective-permute-done.10.refs_2_), channel_id=1, source_target_pairs={{0,4},{4,0},{1,5},{5,1},{2,6},{6,2},{3,7},{7,3},{8,12},{12,8},{9,1... | collective-permute-start | bytes 147464 | tf_op jit(solution)/shard_map/ppermute | solution.py:317
